TPU v7x, 32 devices: a whole 2x2x4 slice. The times are simulated.
32 devices in a mesh: grp: 2 (over y), path: 4 (over z), scen: 2 (over x), sub: 2 (over core).
Axes of the slice: x: 2, y: 2, z: 4, core: 2. Of those that a mesh axis runs over, the one named last changes fastest.
Arguments:
- path_links: int32 [8, 16384], P(None, ('grp', 'path')), parts along dimension 1, may hold values from -1 to 3583, as said below
- block_tiles: int32 [128, 16], P(('grp', 'path')), parts along dimension 0, may hold values from 0 to 27, as said below
- block_count: int32 [128], P(('grp', 'path')), parts along dimension 0, may hold values from 1 to 16
- path_commodity: int32 [128, 128], P(('grp', 'path')), parts along dimension 0, may hold values from 0 to 31, never falling along the last dimension, each value on 1 to 8 neighbouring positions
- demand: int32 [256, 4096], P(('scen', 'sub'), ('grp', 'path')), parts along dimension 1, may hold values from 1 to 64
- lengths: float32 [256, 7168], P(('scen', 'sub'), ('grp', 'path')), parts along dimension 1, may hold values from 0.05 to 10
- capacity: float32 [7168], P(('grp', 'path')), parts along dimension 0, may hold values from 4 to 32
- scenario_weight: float32 [512], P(('grp', 'scen', 'sub')), parts along dimension 0, may hold values from 0.5 to 2
Outputs:
- flows: float32 [256, 16384], P(('scen', 'sub'), ('grp', 'path')), parts along dimension 1
- lengths_next: float32 [256, 7168], P(('scen', 'sub'), ('grp', 'path')), parts along dimension 1
- robust_cost: float32 [16384], P(('grp', 'path')), parts along dimension 0
There are 2 independent parts, one for each index of `grp`. A program takes and returns all parts, laid end to end along the dimension named above; each array names one. Nothing has to cross between parts.
Inputs may be any that keep to these rules, and one draw needn't show every extreme that they name: `path_links`: entry [h, p] is the link of hop h of path p, or -1 past the path's last hop (hop 0 is never -1). Every link of a path in block b = p // 128 lies in a link block named by block_tiles[b, 0] to block_tiles[b, block_count[b] - 1]; link block j holds links j * 128 to (j + 1) * 128 - 1. `block_tiles`: the entries of one row are distinct link blocks.
All inputs are finite; a program needn't handle non-finite values.
Results may differ from a plain program's by a relative error of at most 0.0003.
Values sent between devices are 32-bit elements; how exact they have to be, the bound alone decides.
No kernel may reach another device: no remote copies, remote signals or barrier semaphores. Data moves between devices by JAX's collectives and lax.ppermute only.
A program may use at most 64 MiB of HBM per device.

v0:
```python
import jax
import jax.numpy as jnp
from jax import lax
from jax.sharding import PartitionSpec as P

PATHS_PER_BLOCK = 128
LB = 128
MAXT = 16
COMMODITY_BLOCK = 32
S = 256


SOFTMIN_RATE = 0.25
STEP_RATE = 1.0
DEMAND_UNIT = 0.0625
PRECISE = lax.Precision.HIGHEST


def incidence(hop_links, tile_ids, live_count):
    link_block = hop_links // LB
    column = hop_links % LB
    live_slots = jnp.arange(MAXT) < live_count
    slot_match = (
        (link_block[:, :, None] == tile_ids[None, None, :]) & live_slots[None, None, :]
    ).astype(jnp.float32)
    column_hot = (column[:, :, None] == jnp.arange(LB)[None, None, :]).astype(jnp.float32)
    return jnp.einsum("hpt,hpl->ptl", slot_match, column_hot, precision=PRECISE)


def tile_costs(table_grid, tile_ids, tile_hits):
    chosen = jnp.take(table_grid, tile_ids, axis=1)
    return jnp.einsum("stl,ptl->sp", chosen, tile_hits, precision=PRECISE)


def tile_loads(block_flow, tile_hits):
    return jnp.einsum("sp,ptl->stl", block_flow, tile_hits, precision=PRECISE)


def block_flows(block_cost, commodity_id, block_demand):
    commodity_onehot = (commodity_id[:, None] == jnp.arange(COMMODITY_BLOCK)[None, :]).astype(
        jnp.float32
    )
    weight = jnp.exp(-SOFTMIN_RATE * block_cost)
    totals = jnp.dot(
        weight, commodity_onehot, preferred_element_type=jnp.float32, precision=PRECISE
    )
    per_path = jnp.dot(
        totals, commodity_onehot.T, preferred_element_type=jnp.float32, precision=PRECISE
    )
    wanted = jnp.dot(
        block_demand.astype(jnp.float32) * DEMAND_UNIT,
        commodity_onehot.T,
        preferred_element_type=jnp.float32,
        precision=PRECISE,
    )
    return wanted * weight / per_path


def flow_sweep(length_wide, links_by_block, tile_table, count_table, comm_table, block_demands):
    scenario_rows = length_wide.shape[0]
    length_grid = length_wide.reshape(scenario_rows, -1, LB)

    def first_pass(load_grid, pieces):
        hop_links, tile_ids, live_count, commodity_id, block_demand = pieces
        tile_hits = incidence(hop_links, tile_ids, live_count)
        block_cost = tile_costs(length_grid, tile_ids, tile_hits)
        block_flow = block_flows(block_cost, commodity_id, block_demand)
        load_grid = load_grid.at[:, tile_ids, :].add(tile_loads(block_flow, tile_hits))
        return (load_grid, block_flow)

    load_grid, flow_blocks = lax.scan(
        first_pass,
        jnp.zeros(length_grid.shape, jnp.float32),
        (links_by_block, tile_table, count_table, comm_table, block_demands),
    )
    flows = flow_blocks.transpose(1, 0, 2).reshape(scenario_rows, -1)
    return (flows, load_grid.reshape(scenario_rows, -1))


def cost_sweep(next_wide, weight_rows, links_by_block, tile_table, count_table):
    scenario_rows = next_wide.shape[0]
    next_grid = next_wide.reshape(scenario_rows, -1, LB)

    def second_pass(carried, pieces):
        hop_links, tile_ids, live_count = pieces
        tile_hits = incidence(hop_links, tile_ids, live_count)
        block_cost = tile_costs(next_grid, tile_ids, tile_hits)
        mixed = (
            jnp.dot(
                weight_rows[None, :],
                block_cost,
                preferred_element_type=jnp.float32,
                precision=PRECISE,
            )[0]
            / S
        )
        return (carried, mixed)

    _, partial_value = lax.scan(
        second_pass, jnp.zeros((), jnp.float32), (links_by_block, tile_table, count_table)
    )
    return partial_value.reshape(-1)


def body(
    path_links, block_tiles, block_count, path_commodity, demand, lengths, capacity, scenario_weight
):
    hop_count, path_total = path_links.shape
    block_list = block_tiles.shape[0]
    scenario_rows, link_rows = lengths.shape
    links_by_block = path_links.reshape(hop_count, block_list, PATHS_PER_BLOCK).transpose(1, 0, 2)
    block_demands = demand.reshape(scenario_rows, block_list, COMMODITY_BLOCK).transpose(1, 0, 2)
    gathered = lax.all_gather(lengths, "path", axis=1, tiled=True)
    flows, load_full = flow_sweep(
        gathered, links_by_block, block_tiles, block_count, path_commodity, block_demands
    )
    link_total = gathered.shape[1]
    own_loads = lax.psum_scatter(load_full, "path", scatter_dimension=1, tiled=True)
    grown_len = lengths * jnp.exp(STEP_RATE * own_loads / capacity[None, :])
    totals = lax.psum(jnp.sum(grown_len, axis=1), "path")
    lengths_next = grown_len * (link_total / totals)[:, None]
    wide_next = lax.all_gather(lengths_next, "path", axis=1, tiled=True)
    partial_value = cost_sweep(wide_next, scenario_weight, links_by_block, block_tiles, block_count)
    robust = lax.psum(partial_value, ("scen", "sub"))
    return (flows, lengths_next, robust)


def solution(mesh):
    return jax.shard_map(
        body,
        mesh=mesh,
        in_specs=(
            P(None, ("grp", "path")),
            P(("grp", "path"), None),
            P(("grp", "path")),
            P(("grp", "path"), None),
            P(("scen", "sub"), ("grp", "path")),
            P(("scen", "sub"), ("grp", "path")),
            P(("grp", "path")),
            P(("grp", "scen", "sub")),
        ),
        out_specs=(
            P(("scen", "sub"), ("grp", "path")),
            P(("scen", "sub"), ("grp", "path")),
            P(("grp", "path")),
        ),
        check_vma=False,
    )
```

profile of v0, /device:TPU:0, one launch (start us, length us, event | category | flops | bytes accessed | tf_op | source)
XLA Modules:
  0.0 389.9 jit_solution(973819889943569372)
XLA Ops:
  7.2 23.0 %all_gather.6 = f32[64,3584]{1,0:T(8,128)S(1)} all-gather(f32[64,896]{1,0:T(8,128)} %param.19), channel_id=1, replica_groups=mesh['grp'=2,'path'=4,'scen'=2,'sub'=2] {'path'}, dimensions={1}, use_global_device_ids=true | all-gather | bytes 1146880 | tf_op jit(solution)/shard_map/all_gather | solution.py:113
  32.6 185.0 %while.26 = (s32[]{:T(128)}, f32[64,28,128]{2,0,1:T(8,128)S(1)}, f32[16,64,128]{2,1,0:T(8,128)}, s32[16,16]{1,0:T(8,128)}, s32[16,64,32]{1,2,0:T(8,128)}, /*inde...) while((s32[]{:T(128)}, f32[64,28,128]{2,0,1:T(8,128)S(1)}, ...), condition=%wide.region_2.4_spmd, body=%wide.region_0.3_spmd.sunk | while | flops 416772288 | bytes 7180105 | solution.py:71
  36.8 1.4 fusion.88
  48.3 1.4 fusion.88
  59.9 1.4 fusion.88
  71.5 1.4 fusion.88
  83.0 1.4 fusion.88
  94.6 1.4 fusion.88
  106.2 1.4 fusion.88
  117.7 1.4 fusion.88
  129.3 1.4 fusion.88
  140.9 1.4 fusion.88
  152.4 1.4 fusion.88
  164.0 1.4 fusion.88
  175.6 1.4 fusion.88
  187.1 1.4 fusion.88
  198.7 1.4 fusion.88
  210.3 1.4 fusion.88
  220.5 23.0 %reduce-scatter.2.cloned.1.call-done = f32[64,896]{1,0:T(8,128)} async-done(((f32[64,3584]{1,0:T(8,128)}), f32[64,896]{1,0:T(8,128)}) %reduce-scatter.2.cloned.1.call-update) | async-done | bytes 229392 | tf_op jit(solution)/shard_map/reduce_scatter | solution.py:118
  244.6 9.7 %psum.14 = f32[64]{0:T(128)S(1)} all-reduce(f32[64]{0:T(128)S(1)} %fusion.47), channel_id=1, replica_groups=mesh['grp'=2,'path'=4,'scen'=2,'sub'=2] {'path'}, use_global_device_ids=true, to_apply=%region_5.7 | all-reduce | flops 64 | bytes 512 | tf_op jit(solution)/shard_map/psum | solution.py:120
  254.5 18.4 %all_gather.7 = f32[64,3584]{1,0:T(8,128)S(1)} all-gather(f32[64,896]{1,0:T(8,128)S(1)} %broadcast_multiply_fusion), channel_id=1, replica_groups=mesh['grp'=2,'path'=4,'scen'=2,'sub'=2] {'path'}, dimensions={1}, use_global_device_ids=true | all-gather | bytes 1146880 | tf_op jit(solution)/shard_map/all_gather | solution.py:122
  273.5 103.2 %while.27 = (s32[]{:T(128)}, f32[16,128]{1,0:T(8,128)S(1)}, s32[16,16]{1,0:T(8,128)}, f32[64,28,128]{2,0,1:T(8,128)S(1)}, s32[16,8,128]{2,1,0:T(8,128)}, /*index...) while((s32[]{:T(128)}, f32[16,128]{1,0:T(8,128)S(1)}, s32[16,16]{1,0:T(8,128)}, ...), condition=%wide.region_7.9_spmd, body=%wide.region_6.8_spmd.sunk | while | flops 205941024 | bytes 4063613 | solution.py:99
  278.4 1.4 convolution_bitcast_fusion.7
  376.7 6.3 %psum.15 = f32[2048]{0:T(1024)} all-reduce(f32[2048]{0:T(1024)S(1)} %bitcast.175), channel_id=1, replica_groups=mesh['grp'=2,'path'=4,'scen'=2,'sub'=2] {'scen','sub'}, use_global_device_ids=true, to_apply=%region_8.10 | all-reduce | flops 2048 | bytes 16384 | tf_op jit(solution)/shard_map/psum | solution.py:124
  (524 shorter events, 269.5 us)
Async XLA Ops:
  7.2 236.3 %reduce-scatter.2.cloned.1.call-start = ((), (), s32[]{:S(2)}) async-start(), calls=%async_computation.1 | async-start | bytes 1146880 | tf_op jit(solution)/shard_map/reduce_scatter | solution.py:118
  30.2 0.9 copy-start.4
  31.9 0.7 copy-start.7
  218.6 1.0 copy-start.3
  219.7 23.8 %copy-start = (f32[64,896]{1,0:T(8,128)S(1)}, f32[64,896]{1,0:T(8,128)}, u32[]{:S(2)}) copy-start(f32[64,896]{1,0:T(8,128)} %param.19) | copy-start | bytes 688132
  219.7 23.8 %copy-start.5 = (f32[896]{0:T(1024)S(1)}, f32[896]{0:T(1024)}, u32[]{:S(2)}) copy-start(f32[896]{0:T(1024)} %param.20) | copy-start | bytes 10756
  243.5 10.9 %copy-start.1 = (f32[64,896]{1,0:T(8,128)S(1)}, f32[64,896]{1,0:T(8,128)}, u32[]{:S(2)}) copy-start(f32[64,896]{1,0:T(8,128)} %reduce-scatter.2.cloned.1.call-done) | copy-start | bytes 688132
  254.4 18.4 %copy-start.2 = (f32[64,896]{1,0:T(8,128)}, f32[64,896]{1,0:T(8,128)S(1)}, u32[]{:S(2)}) copy-start(f32[64,896]{1,0:T(8,128)S(1)} %broadcast_multiply_fusion) | copy-start | bytes 688132
  272.8 0.7 copy-start.6
Sparse Core Ops, SparseCore 0:
  218.8 24.6 reduce-scatter.1
where the time goes:
time: 395 us; the launch traced here: 390 us
  other arithmetic  106 us (27%)
  matrix products  106 us (27%)
  local copies, waits for them, and re-layouts  80.8 us (20%)
  blocking collectives  57.4 us (15%)
  waiting for transfers between devices  23 us (6%)
  between operations  14.1 us (4%)
    dynamic_slice x96, local copies, waits for them, and re-layouts, flow_sweep(): lax.scan(first_pass, jnp.zeros(length_grid.shape, jnp.float32), (links_by...  44.7 us
    dot_general x32, matrix products, tile_costs(): return jnp.einsum('stl,ptl->sp', chosen, tile_hits, precision=PRECISE)  44.3 us
    and x32, other arithmetic, tile_costs(): chosen = jnp.take(table_grid, tile_ids, axis=1)  42.4 us
    reduce_scatter x1, waiting for transfers between devices, body(): lax.psum_scatter(load_full, 'path', scatter_dimension=1, tiled=True)  23 us
    all_gather x1, blocking collectives, body(): gathered = lax.all_gather(lengths, 'path', axis=1, tiled=True)  23 us
    scatter-add x16, other arithmetic, first_pass(): load_grid.at[:, tile_ids, :].add(tile_loads(block_flow, tile_hits))  21.2 us
    dot_general x32, matrix products, incidence(): return jnp.einsum('hpt,hpl->ptl', slot_match, column_hot, precision=PRECISE)  21.2 us
    gather x32, local copies, waits for them, and re-layouts, tile_costs(): chosen = jnp.take(table_grid, tile_ids, axis=1)  18.6 us
  transfers between devices with their start and end apart: 1, of which 1 were waited for; matrix products, arithmetic and copies ran while one was open for 0% of the time, Pallas kernels for 0%

commit v1 on v0

v1 whole, which is shorter than its diff:
```python
import jax
import jax.numpy as jnp
from jax import lax
from jax.experimental import pallas as pl
from jax.experimental.pallas import tpu as pltpu
from jax.sharding import PartitionSpec as P

PATHS_PER_BLOCK = 128
LB = 128
MAXT = 16
COMMODITY_BLOCK = 32
S = 256
GROUP = LB // COMMODITY_BLOCK

SOFTMIN_RATE = 0.25
STEP_RATE = 1.0
DEMAND_UNIT = 0.0625
VMEM_BYTES = 56 * 1024 * 1024

F32 = jnp.float32
BF16 = jnp.bfloat16


def split(x):
    high = x.astype(BF16)
    return high, (x - high.astype(F32)).astype(BF16)


def whole(shape):
    return pl.BlockSpec(shape, lambda *_: (0,) * len(shape))


SCALARS = pl.BlockSpec(memory_space=pltpu.SMEM)


def incidence_kernel(tiles_ref, count_ref, links_ref, comm_ref, demand_ref, hits_ref, same_ref, wanted_ref):
    step = pl.program_id(0)
    pack = 16
    lane_rows = [
        (lax.broadcasted_iota(jnp.int32, (pack, LB), 0) + pack * g).astype(F32).astype(BF16) for g in range(LB // pack)
    ]
    demand = demand_ref[...].astype(F32).astype(BF16)
    commodity_rows = lax.broadcasted_iota(jnp.int32, (LB, PATHS_PER_BLOCK), 0)
    for j in range(GROUP):
        block = step * GROUP + j
        links = links_ref[:, j * PATHS_PER_BLOCK : (j + 1) * PATHS_PER_BLOCK]
        live = count_ref[block]
        commodity = comm_ref[pl.ds(block, 1), :] + COMMODITY_BLOCK * j
        onehot = (commodity_rows == commodity).astype(F32).astype(BF16)
        same = lax.dot_general(onehot, onehot, (((0,), (0,)), ((), ())), preferred_element_type=F32)
        same_ref[j] = same.astype(BF16)
        wanted = jnp.dot(demand, onehot, preferred_element_type=F32)
        wanted_ref[:, j * PATHS_PER_BLOCK : (j + 1) * PATHS_PER_BLOCK] = wanted * DEMAND_UNIT

        def one_slot(t, carry, j=j, block=block, links=links, live=live):
            start = pl.multiple_of(t * LB, LB)

            @pl.when(t < live)
            def _():
                place = (links - tiles_ref[block, t] * LB).astype(F32)
                totals = [jnp.zeros((pack, PATHS_PER_BLOCK), BF16) for _ in lane_rows]
                for h in range(links.shape[0]):
                    row = jnp.broadcast_to(place[h : h + 1, :], (pack, PATHS_PER_BLOCK)).astype(BF16)
                    totals = [
                        a + jnp.where(row == lane, jnp.ones_like(a), jnp.zeros_like(a))
                        for a, lane in zip(totals, lane_rows)
                    ]
                for g, a in enumerate(totals):
                    hits_ref[j, pl.ds(start + g * pack, pack), :] = a

            @pl.when(t >= live)
            def _():
                hits_ref[j, pl.ds(start, LB), :] = jnp.zeros((LB, PATHS_PER_BLOCK), BF16)

            return carry

        lax.fori_loop(0, MAXT, one_slot, 0)


def build_incidence(path_links, block_tiles, block_count, path_commodity, demand):
    hops, paths = path_links.shape
    blocks = block_tiles.shape[0]
    rows = demand.shape[0]
    wide = GROUP * PATHS_PER_BLOCK
    return pl.pallas_call(
        incidence_kernel,
        grid=(blocks // GROUP,),
        in_specs=[
            SCALARS,
            SCALARS,
            pl.BlockSpec((hops, wide), lambda i: (0, i)),
            whole(path_commodity.shape),
            pl.BlockSpec((rows, LB), lambda i: (0, i)),
        ],
        out_specs=[
            pl.BlockSpec((GROUP, MAXT * LB, PATHS_PER_BLOCK), lambda i: (i, 0, 0)),
            pl.BlockSpec((GROUP, PATHS_PER_BLOCK, PATHS_PER_BLOCK), lambda i: (i, 0, 0)),
            pl.BlockSpec((rows, wide), lambda i: (0, i)),
        ],
        out_shape=[
            jax.ShapeDtypeStruct((blocks, MAXT * LB, PATHS_PER_BLOCK), BF16),
            jax.ShapeDtypeStruct((blocks, PATHS_PER_BLOCK, PATHS_PER_BLOCK), BF16),
            jax.ShapeDtypeStruct((rows, paths), F32),
        ],
        compiler_params=pltpu.CompilerParams(vmem_limit_bytes=VMEM_BYTES),
        cost_estimate=pl.CostEstimate(flops=10**9, bytes_accessed=10**7, transcendentals=0),
        name="incidence",
    )(block_tiles, block_count, path_links, path_commodity, demand)


def flow_kernel(pieces, chunks, origin_ref, tiles_ref, *refs):
    piece_refs, (hits_ref, same_ref, wanted_ref) = refs[:pieces], refs[pieces : pieces + 3]
    flows_ref, *out_refs = refs[pieces + 3 : -2]
    split_ref, load_ref = refs[-2:]
    step = pl.program_id(0)
    tile_total, rows2, _ = split_ref.shape
    rows = rows2 // 2
    shard_tiles = piece_refs[0].shape[-1] // LB
    shards = [(i, r, s) for i, r in enumerate(piece_refs) for s in range(r.shape[0])]

    @pl.when(step == 0)
    def _():
        for i, ref, s in shards:
            first = (origin_ref[i] + s) * shard_tiles
            for k in range(shard_tiles):
                high, low = split(ref[s, :, k * LB : (k + 1) * LB])
                split_ref[first + k, :rows, :] = high
                split_ref[first + k, rows:, :] = low
        load_ref[...] = jnp.zeros_like(load_ref)

    for j in range(GROUP):
        block = step * GROUP + j
        ids = [tiles_ref[block, t] for t in range(MAXT)]
        chosen = jnp.concatenate([split_ref[i] for i in ids], axis=1)
        cost = jnp.dot(chosen, hits_ref[j], preferred_element_type=F32)
        cost = cost[:rows] + cost[rows:]
        weight = jnp.exp(-SOFTMIN_RATE * cost)
        high, low = split(weight)
        total = jnp.dot(jnp.concatenate([high, low], axis=0), same_ref[j], preferred_element_type=F32)
        total = total[:rows] + total[rows:]
        columns = slice(j * PATHS_PER_BLOCK, (j + 1) * PATHS_PER_BLOCK)
        flow = wanted_ref[:, columns] * weight / total
        flows_ref[:, columns] = flow
        high, low = split(flow)
        load = lax.dot_general(
            jnp.concatenate([high, low], axis=0), hits_ref[j], (((1,), (1,)), ((), ())), preferred_element_type=F32
        )
        for t, i in enumerate(ids):
            load_ref[i] += load[:, t * LB : (t + 1) * LB]

    @pl.when(step == pl.num_programs(0) - 1)
    def _():
        if not chunks:
            for k in range(tile_total):
                out_refs[0][:, k * LB : (k + 1) * LB] = load_ref[k, :rows, :] + load_ref[k, rows:, :]
            return
        height = rows // chunks
        for d in range(chunks):
            row = pl.multiple_of(lax.rem(origin_ref[0] + d, chunks) * height, height)
            for k in range(tile_total):
                out_refs[d][:, k * LB : (k + 1) * LB] = (
                    load_ref[k, pl.ds(row, height), :] + load_ref[k, pl.ds(rows + row, height), :]
                )
        row = pl.multiple_of(origin_ref[0] * height, height)
        for i, ref, s in shards:
            first = (origin_ref[i] + s) * shard_tiles
            for k in range(shard_tiles):
                out_refs[chunks][:, pl.ds(pl.multiple_of((first + k) * LB, LB), LB)] = ref[
                    s, pl.ds(row, height), k * LB : (k + 1) * LB
                ]


def flows_and_loads(pieces, origin, block_tiles, hits, same, wanted, chunks):
    blocks = block_tiles.shape[0]
    _, rows, own = pieces[0].shape
    paths = wanted.shape[1]
    links = own * sum(p.shape[0] for p in pieces)
    wide = GROUP * PATHS_PER_BLOCK
    outs = [(rows // chunks, links)] * (chunks + 1) if chunks else [(rows, links)]
    return pl.pallas_call(
        lambda *refs: flow_kernel(len(pieces), chunks, *refs),
        grid=(blocks // GROUP,),
        in_specs=[SCALARS, SCALARS]
        + [whole(p.shape) for p in pieces]
        + [
            pl.BlockSpec((GROUP, MAXT * LB, PATHS_PER_BLOCK), lambda i: (i, 0, 0)),
            pl.BlockSpec((GROUP, PATHS_PER_BLOCK, PATHS_PER_BLOCK), lambda i: (i, 0, 0)),
            pl.BlockSpec((rows, wide), lambda i: (0, i)),
        ],
        out_specs=[pl.BlockSpec((rows, wide), lambda i: (0, i))] + [whole(o) for o in outs],
        out_shape=[jax.ShapeDtypeStruct((rows, paths), F32)] + [jax.ShapeDtypeStruct(o, F32) for o in outs],
        scratch_shapes=[
            pltpu.VMEM((links // LB, 2 * rows, LB), BF16),
            pltpu.VMEM((links // LB, 2 * rows, LB), F32),
        ],
        compiler_params=pltpu.CompilerParams(vmem_limit_bytes=VMEM_BYTES),
        cost_estimate=pl.CostEstimate(flops=10**10, bytes_accessed=10**7, transcendentals=10**5),
        name="flows",
    )(origin, block_tiles, *pieces, hits, same, wanted)


def growth_kernel(chunks, me_ref, *refs):
    load_refs, (length_ref, weight_ref) = refs[:chunks], refs[chunks : chunks + 2]
    capacity_refs = refs[chunks + 2 : 2 * chunks + 2]
    next_refs, mixed_ref = refs[2 * chunks + 2 : 3 * chunks + 2], refs[-2]
    grown_ref = refs[-1]
    me = me_ref[0]
    height, links = length_ref.shape
    shard = links // chunks
    tiles = shard // LB
    total = jnp.zeros((height, LB), F32)
    for d in range(chunks):
        first = lax.rem(me + chunks - d, chunks)
        for k in range(tiles):
            place = pl.ds(pl.multiple_of((first * tiles + k) * LB, LB), LB)
            load = load_refs[0][:, place]
            for ref in load_refs[1:]:
                load = load + ref[:, place]
            grown = length_ref[:, place] * jnp.exp(STEP_RATE * load / capacity_refs[d][:, k * LB : (k + 1) * LB])
            grown_ref[first * tiles + k] = grown
            total = total + grown
    factor = links / jnp.sum(total, axis=1, keepdims=True)
    weight = weight_ref[pl.ds(pl.multiple_of(me * height, height), height), :]
    for d in range(chunks):
        first = lax.rem(me + d, chunks)
        for k in range(tiles):
            new = grown_ref[first * tiles + k] * factor
            next_refs[d][:, k * LB : (k + 1) * LB] = new
            mixed_ref[pl.ds(first * tiles + k, 1), :] = jnp.sum(weight * new, axis=0, keepdims=True)


def grow(me, loads, lengths, weights, capacities):
    chunks = len(loads)
    height, links = lengths.shape
    out = [jax.ShapeDtypeStruct((height, links // chunks), F32)] * chunks + [jax.ShapeDtypeStruct((links // LB, LB), F32)]
    vmem = pl.BlockSpec(memory_space=pltpu.VMEM)
    return pl.pallas_call(
        lambda *refs: growth_kernel(chunks, *refs),
        in_specs=[SCALARS] + [vmem] * (2 * chunks + 2),
        out_specs=[vmem] * (chunks + 1),
        out_shape=out,
        scratch_shapes=[pltpu.VMEM((links // LB, height, LB), F32)],
        compiler_params=pltpu.CompilerParams(vmem_limit_bytes=VMEM_BYTES),
        name="growth",
    )(me, *loads, lengths, weights, *capacities)


def robust_kernel(parts, tiles_ref, *refs):
    part_refs, hits_ref, out_ref, mixed_ref = refs[:parts], refs[parts], refs[-2], refs[-1]
    step = pl.program_id(0)

    @pl.when(step == 0)
    def _():
        mixed = part_refs[0][...]
        for ref in part_refs[1:]:
            mixed = mixed + ref[...]
        high = mixed.astype(BF16)
        rest = mixed - high.astype(F32)
        middle = rest.astype(BF16)
        low = (rest - middle.astype(F32)).astype(BF16)
        for k in range(mixed.shape[0]):
            mixed_ref[k] = jnp.concatenate(
                [jnp.broadcast_to(v[k : k + 1].astype(F32), (8, LB)) for v in (high, middle, low)], axis=0
            ).astype(BF16)

    for j in range(GROUP):
        block = step * GROUP + j
        chosen = jnp.concatenate([mixed_ref[tiles_ref[block, t]] for t in range(MAXT)], axis=1)
        cost = jnp.dot(chosen, hits_ref[j], preferred_element_type=F32)
        out_ref[pl.ds(block, 1), :] = (cost[0:1] + cost[8:9] + cost[16:17]) / S


def robust_costs(block_tiles, parts, hits):
    blocks = block_tiles.shape[0]
    out = pl.pallas_call(
        lambda *refs: robust_kernel(len(parts), *refs),
        grid=(blocks // GROUP,),
        in_specs=[SCALARS]
        + [whole(p.shape) for p in parts]
        + [pl.BlockSpec((GROUP, MAXT * LB, PATHS_PER_BLOCK), lambda i: (i, 0, 0))],
        out_specs=whole((blocks, PATHS_PER_BLOCK)),
        out_shape=jax.ShapeDtypeStruct((blocks, PATHS_PER_BLOCK), F32),
        scratch_shapes=[pltpu.VMEM((parts[0].shape[0], 24, LB), BF16)],
        compiler_params=pltpu.CompilerParams(vmem_limit_bytes=VMEM_BYTES),
        name="robust",
    )(block_tiles, *parts, hits)
    return out.reshape(-1)


def exchange(x, axis, n, bit):
    return lax.ppermute(x, axis, [(i, i ^ bit) for i in range(n)])


def shift(x, axis, n, d):
    return lax.ppermute(x, axis, [(i, (i + d) % n) for i in range(n)])


def power_of_two(n):
    return n & (n - 1) == 0


def body_direct(sizes, path_links, block_tiles, block_count, path_commodity, demand, lengths, capacity, scenario_weight):
    n = sizes["path"]
    rows, own = lengths.shape
    index = lax.axis_index("path").astype(jnp.int32)
    origin = jnp.stack([lax.rem(index + n - d, n) for d in range(n)])
    pieces = [lengths] + [shift(lengths, "path", n, d) for d in range(1, n)]
    capacity_row = capacity[None, :]
    capacities = [capacity_row] + [shift(capacity_row, "path", n, d) for d in range(1, n)]
    hits, same, wanted = build_incidence(path_links, block_tiles, block_count, path_commodity, demand)
    flows, *chunks = flows_and_loads([p[None] for p in pieces], origin, block_tiles, hits, same, wanted, n)
    loads = [chunks[0]] + [shift(chunks[d], "path", n, d) for d in range(1, n)]
    *new, mixed = grow(origin, loads, chunks[n], scenario_weight[:, None], capacities)
    arrived = [new[0]] + [shift(new[d], "path", n, d) for d in range(1, n)]
    height = rows // n
    for axis in ("sub", "scen"):
        bit = 1
        while bit < sizes[axis]:
            mixed = mixed + exchange(mixed, axis, sizes[axis], bit)
            bit *= 2
    bit, parts = 1, [mixed]
    while bit < n:
        mixed = sum(parts[1:], parts[0])
        parts = [mixed, exchange(mixed, "path", n, bit)]
        bit *= 2
    robust = robust_costs(block_tiles, parts, hits)
    lengths_next = jnp.zeros((rows, own), F32)
    for d in range(n):
        lengths_next = lax.dynamic_update_slice(lengths_next, arrived[d], (origin[d] * height, 0))
    return flows, lengths_next, robust


def body_wide(sizes, path_links, block_tiles, block_count, path_commodity, demand, lengths, capacity, scenario_weight):
    gathered = lax.all_gather(lengths, "path", axis=0, tiled=False)
    hits, same, wanted = build_incidence(path_links, block_tiles, block_count, path_commodity, demand)
    origin = jnp.zeros((1,), jnp.int32)
    flows, loads = flows_and_loads([gathered], origin, block_tiles, hits, same, wanted, 0)
    own_loads = lax.psum_scatter(loads, "path", scatter_dimension=1, tiled=True)
    grown = lengths * jnp.exp(STEP_RATE * own_loads / capacity[None, :])
    totals = lax.psum(jnp.sum(grown, axis=1), "path")
    lengths_next = grown * (loads.shape[1] / totals)[:, None]
    mixed = lax.psum(jnp.sum(lengths_next * scenario_weight[:, None], axis=0), ("scen", "sub"))
    mixed = lax.all_gather(mixed.reshape(-1, LB), "path", axis=0, tiled=True)
    return flows, lengths_next, robust_costs(block_tiles, [mixed], hits)


def solution(mesh):
    sizes = dict(mesh.shape)

    def body(*args):
        n, rows = sizes["path"], args[5].shape[0]
        direct = n <= 8 and rows % (16 * n) == 0 and all(power_of_two(sizes[a]) for a in ("path", "scen", "sub"))
        return (body_direct if direct else body_wide)(sizes, *args)

    return jax.shard_map(
        body,
        mesh=mesh,
        in_specs=(
            P(None, ("grp", "path")),
            P(("grp", "path"), None),
            P(("grp", "path")),
            P(("grp", "path"), None),
            P(("scen", "sub"), ("grp", "path")),
            P(("scen", "sub"), ("grp", "path")),
            P(("grp", "path")),
            P(("grp", "scen", "sub")),
        ),
        out_specs=(
            P(("scen", "sub"), ("grp", "path")),
            P(("scen", "sub"), ("grp", "path")),
            P(("grp", "path")),
        ),
        check_vma=False,
    )
```

time: 395 us -> 91 us (0.23); the launches traced: 390 us -> 90.7 us
  matrix products: 106 us -> 0 us
  other arithmetic: 106 us -> 1.37 us
  local copies, waits for them, and re-layouts: 80.8 us -> 4.48 us
  blocking collectives: 57.4 us -> 0 us
  Pallas kernels: 0 us -> 34.6 us
  starting transfers between devices: 0.04 us -> 26.9 us
  between operations: 14.1 us -> 0.8 us
    dot_general x144 -> x0, matrix products: 106 us -> none  [the longest x32 44.3 us: tile_costs(): return jnp.einsum('stl,ptl->sp', chosen, tile_hits, precision=PRECISE)]
    and x48 -> x0, other arithmetic: 45.7 us -> none  [the longest x32 42.4 us: tile_costs(): chosen = jnp.take(table_grid, tile_ids, axis=1)]
    dynamic_slice x96 -> x0, local copies, waits for them, and re-layouts: 44.7 us -> none  [flow_sweep(): lax.scan(first_pass, jnp.zeros(length_grid.shape, jnp.float32), (links_by...]
    all_gather x2 -> x0, blocking collectives: 41.3 us -> none  [the longest x1 23 us: body(): gathered = lax.all_gather(lengths, 'path', axis=1, tiled=True)]
    select_n x96 -> x0, other arithmetic: 34.6 us -> none  [the longest x32 12.1 us: incidence(): link_block = hop_links // LB]
    pallas_call x0 -> x4, Pallas kernels: none -> 34.6 us  [the longest x1 13.5 us: build_incidence(): pl.pallas_call(incidence_kernel, grid=(blocks // GROUP,), in_specs=[SCALA...]
    ppermute x0 -> x16, starting transfers between devices: none -> 26.9 us  [the longest x12 21.6 us: shift(): return lax.ppermute(x, axis, [(i, (i + d) % n) for i in range(n)])]
    reduce_scatter x1 -> x0, waiting for transfers between devices: 23 us -> none  [body(): lax.psum_scatter(load_full, 'path', scatter_dimension=1, tiled=True)]
  transfers between devices with their start and end apart: 1 -> 16, of which waited for: 1 -> 6; matrix products, arithmetic and copies ran while one was open for 0% -> 2% of each run, Pallas kernels for 0% -> 21%
where the time goes in v1:
time: 91 us; the launch traced here: 90.7 us
  Pallas kernels  34.6 us (38%)
  starting transfers between devices  26.9 us (30%)
  waiting for transfers between devices  22.5 us (25%)
  local copies, waits for them, and re-layouts  4.48 us (5%)
  other arithmetic  1.37 us (2%)
    ppermute x12, starting transfers between devices, shift(): return lax.ppermute(x, axis, [(i, (i + d) % n) for i in range(n)])  21.6 us
    ppermute x12, waiting for transfers between devices, shift(): return lax.ppermute(x, axis, [(i, (i + d) % n) for i in range(n)])  16.5 us
    pallas_call x1, Pallas kernels, build_incidence(): pl.pallas_call(incidence_kernel, grid=(blocks // GROUP,), in_specs=[SCALA...  13.5 us
    pallas_call x1, Pallas kernels, flows_and_loads(): pl.pallas_call(lambda *refs: flow_kernel(len(pieces), chunks, *refs), gri...  13.2 us
    ppermute x4, waiting for transfers between devices, exchange(): return lax.ppermute(x, axis, [(i, i ^ bit) for i in range(n)])  6.08 us
    pallas_call x1, Pallas kernels, robust_costs(): pl.pallas_call(lambda *refs: robust_kernel(len(parts), *refs), grid=(bloc...  5.54 us
    ppermute x4, starting transfers between devices, exchange(): return lax.ppermute(x, axis, [(i, i ^ bit) for i in range(n)])  5.32 us
    unnamed x30, local copies, waits for them, and re-layouts  2.9 us
  transfers between devices with their start and end apart: 16, of which 6 were waited for; matrix products, arithmetic and copies ran while one was open for 2% of the time, Pallas kernels for 21%

profile of v1, /device:TPU:0, one launch (start us, length us, event | category | flops | bytes accessed | tf_op | source)
XLA Modules:
  0.0 90.7 jit_solution(16507008396888443246)
XLA Ops:
  0.6 3.1 %collective-permute-start = (f32[64,896]{1,0:T(8,128)}, f32[64,896]{1,0:T(8,128)S(1)}, u32[]{:S(2)}, u32[]{:S(2)}) collective-permute-start(f32[64,896]{1,0:T(8,128)} %param.13), channel_id=1, source_target_pairs={{0,4},{4,8},{8,12},{12,0},{1,5},{5,9},{9,13},{13,1},{2,6},{6,10},{... | collective-permute-start | bytes 688136 | tf_op jit(solution)/shard_map/ppermute | solution.py:295
  3.7 2.6 %collective-permute-start.1 = (f32[64,896]{1,0:T(8,128)}, f32[64,896]{1,0:T(8,128)S(1)}, u32[]{:S(2)}, u32[]{:S(2)}) collective-permute-start(f32[64,896]{1,0:T(8,128)} %param.13), channel_id=1, source_target_pairs={{0,8},{4,12},{8,0},{12,4},{1,9},{5,13},{9,1},{13,5},{2,10},{6,14},... | collective-permute-start | bytes 688136 | tf_op jit(solution)/shard_map/ppermute | solution.py:295
  6.3 1.3 %collective-permute-start.2 = (f32[64,896]{1,0:T(8,128)}, f32[64,896]{1,0:T(8,128)S(1)}, u32[]{:S(2)}, u32[]{:S(2)}) collective-permute-start(f32[64,896]{1,0:T(8,128)} %param.13), channel_id=1, source_target_pairs={{0,12},{4,0},{8,4},{12,8},{1,13},{5,1},{9,5},{13,9},{2,14},{6,2},{... | collective-permute-start | bytes 688136 | tf_op jit(solution)/shard_map/ppermute | solution.py:295
  7.6 13.5 %incidence.1 = (bf16[16,2048,128]{2,1,0:T(8,128)(2,1)}, bf16[16,128,128]{2,1,0:T(8,128)(2,1)}, f32[64,2048]{1,0:T(8,128)}) custom-call(s32[16,16]{1,0:T(8,128)} %refs_0_.1, s32[16]{0:T(128)} %count_ref.1, s32[8,2048]{1,0:T(8,128)} %links_ref.1, s32[16,128]{1,0:T(8,128)} %comm_ref.1, s32[64,512]{1,0:T(8,128)} %demand_ref.1), custom_call_target="tpu_custom_call" | custom-call | flops 1000000000 | bytes 10000000 | tf_op jit(solution)/shard_map/incidence/pallas_call | solution.py:85
  22.6 13.2 %flows.1 = (f32[64,2048]{1,0:T(8,128)}, f32[16,3584]{1,0:T(8,128)}, f32[16,3584]{1,0:T(8,128)}, f32[16,3584]{1,0:T(8,128)}, f32[16,3584]{1,0:T(8,128)}, /*index=5*/f32[16,3584]{1,0:T(8,128)}) custom-call(s32[4]{0:T(128)} %pad_add_fusion.refs_0_, s32[16,16]{1,0:T(8,128)} %refs_0_.1, f32[1,64,896]{2,1,0:T(8,128)} %bitcast.12, f32[1,64,896]{2,1,0:T(8,128)} %bitcast.13, ...), custom_call_target="tpu_custom_call" | custom-call | flops 10000000000 | bytes 10000000 | tf_op jit(solution)/shard_map/flows/pallas_call | solution.py:180
  35.8 5.1 %collective-permute-start.3 = (f32[16,3584]{1,0:T(8,128)}, f32[16,3584]{1,0:T(8,128)S(1)}, u32[]{:S(2)}, u32[]{:S(2)}) collective-permute-start(f32[16,3584]{1,0:T(8,128)} %get-tuple-element.22), channel_id=1, source_target_pairs={{0,4},{4,8},{8,12},{12,0},{1,5},{5,9},{9,13},{13,1},{2,6},{6,10},{... | collective-permute-start | bytes 688136 | tf_op jit(solution)/shard_map/ppermute | solution.py:295
  40.9 1.6 %collective-permute-start.4 = (f32[16,3584]{1,0:T(8,128)}, f32[16,3584]{1,0:T(8,128)S(1)}, u32[]{:S(2)}, u32[]{:S(2)}) collective-permute-start(f32[16,3584]{1,0:T(8,128)} %get-tuple-element.23), channel_id=1, source_target_pairs={{0,8},{4,12},{8,0},{12,4},{1,9},{5,13},{9,1},{13,5},{2,10},{6,14},... | collective-permute-start | bytes 688136 | tf_op jit(solution)/shard_map/ppermute | solution.py:295
  42.5 0.8 collective-permute-start.5
  43.3 1.3 %collective-permute-start.6 = (f32[1,896]{1,0:T(1,128)S(1)}, f32[1,896]{1,0:T(1,128)S(1)}, u32[]{:S(2)}, u32[]{:S(2)}) collective-permute-start(f32[1,896]{1,0:T(1,128)S(1)} %broadcast_in_dim.27.refs_7_), channel_id=1, source_target_pairs={{0,4},{4,8},{8,12},{12,0},{1,5},{5,9},{9,13},{13,1},{2,6},{6,10},{... | collective-permute-start | bytes 10760 | tf_op jit(solution)/shard_map/ppermute | solution.py:295
  44.6 1.3 %collective-permute-start.7 = (f32[1,896]{1,0:T(1,128)S(1)}, f32[1,896]{1,0:T(1,128)S(1)}, u32[]{:S(2)}, u32[]{:S(2)}) collective-permute-start(f32[1,896]{1,0:T(1,128)S(1)} %broadcast_in_dim.27.refs_7_), channel_id=1, source_target_pairs={{0,8},{4,12},{8,0},{12,4},{1,9},{5,13},{9,1},{13,5},{2,10},{6,14},... | collective-permute-start | bytes 10760 | tf_op jit(solution)/shard_map/ppermute | solution.py:295
  45.9 11.1 %collective-permute-done.6.refs_8_ = f32[1,896]{1,0:T(1,128)S(1)} collective-permute-done((f32[1,896]{1,0:T(1,128)S(1)}, f32[1,896]{1,0:T(1,128)S(1)}, u32[]{:S(2)}, u32[]{:S(2)}) %collective-permute-start.6) | collective-permute-done | bytes 3616 | tf_op jit(solution)/shard_map/ppermute | solution.py:295
  57.7 4.2 %collective-permute-done.7.refs_9_ = f32[1,896]{1,0:T(1,128)S(1)} collective-permute-done((f32[1,896]{1,0:T(1,128)S(1)}, f32[1,896]{1,0:T(1,128)S(1)}, u32[]{:S(2)}, u32[]{:S(2)}) %collective-permute-start.7) | collective-permute-done | bytes 3616 | tf_op jit(solution)/shard_map/ppermute | solution.py:295
  61.9 1.2 %collective-permute-done.8.refs_10_ = f32[1,896]{1,0:T(1,128)S(1)} collective-permute-done((f32[1,896]{1,0:T(1,128)S(1)}, f32[1,896]{1,0:T(1,128)S(1)}, u32[]{:S(2)}, u32[]{:S(2)}) %collective-permute-start.8) | collective-permute-done | bytes 3616 | tf_op jit(solution)/shard_map/ppermute | solution.py:295
  63.9 2.4 %growth.1 = (f32[16,896]{1,0:T(8,128)}, f32[16,896]{1,0:T(8,128)}, f32[16,896]{1,0:T(8,128)}, f32[16,896]{1,0:T(8,128)}, f32[28,128]{1,0:T(8,128)}) custom-call(s32[4]{0:T(128)} %pad_add_fusion.refs_0_, f32[16,3584]{1,0:T(8,128)} %get-tuple-element.21.refs_1_, f32[16,3584]{1,0:T(8,128)} %copy-done.1, f32[16,3584]{1,0:T(8,128)} %copy-done.2, ...), custom_call_target="tpu_custom_call" | custom-call | tf_op jit(solution)/shard_map/growth/pallas_call | solution.py:237
  66.3 1.4 %collective-permute-done.12 = f32[28,128]{1,0:T(8,128)S(1)} collective-permute-done((f32[28,128]{1,0:T(8,128)}, f32[28,128]{1,0:T(8,128)S(1)}, u32[]{:S(2)}, u32[]{:S(2)}) %collective-permute-start.12) | collective-permute-done | bytes 14368 | tf_op jit(solution)/shard_map/ppermute | solution.py:291
  68.4 1.5 %collective-permute-start.13 = (f32[28,128]{1,0:T(8,128)S(1)}, f32[28,128]{1,0:T(8,128)S(1)}, u32[]{:S(2)}, u32[]{:S(2)}) collective-permute-start(f32[28,128]{1,0:T(8,128)S(1)} %add.41), channel_id=1, source_target_pairs={{0,2},{2,0},{1,3},{3,1},{4,6},{6,4},{5,7},{7,5},{8,10},{10,8},{9,1... | collective-permute-start | bytes 43016 | tf_op jit(solution)/shard_map/ppermute | solution.py:291
  69.8 2.3 %collective-permute-done.13 = f32[28,128]{1,0:T(8,128)S(1)} collective-permute-done((f32[28,128]{1,0:T(8,128)S(1)}, f32[28,128]{1,0:T(8,128)S(1)}, u32[]{:S(2)}, u32[]{:S(2)}) %collective-permute-start.13) | collective-permute-done | bytes 14368 | tf_op jit(solution)/shard_map/ppermute | solution.py:291
  72.1 2.4 %collective-permute-start.14 = (f32[28,128]{1,0:T(8,128)S(1)}, f32[28,128]{1,0:T(8,128)S(1)}, u32[]{:S(2)}, u32[]{:S(2)}) collective-permute-start(f32[28,128]{1,0:T(8,128)S(1)} %add.42), channel_id=1, source_target_pairs={{0,4},{4,0},{8,12},{12,8},{1,5},{5,1},{9,13},{13,9},{2,6},{6,2},{1... | collective-permute-start | bytes 43016 | tf_op jit(solution)/shard_map/ppermute | solution.py:291
  74.6 3.4 %collective-permute-start.10 = (f32[16,896]{1,0:T(8,128)}, f32[16,896]{1,0:T(8,128)S(1)}, u32[]{:S(2)}, u32[]{:S(2)}) collective-permute-start(f32[16,896]{1,0:T(8,128)} %get-tuple-element.28), channel_id=1, source_target_pairs={{0,8},{4,12},{8,0},{12,4},{1,9},{5,13},{9,1},{13,5},{2,10},{6,14},... | collective-permute-start | bytes 172040 | tf_op jit(solution)/shard_map/ppermute | solution.py:295
  78.0 1.0 %collective-permute-start.11 = (f32[16,896]{1,0:T(8,128)}, f32[16,896]{1,0:T(8,128)S(1)}, u32[]{:S(2)}, u32[]{:S(2)}) collective-permute-start(f32[16,896]{1,0:T(8,128)} %get-tuple-element.29), channel_id=1, source_target_pairs={{0,12},{4,0},{8,4},{12,8},{1,13},{5,1},{9,5},{13,9},{2,14},{6,2},{... | collective-permute-start | bytes 172040 | tf_op jit(solution)/shard_map/ppermute | solution.py:295
  79.0 1.4 %collective-permute-start.15 = (f32[28,128]{1,0:T(8,128)S(1)}, f32[28,128]{1,0:T(8,128)S(1)}, u32[]{:S(2)}, u32[]{:S(2)}) collective-permute-start(f32[28,128]{1,0:T(8,128)S(1)} %add.43.refs_1_), channel_id=1, source_target_pairs={{0,8},{4,12},{8,0},{12,4},{1,9},{5,13},{9,1},{13,5},{2,10},{6,14},... | collective-permute-start | bytes 43016 | tf_op jit(solution)/shard_map/ppermute | solution.py:291
  80.5 0.8 constant_dynamic-update-slice_fusion.3
  81.3 2.4 %collective-permute-done.15.refs_2_ = f32[28,128]{1,0:T(8,128)S(1)} collective-permute-done((f32[28,128]{1,0:T(8,128)S(1)}, f32[28,128]{1,0:T(8,128)S(1)}, u32[]{:S(2)}, u32[]{:S(2)}) %collective-permute-start.15) | collective-permute-done | bytes 14368 | tf_op jit(solution)/shard_map/ppermute | solution.py:291
  84.3 5.5 %robust.1 = f32[16,128]{1,0:T(8,128)} custom-call(s32[16,16]{1,0:T(8,128)} %refs_0_.1, f32[28,128]{1,0:T(8,128)} %copy-done.4, f32[28,128]{1,0:T(8,128)} %copy-done.5, bf16[16,2048,128]{2,1,0:T(8,128)(2,1)} %get-tuple-element.17.refs_6_.refs_3_), custom_call_target="tpu_custom_call" | custom-call | tf_op jit(solution)/shard_map/robust/pallas_call | solution.py:275
  (53 shorter events, 5.1 us)
Async XLA Ops:
  0.6 21.1 %collective-permute-start = (f32[64,896]{1,0:T(8,128)}, f32[64,896]{1,0:T(8,128)S(1)}, u32[]{:S(2)}, u32[]{:S(2)}) collective-permute-start(f32[64,896]{1,0:T(8,128)} %param.13), channel_id=1, source_target_pairs={{0,4},{4,8},{8,12},{12,0},{1,5},{5,9},{9,13},{13,1},{2,6},{6,10},{... | collective-permute-start | bytes 688136 | tf_op jit(solution)/shard_map/ppermute | solution.py:295
  3.7 18.0 %collective-permute-start.1 = (f32[64,896]{1,0:T(8,128)}, f32[64,896]{1,0:T(8,128)S(1)}, u32[]{:S(2)}, u32[]{:S(2)}) collective-permute-start(f32[64,896]{1,0:T(8,128)} %param.13), channel_id=1, source_target_pairs={{0,8},{4,12},{8,0},{12,4},{1,9},{5,13},{9,1},{13,5},{2,10},{6,14},... | collective-permute-start | bytes 688136 | tf_op jit(solution)/shard_map/ppermute | solution.py:295
  6.3 15.5 %collective-permute-start.2 = (f32[64,896]{1,0:T(8,128)}, f32[64,896]{1,0:T(8,128)S(1)}, u32[]{:S(2)}, u32[]{:S(2)}) collective-permute-start(f32[64,896]{1,0:T(8,128)} %param.13), channel_id=1, source_target_pairs={{0,12},{4,0},{8,4},{12,8},{1,13},{5,1},{9,5},{13,9},{2,14},{6,2},{... | collective-permute-start | bytes 688136 | tf_op jit(solution)/shard_map/ppermute | solution.py:295
  21.8 0.8 copy-start.14
  22.6 20.7 %copy-start.7 = (f32[896]{0:T(1024)S(1)}, f32[896]{0:T(1024)}, u32[]{:S(2)}) copy-start(f32[896]{0:T(1024)} %param.14) | copy-start | bytes 10756
  22.6 34.4 %copy-start.11 = (f32[64]{0:T(128)S(1)}, f32[64]{0:T(128)}, u32[]{:S(2)}) copy-start(f32[64]{0:T(128)} %param.15) | copy-start | bytes 772
  35.8 27.2 %collective-permute-start.3 = (f32[16,3584]{1,0:T(8,128)}, f32[16,3584]{1,0:T(8,128)S(1)}, u32[]{:S(2)}, u32[]{:S(2)}) collective-permute-start(f32[16,3584]{1,0:T(8,128)} %get-tuple-element.22), channel_id=1, source_target_pairs={{0,4},{4,8},{8,12},{12,0},{1,5},{5,9},{9,13},{13,1},{2,6},{6,10},{... | collective-permute-start | bytes 688136 | tf_op jit(solution)/shard_map/ppermute | solution.py:295
  40.9 22.2 %collective-permute-start.4 = (f32[16,3584]{1,0:T(8,128)}, f32[16,3584]{1,0:T(8,128)S(1)}, u32[]{:S(2)}, u32[]{:S(2)}) collective-permute-start(f32[16,3584]{1,0:T(8,128)} %get-tuple-element.23), channel_id=1, source_target_pairs={{0,8},{4,12},{8,0},{12,4},{1,9},{5,13},{9,1},{13,5},{2,10},{6,14},... | collective-permute-start | bytes 688136 | tf_op jit(solution)/shard_map/ppermute | solution.py:295
  42.5 20.6 %collective-permute-start.5 = (f32[16,3584]{1,0:T(8,128)}, f32[16,3584]{1,0:T(8,128)S(1)}, u32[]{:S(2)}, u32[]{:S(2)}) collective-permute-start(f32[16,3584]{1,0:T(8,128)} %get-tuple-element.24), channel_id=1, source_target_pairs={{0,12},{4,0},{8,4},{12,8},{1,13},{5,1},{9,5},{13,9},{2,14},{6,2},{... | collective-permute-start | bytes 688136 | tf_op jit(solution)/shard_map/ppermute | solution.py:295
  43.3 19.8 %copy-start.6 = (f32[1,896]{1,0:T(1,128)}, f32[1,896]{1,0:T(1,128)S(1)}, u32[]{:S(2)}) copy-start(f32[1,896]{1,0:T(1,128)S(1)} %broadcast_in_dim.27.refs_7_) | copy-start | bytes 10756
  43.3 13.7 %collective-permute-start.6 = (f32[1,896]{1,0:T(1,128)S(1)}, f32[1,896]{1,0:T(1,128)S(1)}, u32[]{:S(2)}, u32[]{:S(2)}) collective-permute-start(f32[1,896]{1,0:T(1,128)S(1)} %broadcast_in_dim.27.refs_7_), channel_id=1, source_target_pairs={{0,4},{4,8},{8,12},{12,0},{1,5},{5,9},{9,13},{13,1},{2,6},{6,10},{... | collective-permute-start | bytes 10760 | tf_op jit(solution)/shard_map/ppermute | solution.py:295
  44.6 17.3 %collective-permute-start.7 = (f32[1,896]{1,0:T(1,128)S(1)}, f32[1,896]{1,0:T(1,128)S(1)}, u32[]{:S(2)}, u32[]{:S(2)}) collective-permute-start(f32[1,896]{1,0:T(1,128)S(1)} %broadcast_in_dim.27.refs_7_), channel_id=1, source_target_pairs={{0,8},{4,12},{8,0},{12,4},{1,9},{5,13},{9,1},{13,5},{2,10},{6,14},... | collective-permute-start | bytes 10760 | tf_op jit(solution)/shard_map/ppermute | solution.py:295
  57.0 6.1 %copy-start.8 = (f32[1,896]{1,0:T(1,128)}, f32[1,896]{1,0:T(1,128)S(1)}, u32[]{:S(2)}) copy-start(f32[1,896]{1,0:T(1,128)S(1)} %collective-permute-done.6.refs_8_) | copy-start | bytes 10756
  57.0 6.1 %collective-permute-start.8 = (f32[1,896]{1,0:T(1,128)S(1)}, f32[1,896]{1,0:T(1,128)S(1)}, u32[]{:S(2)}, u32[]{:S(2)}) collective-permute-start(f32[1,896]{1,0:T(1,128)S(1)} %broadcast_in_dim.27.refs_7_), channel_id=1, source_target_pairs={{0,12},{4,0},{8,4},{12,8},{1,13},{5,1},{9,5},{13,9},{2,14},{6,2},{... | collective-permute-start | bytes 10760 | tf_op jit(solution)/shard_map/ppermute | solution.py:295
  61.9 1.2 %copy-start.9 = (f32[1,896]{1,0:T(1,128)}, f32[1,896]{1,0:T(1,128)S(1)}, u32[]{:S(2)}) copy-start(f32[1,896]{1,0:T(1,128)S(1)} %collective-permute-done.7.refs_9_) | copy-start | bytes 10756
  63.1 0.8 copy-start.3
  66.3 1.4 %collective-permute-start.12 = (f32[28,128]{1,0:T(8,128)}, f32[28,128]{1,0:T(8,128)S(1)}, u32[]{:S(2)}, u32[]{:S(2)}) collective-permute-start(f32[28,128]{1,0:T(8,128)} %get-tuple-element.30), channel_id=1, source_target_pairs={{0,1},{1,0},{2,3},{3,2},{4,5},{5,4},{6,7},{7,6},{8,9},{9,8},{10,11... | collective-permute-start | bytes 43016 | tf_op jit(solution)/shard_map/ppermute | solution.py:291
  68.4 3.7 %collective-permute-start.13 = (f32[28,128]{1,0:T(8,128)S(1)}, f32[28,128]{1,0:T(8,128)S(1)}, u32[]{:S(2)}, u32[]{:S(2)}) collective-permute-start(f32[28,128]{1,0:T(8,128)S(1)} %add.41), channel_id=1, source_target_pairs={{0,2},{2,0},{1,3},{3,1},{4,6},{6,4},{5,7},{7,5},{8,10},{10,8},{9,1... | collective-permute-start | bytes 43016 | tf_op jit(solution)/shard_map/ppermute | solution.py:291
  72.1 6.9 %collective-permute-start.14 = (f32[28,128]{1,0:T(8,128)S(1)}, f32[28,128]{1,0:T(8,128)S(1)}, u32[]{:S(2)}, u32[]{:S(2)}) collective-permute-start(f32[28,128]{1,0:T(8,128)S(1)} %add.42), channel_id=1, source_target_pairs={{0,4},{4,0},{8,12},{12,8},{1,5},{5,1},{9,13},{13,9},{2,6},{6,2},{1... | collective-permute-start | bytes 43016 | tf_op jit(solution)/shard_map/ppermute | solution.py:291
  74.5 15.3 %collective-permute-start.9 = (f32[16,896]{1,0:T(8,128)}, f32[16,896]{1,0:T(8,128)S(1)}, u32[]{:S(2)}, u32[]{:S(2)}) collective-permute-start(f32[16,896]{1,0:T(8,128)} %get-tuple-element.27), channel_id=1, source_target_pairs={{0,4},{4,8},{8,12},{12,0},{1,5},{5,9},{9,13},{13,1},{2,6},{6,10},{... | collective-permute-start | bytes 172040 | tf_op jit(solution)/shard_map/ppermute | solution.py:295
  74.6 15.3 %collective-permute-start.10 = (f32[16,896]{1,0:T(8,128)}, f32[16,896]{1,0:T(8,128)S(1)}, u32[]{:S(2)}, u32[]{:S(2)}) collective-permute-start(f32[16,896]{1,0:T(8,128)} %get-tuple-element.28), channel_id=1, source_target_pairs={{0,8},{4,12},{8,0},{12,4},{1,9},{5,13},{9,1},{13,5},{2,10},{6,14},... | collective-permute-start | bytes 172040 | tf_op jit(solution)/shard_map/ppermute | solution.py:295
  78.0 11.9 %collective-permute-start.11 = (f32[16,896]{1,0:T(8,128)}, f32[16,896]{1,0:T(8,128)S(1)}, u32[]{:S(2)}, u32[]{:S(2)}) collective-permute-start(f32[16,896]{1,0:T(8,128)} %get-tuple-element.29), channel_id=1, source_target_pairs={{0,12},{4,0},{8,4},{12,8},{1,13},{5,1},{9,5},{13,9},{2,14},{6,2},{... | collective-permute-start | bytes 172040 | tf_op jit(solution)/shard_map/ppermute | solution.py:295
  79.0 4.7 %copy-start.4 = (f32[28,128]{1,0:T(8,128)}, f32[28,128]{1,0:T(8,128)S(1)}, u32[]{:S(2)}) copy-start(f32[28,128]{1,0:T(8,128)S(1)} %add.43.refs_1_) | copy-start | bytes 43012
  79.0 4.7 %collective-permute-start.15 = (f32[28,128]{1,0:T(8,128)S(1)}, f32[28,128]{1,0:T(8,128)S(1)}, u32[]{:S(2)}, u32[]{:S(2)}) collective-permute-start(f32[28,128]{1,0:T(8,128)S(1)} %add.43.refs_1_), channel_id=1, source_target_pairs={{0,8},{4,12},{8,0},{12,4},{1,9},{5,13},{9,1},{13,5},{2,10},{6,14},... | collective-permute-start | bytes 43016 | tf_op jit(solution)/shard_map/ppermute | solution.py:291
  (7 other events, 4.8 us)

commit v2 on v0

v2 whole, which is shorter than its diff:
```python
import jax
import jax.numpy as jnp
from jax import lax
from jax.experimental import pallas as pl
from jax.experimental.pallas import tpu as pltpu
from jax.sharding import PartitionSpec as P

PATHS_PER_BLOCK = 128
LB = 128
MAXT = 16
COMMODITY_BLOCK = 32
S = 256

SOFTMIN_RATE = 0.25
STEP_RATE = 1.0
DEMAND_UNIT = 0.0625
MIB = 1024 * 1024

F32 = jnp.float32
BF16 = jnp.bfloat16
PACK = 16
BATCH = 16
GROUP = LB // COMMODITY_BLOCK

SCALARS = pl.BlockSpec(memory_space=pltpu.SMEM)
ARRAY = pl.BlockSpec(memory_space=pltpu.VMEM)
LISTS = 4


def split(x):
    high = x.astype(BF16)
    return high, (x - high.astype(F32)).astype(BF16)


def stacked(x):
    return jnp.concatenate(split(x), axis=0)


def aligned(start, size, unit):
    return pl.ds(pl.multiple_of(start * unit, unit), size)


def incidence_kernel(*refs):
    given, (hits_ref, turned_ref, list_ref, total_ref, same_ref, wanted_ref) = refs[:5], refs[5:11]
    local, arrived = refs[11:16], refs[16]
    copies = [pltpu.make_async_copy(a, b, arrived.at[i]) for i, (a, b) in enumerate(zip(given, local))]
    for copy in copies:
        copy.start()
    for copy in copies:
        copy.wait()
    tiles_ref, count_ref, links_ref, comm_ref, demand_ref = local
    blocks = tiles_ref.shape[0]
    lanes = [(lax.broadcasted_iota(jnp.int32, (PACK, LB), 0) + PACK * g).astype(F32).astype(BF16) for g in range(LB // PACK)]
    one, zero = jnp.ones((PACK, PATHS_PER_BLOCK), BF16), jnp.zeros((PACK, PATHS_PER_BLOCK), BF16)
    spare = blocks * MAXT

    for ref in (hits_ref, turned_ref):
        ref[spare * LB :, :] = jnp.zeros((2 * LB, LB), BF16)

    def one_block(block, entry):
        links = links_ref[:, aligned(block, PATHS_PER_BLOCK, PATHS_PER_BLOCK)]
        live = count_ref[block]

        def one_pair(pair, entry):
            slot = block * MAXT + 2 * pair
            list_ref[0, entry] = slot
            list_ref[1, entry] = block
            for side in range(2):
                tile = tiles_ref[block, 2 * pair + side]
                list_ref[2 + side, entry] = tile
                first = jnp.where(2 * pair + side < live, tile * LB, 1 << 20)
                place = (links - first).astype(F32)
                counts = None
                for h in range(links.shape[0]):
                    row = jnp.broadcast_to(place[h : h + 1, :], (PACK, PATHS_PER_BLOCK)).astype(BF16)
                    hit = [jnp.where(row == lane, one, zero) for lane in lanes]
                    counts = hit if counts is None else [a + b for a, b in zip(counts, hit)]
                table = jnp.concatenate(counts, axis=0)
                where = aligned(slot + side, LB, LB)
                hits_ref[where, :] = table
                turned_ref[where, :] = table.T
            return entry + 1

        return lax.fori_loop(0, (live + 1) // 2, one_pair, entry)

    entries = lax.fori_loop(0, blocks, one_block, 0)
    batches = (entries + BATCH - 1) // BATCH
    total_ref[0] = batches

    def pad(entry, carry):
        list_ref[0, entry] = spare
        for i in range(1, LISTS):
            list_ref[i, entry] = 0
        return carry

    lax.fori_loop(entries, batches * BATCH, pad, 0)

    commodity_rows = lax.broadcasted_iota(jnp.int32, (LB, PATHS_PER_BLOCK), 0)
    for block in range(blocks):
        group, j = block // GROUP, block % GROUP
        demand = demand_ref[:, group * LB : (group + 1) * LB].astype(F32).astype(BF16)
        onehot = (commodity_rows == comm_ref[block : block + 1, :] + COMMODITY_BLOCK * j).astype(F32).astype(BF16)
        same = lax.dot_general(onehot, onehot, (((0,), (0,)), ((), ())), preferred_element_type=F32)
        same_ref[block] = same.astype(BF16)
        wanted = jnp.dot(demand, onehot, preferred_element_type=F32)
        wanted_ref[block] = wanted * DEMAND_UNIT


def build_incidence(path_links, block_tiles, block_count, path_commodity, demand):
    blocks = block_tiles.shape[0]
    rows = demand.shape[0]
    slots = blocks * MAXT + 2
    given = (block_tiles, block_count, path_links, path_commodity, demand)
    given = tuple(pltpu.with_memory_space_constraint(a, pltpu.HBM) for a in given)
    return pl.pallas_call(
        incidence_kernel,
        in_specs=[pl.BlockSpec(memory_space=pltpu.HBM)] * 5,
        out_specs=[ARRAY, ARRAY, SCALARS, SCALARS, ARRAY, ARRAY],
        scratch_shapes=[pltpu.SMEM(a.shape, a.dtype) for a in given[:2]]
        + [pltpu.VMEM(a.shape, a.dtype) for a in given[2:]]
        + [pltpu.SemaphoreType.DMA((5,))],
        out_shape=[
            jax.ShapeDtypeStruct((slots * LB, PATHS_PER_BLOCK), BF16),
            jax.ShapeDtypeStruct((slots * PATHS_PER_BLOCK, LB), BF16),
            jax.ShapeDtypeStruct((LISTS, blocks * MAXT // 2 + BATCH), jnp.int32),
            jax.ShapeDtypeStruct((1,), jnp.int32),
            jax.ShapeDtypeStruct((blocks, PATHS_PER_BLOCK, PATHS_PER_BLOCK), BF16),
            jax.ShapeDtypeStruct((blocks, rows, PATHS_PER_BLOCK), F32),
        ],
        compiler_params=pltpu.CompilerParams(vmem_limit_bytes=8 * MIB),
        cost_estimate=pl.CostEstimate(flops=10**9, bytes_accessed=25 * 10**6, transcendentals=0),
        name="incidence",
    )(*given)


def sweep(list_ref, total_ref, hits_ref, turned_ref, same_ref, wanted_at, put_flow, split_ref, cost_ref, flow_ref, load_ref):
    blocks, rows2, _ = cost_ref.shape
    rows = rows2 // 2
    load_ref[...] = jnp.zeros_like(load_ref)
    cost_ref[...] = jnp.zeros_like(cost_ref)
    batches = total_ref[0]

    def cost_batch(batch, carry):
        done = []
        for j in range(BATCH):
            slot, block, left, right = (list_ref[i, batch * BATCH + j] for i in range(LISTS))
            chosen = jnp.concatenate([split_ref[left], split_ref[right]], axis=1)
            done.append((block, jnp.dot(chosen, hits_ref[aligned(slot, 2 * LB, LB), :], preferred_element_type=F32)))
        for block, cost in done:
            cost_ref[block] += cost
        return carry

    lax.fori_loop(0, batches, cost_batch, 0)

    for block in range(blocks):
        weight = jnp.exp(-SOFTMIN_RATE * (cost_ref[block, :rows] + cost_ref[block, rows:]))
        total = jnp.dot(stacked(weight), same_ref[block], preferred_element_type=F32)
        flow = wanted_at(block) * weight / (total[:rows] + total[rows:])
        put_flow(block, flow)
        flow_ref[block] = stacked(flow)

    def load_batch(batch, carry):
        done = []
        for j in range(BATCH):
            slot, block, left, right = (list_ref[i, batch * BATCH + j] for i in range(LISTS))
            for side, tile in enumerate((left, right)):
                turned = turned_ref[aligned(slot + side, LB, LB), :]
                done.append((tile, jnp.dot(flow_ref[block], turned, preferred_element_type=F32)))
        for tile, load in done:
            load_ref[tile] += load
        return carry

    lax.fori_loop(0, batches, load_batch, 0)


def spread(split_ref, first, shard):
    for k in range(shard.shape[-1] // LB):
        split_ref[first + k] = stacked(shard[:, k * LB : (k + 1) * LB])


def path_columns(block):
    return slice(block * PATHS_PER_BLOCK, (block + 1) * PATHS_PER_BLOCK)


def sweep_scratch(rows, tiles, blocks):
    return [
        pltpu.VMEM((tiles, 2 * rows, LB), BF16),
        pltpu.VMEM((blocks, 2 * rows, PATHS_PER_BLOCK), F32),
        pltpu.VMEM((blocks, 2 * rows, PATHS_PER_BLOCK), BF16),
        pltpu.VMEM((tiles, 2 * rows, LB), F32),
    ]


SWEEP_COST = pl.CostEstimate(flops=10**9, bytes_accessed=25 * 10**6, transcendentals=10**5)


def half_kernel(far, n, list_ref, total_ref, *refs):
    pieces, (hits_ref, turned_ref, same_ref, wanted_ref) = refs[:n], refs[n : n + 4]
    flows_ref, mine_ref, other_ref, *scratch = refs[-7:]
    z = lax.axis_index("path")
    rows = scratch[0].shape[1] // 2
    side = lax.div(z, 2)
    side = 1 - side if far else side
    shard_tiles = pieces[0].shape[1] // LB
    for m, piece in enumerate(pieces):
        start = side if piece.shape[0] == 2 * rows else 0
        spread(scratch[0], (z ^ m) * shard_tiles, piece[aligned(start, rows, rows), :])

    def wanted_at(block):
        return wanted_ref[block, aligned(side, rows, rows), :]

    def put_flow(block, flow):
        if far:
            flows_ref[:, path_columns(block)] = flow
        else:
            flows_ref[aligned(side, rows, rows), path_columns(block)] = flow

    if not far:
        flows_ref[aligned(1 - side, rows, rows), :] = refs[n + 4][...]
    sweep(list_ref, total_ref, hits_ref, turned_ref, same_ref, wanted_at, put_flow, *scratch)
    load_ref = scratch[3]
    height = rows // 2
    for out_ref, place in ((mine_ref, lax.rem(z, 2)), (other_ref, 1 - lax.rem(z, 2))):
        for k in range(load_ref.shape[0]):
            high = load_ref[k, aligned(place, height, height), :]
            out_ref[k] = high + load_ref[k, pl.ds(pl.multiple_of(rows + place * height, height), height), :]


def half_sweep(pieces, rows, built, far_flows=None):
    hits, turned, pairs, total, same, wanted = built
    own = pieces[0].shape[1]
    n = len(pieces)
    blocks = wanted.shape[0]
    tiles = n * own // LB
    far = far_flows is None
    extra = [] if far else [far_flows]
    return pl.pallas_call(
        lambda *refs: half_kernel(far, n, *refs),
        in_specs=[SCALARS, SCALARS] + [ARRAY] * (n + 4 + len(extra)),
        out_specs=[ARRAY] * 3,
        out_shape=[jax.ShapeDtypeStruct((rows if far else 2 * rows, blocks * PATHS_PER_BLOCK), F32)]
        + [jax.ShapeDtypeStruct((tiles, rows // 2, LB), F32)] * 2,
        scratch_shapes=sweep_scratch(rows, tiles, blocks),
        compiler_params=pltpu.CompilerParams(vmem_limit_bytes=16 * MIB),
        cost_estimate=SWEEP_COST,
        name="far_sweep" if far else "near_sweep",
    )(pairs, total, *pieces, hits, turned, same, wanted, *extra)


def wide_kernel(list_ref, total_ref, lengths_ref, hits_ref, turned_ref, same_ref, wanted_ref, flows_ref, out_ref, *scratch):
    shards, _, own = lengths_ref.shape
    rows = lengths_ref.shape[1]

    def one_shard(i, carry):
        spread(scratch[0], i * (own // LB), lengths_ref[i])
        return carry

    lax.fori_loop(0, shards, one_shard, 0)

    def put_flow(block, flow):
        flows_ref[:, path_columns(block)] = flow

    sweep(
        list_ref, total_ref, hits_ref, turned_ref, same_ref, lambda block: wanted_ref[block], put_flow, *scratch
    )
    out_ref[...] = scratch[3][:, :rows, :] + scratch[3][:, rows:, :]


def wide_sweep(lengths, built):
    hits, turned, pairs, total, same, wanted = built
    shards, rows, own = lengths.shape
    blocks = wanted.shape[0]
    tiles = shards * own // LB
    return pl.pallas_call(
        wide_kernel,
        in_specs=[SCALARS, SCALARS] + [ARRAY] * 5,
        out_specs=[ARRAY] * 2,
        out_shape=[
            jax.ShapeDtypeStruct((rows, blocks * PATHS_PER_BLOCK), F32),
            jax.ShapeDtypeStruct((tiles, rows, LB), F32),
        ],
        scratch_shapes=sweep_scratch(rows, tiles, blocks),
        compiler_params=pltpu.CompilerParams(vmem_limit_bytes=48 * MIB),
        cost_estimate=SWEEP_COST,
        name="wide_sweep",
    )(pairs, total, lengths, hits, turned, same, wanted)


def growth_kernel(n, parts, *refs):
    lengths, capacities, weight_ref = refs[:n], refs[n : 2 * n], refs[2 * n]
    loads = refs[2 * n + 1 : 2 * n + 1 + parts]
    next_refs, mixed_ref, grown_ref = refs[-n - 2 : -2], refs[-2], refs[-1]
    z = lax.axis_index("path")
    links_total, height, _ = grown_ref.shape
    shard_tiles = links_total // n
    total = jnp.zeros((height, LB), F32)
    for m in range(n):
        row = aligned(z if lengths[m].shape[0] == n * height else lax.rem(z, 2), height, height)
        first = (z ^ m) * shard_tiles
        for k in range(shard_tiles):
            columns = slice(k * LB, (k + 1) * LB)
            load = loads[0][first + k]
            for ref in loads[1:]:
                load = load + ref[first + k]
            grown = lengths[m][row, columns] * jnp.exp(STEP_RATE * load / capacities[m][-1:, columns])
            grown_ref[m * shard_tiles + k] = grown
            total = total + grown
    factor = (links_total * LB) / jnp.sum(total, axis=1, keepdims=True)
    weight = weight_ref[aligned(z, height, height), :]
    for m in range(n):
        first = (z ^ m) * shard_tiles
        for k in range(shard_tiles):
            new = grown_ref[m * shard_tiles + k] * factor
            next_refs[m][:, k * LB : (k + 1) * LB] = new
            mixed_ref[pl.ds(first + k, 1), :] = jnp.sum(weight * new, axis=0, keepdims=True)


def grow(loads, lengths, capacities, weights):
    n, parts = len(lengths), len(loads)
    tiles, height, _ = loads[0].shape
    return pl.pallas_call(
        lambda *refs: growth_kernel(n, parts, *refs),
        in_specs=[ARRAY] * (2 * n + 1 + parts),
        out_specs=[ARRAY] * (n + 1),
        out_shape=[jax.ShapeDtypeStruct((height, tiles * LB // n), F32)] * n + [jax.ShapeDtypeStruct((tiles, LB), F32)],
        scratch_shapes=[pltpu.VMEM((tiles, height, LB), F32)],
        compiler_params=pltpu.CompilerParams(vmem_limit_bytes=8 * MIB),
        cost_estimate=pl.CostEstimate(flops=10**6, bytes_accessed=5 * 10**6, transcendentals=10**5),
        name="growth",
    )(*lengths, *capacities, weights, *loads)


def robust_kernel(parts, list_ref, total_ref, links_ref, *refs):
    part_refs, (out_ref, mixed_ref, cost_ref) = refs[:parts], refs[parts:]
    blocks = out_ref.shape[0]
    mixed = part_refs[0][...]
    for ref in part_refs[1:]:
        mixed = mixed + ref[...]
    mixed_ref[...] = mixed
    cost_ref[...] = jnp.zeros_like(cost_ref)
    spare = blocks * MAXT

    def batch_step(batch, carry):
        done = []
        for j in range(BATCH):
            slot, block, left, right = (list_ref[i, batch * BATCH + j] for i in range(LISTS))
            links = links_ref[:, aligned(block, PATHS_PER_BLOCK, PATHS_PER_BLOCK)]
            for tile in (left, right):
                place = links - jnp.where(slot < spare, tile * LB, 1 << 20)
                table = jnp.broadcast_to(mixed_ref[pl.ds(tile, 1), :], links.shape)
                found = jnp.take_along_axis(table, place & (LB - 1), axis=1)
                done.append((block, jnp.where((place >= 0) & (place < LB), found, 0.0)))
        for block, cost in done:
            cost_ref[block] += cost
        return carry

    lax.fori_loop(0, total_ref[0], batch_step, 0)
    for block in range(blocks):
        out_ref[block : block + 1, :] = jnp.sum(cost_ref[block], axis=0, keepdims=True) / S


def robust_costs(path_links, built, parts):
    _, _, pairs, total, _, wanted = built
    blocks = wanted.shape[0]
    hops = path_links.shape[0]
    out = pl.pallas_call(
        lambda *refs: robust_kernel(len(parts), *refs),
        in_specs=[SCALARS, SCALARS] + [ARRAY] * (len(parts) + 1),
        out_specs=ARRAY,
        out_shape=jax.ShapeDtypeStruct((blocks, PATHS_PER_BLOCK), F32),
        scratch_shapes=[pltpu.VMEM(parts[0].shape, F32), pltpu.VMEM((blocks, hops, PATHS_PER_BLOCK), F32)],
        compiler_params=pltpu.CompilerParams(vmem_limit_bytes=8 * MIB),
        cost_estimate=pl.CostEstimate(flops=10**8, bytes_accessed=10**7, transcendentals=0),
        name="robust",
    )(pairs, total, path_links, *parts)
    return out.reshape(-1)


def exchange(x, axis, n, bit):
    return lax.ppermute(x, axis, [(i, i ^ bit) for i in range(n)])


def body_paired(sizes, path_links, block_tiles, block_count, path_commodity, demand, lengths, capacity, scenario_weight):
    n = sizes["path"]
    rows, own = lengths.shape
    half, height = rows // 2, rows // n
    z = lax.axis_index("path").astype(jnp.int32)
    side = z // 2
    far = lax.dynamic_slice(lengths, ((1 - side) * half, 0), (half, own))
    far = jnp.concatenate([far, jnp.broadcast_to(capacity[None, :], (8, own))], axis=0)
    near = lax.dynamic_slice(lengths, (side * half, 0), (half, own))

    def swap(x, m):
        return exchange(x, "path", n, m)

    shared = swap(lengths, 1)
    far_pieces = [lengths, shared, swap(near, 2), swap(near, 3)]
    near_pieces = [lengths, shared, swap(far, 2), swap(far, 3)]
    built = build_incidence(path_links, block_tiles, block_count, path_commodity, demand)
    far_flows, straight, crossed = half_sweep(far_pieces, half, built)
    partial = straight + swap(crossed, 1)
    flows, mine, other = half_sweep(near_pieces, half, built, far_flows)
    loads = [mine, swap(other, 1), swap(partial, 2)]
    capacity_row = capacity[None, :]
    capacities = [capacity_row, swap(capacity_row, 1), near_pieces[2], near_pieces[3]]
    *new, mixed = grow(loads, near_pieces, capacities, scenario_weight[:, None])
    mixed = mixed + exchange(mixed, "sub", 2, 1)
    mixed = mixed + exchange(mixed, "scen", 2, 1)
    mixed = mixed + swap(mixed, 1)
    parts = [mixed, swap(mixed, 2)]
    arrived = [new[0]] + [swap(new[m], m) for m in range(1, n)]
    robust = robust_costs(path_links, built, parts)
    lengths_next = jnp.zeros((rows, own), F32)
    for m in range(n):
        lengths_next = lax.dynamic_update_slice(lengths_next, arrived[m], ((z ^ m) * height, 0))
    return flows, lengths_next, robust


def body_wide(sizes, path_links, block_tiles, block_count, path_commodity, demand, lengths, capacity, scenario_weight):
    gathered = lax.all_gather(lengths, "path", axis=0, tiled=False)
    built = build_incidence(path_links, block_tiles, block_count, path_commodity, demand)
    flows, loads = wide_sweep(gathered, built)
    loads = loads.transpose(1, 0, 2).reshape(lengths.shape[0], -1)
    own_loads = lax.psum_scatter(loads, "path", scatter_dimension=1, tiled=True)
    grown = lengths * jnp.exp(STEP_RATE * own_loads / capacity[None, :])
    totals = lax.psum(jnp.sum(grown, axis=1), "path")
    lengths_next = grown * (loads.shape[1] / totals)[:, None]
    mixed = lax.psum(jnp.sum(lengths_next * scenario_weight[:, None], axis=0), ("scen", "sub"))
    mixed = lax.all_gather(mixed.reshape(-1, LB), "path", axis=0, tiled=True)
    return flows, lengths_next, robust_costs(path_links, built, [mixed])


def solution(mesh):
    sizes = dict(mesh.shape)

    def body(*args):
        paired = sizes["path"] == 4 and sizes["scen"] == 2 and sizes["sub"] == 2 and args[5].shape[0] % 64 == 0
        return (body_paired if paired else body_wide)(sizes, *args)

    return jax.shard_map(
        body,
        mesh=mesh,
        in_specs=(
            P(None, ("grp", "path")),
            P(("grp", "path"), None),
            P(("grp", "path")),
            P(("grp", "path"), None),
            P(("scen", "sub"), ("grp", "path")),
            P(("scen", "sub"), ("grp", "path")),
            P(("grp", "path")),
            P(("grp", "scen", "sub")),
        ),
        out_specs=(
            P(("scen", "sub"), ("grp", "path")),
            P(("scen", "sub"), ("grp", "path")),
            P(("grp", "path")),
        ),
        check_vma=False,
    )
```

time: 395 us -> 67.5 us (0.17); the launches traced: 390 us -> 66.8 us
  matrix products: 106 us -> 0 us
  other arithmetic: 106 us -> 0.05 us
  local copies, waits for them, and re-layouts: 80.8 us -> 3.47 us
  blocking collectives: 57.4 us -> 0 us
  starting transfers between devices: 0.04 us -> 25.5 us
  Pallas kernels: 0 us -> 21.8 us
  between operations: 14.1 us -> 0.83 us
  waiting for transfers between devices: 23 us -> 15.2 us
    dot_general x144 -> x0, matrix products: 106 us -> none  [the longest x32 44.3 us: tile_costs(): return jnp.einsum('stl,ptl->sp', chosen, tile_hits, precision=PRECISE)]
    and x48 -> x0, other arithmetic: 45.7 us -> none  [the longest x32 42.4 us: tile_costs(): chosen = jnp.take(table_grid, tile_ids, axis=1)]
    dynamic_slice x96 -> x1, local copies, waits for them, and re-layouts: 44.7 us -> 0.99 us  [body_paired(): near = lax.dynamic_slice(lengths, (side * half, 0), (half, own))]
    all_gather x2 -> x0, blocking collectives: 41.3 us -> none  [the longest x1 23 us: body(): gathered = lax.all_gather(lengths, 'path', axis=1, tiled=True)]
    select_n x96 -> x0, other arithmetic: 34.6 us -> none  [the longest x32 12.1 us: incidence(): link_block = hop_links // LB]
    ppermute x0 -> x16, starting transfers between devices: none -> 25.5 us  [exchange(): return lax.ppermute(x, axis, [(i, i ^ bit) for i in range(n)])]
    reduce_scatter x1 -> x0, waiting for transfers between devices: 23 us -> none  [body(): lax.psum_scatter(load_full, 'path', scatter_dimension=1, tiled=True)]
    pallas_call x0 -> x5, Pallas kernels: none -> 21.8 us  [the longest x2 10.4 us: half_sweep(): pl.pallas_call(lambda *refs: half_kernel(far, n, *refs), in_specs=[SCALAR...]
  transfers between devices with their start and end apart: 1 -> 16, of which waited for: 1 -> 5; matrix products, arithmetic and copies ran while one was open for 0% -> 3% of each run, Pallas kernels for 0% -> 32%
where the time goes in v2:
time: 67.5 us; the launch traced here: 66.8 us
  starting transfers between devices  25.5 us (38%)
  Pallas kernels  21.8 us (32%)
  waiting for transfers between devices  15.2 us (23%)
  local copies, waits for them, and re-layouts  3.47 us (5%)
  between operations  0.83 us (1%)
    ppermute x16, starting transfers between devices, exchange(): return lax.ppermute(x, axis, [(i, i ^ bit) for i in range(n)])  25.5 us
    ppermute x16, waiting for transfers between devices, exchange(): return lax.ppermute(x, axis, [(i, i ^ bit) for i in range(n)])  15.2 us
    pallas_call x2, Pallas kernels, half_sweep(): pl.pallas_call(lambda *refs: half_kernel(far, n, *refs), in_specs=[SCALAR...  10.4 us
    pallas_call x1, Pallas kernels, build_incidence(): pl.pallas_call(incidence_kernel, in_specs=[pl.BlockSpec(memory_space=pltp...  8.49 us
    pallas_call x1, Pallas kernels, robust_costs(): pl.pallas_call(lambda *refs: robust_kernel(len(parts), *refs), in_specs=[...  2.7 us
    unnamed x12, local copies, waits for them, and re-layouts  1.64 us
  transfers between devices with their start and end apart: 16, of which 5 were waited for; matrix products, arithmetic and copies ran while one was open for 3% of the time, Pallas kernels for 32%

profile of v2, /device:TPU:0, one launch (start us, length us, event | category | flops | bytes accessed | tf_op | source)
XLA Modules:
  0.0 66.8 jit_solution(11623093771184833503)
XLA Ops:
  0.6 3.1 %collective-permute-start = (f32[64,896]{1,0:T(8,128)}, f32[64,896]{1,0:T(8,128)S(1)}, u32[]{:S(2)}, u32[]{:S(2)}) collective-permute-start(f32[64,896]{1,0:T(8,128)} %refs_0_.3), channel_id=1, source_target_pairs={{0,4},{4,0},{8,12},{12,8},{1,5},{5,1},{9,13},{13,9},{2,6},{6,2},{1... | collective-permute-start | bytes 688136 | tf_op jit(solution)/shard_map/ppermute | solution.py:380
  3.7 1.0 %constant_dynamic-slice_fusion = (f32[32,896]{1,0:T(8,128)S(1)}, f32[32,896]{1,0:T(8,128)S(1)}) fusion(f32[64,896]{1,0:T(8,128)} %refs_0_.3, s32[]{:T(128)S(6)} %select_n.25, s32[]{:T(128)S(6)} %select_n.24), kind=kLoop, calls=%fused_computation.5 | loop fusion | bytes 458760 | tf_op jit(solution)/shard_map/dynamic_slice | solution.py:391
  4.7 2.7 %collective-permute-start.3 = (f32[32,896]{1,0:T(8,128)S(1)}, f32[32,896]{1,0:T(8,128)S(1)}, u32[]{:S(2)}, u32[]{:S(2)}) collective-permute-start(f32[32,896]{1,0:T(8,128)S(1)} %get-tuple-element.37), channel_id=1, source_target_pairs={{0,8},{4,12},{8,0},{12,4},{1,9},{5,13},{9,1},{13,5},{2,10},{6,14},... | collective-permute-start | bytes 344072 | tf_op jit(solution)/shard_map/ppermute | solution.py:380
  7.4 0.7 %broadcast_in_dim.15 = f32[8,896]{1,0:T(8,128)S(1)} broadcast(f32[896]{0:T(1024)} %param.14), dimensions={1} | broadcast | bytes 32256 | tf_op jit(solution)/shard_map/broadcast_in_dim | solution.py:390
  8.1 2.0 %collective-permute-start.1 = (f32[40,896]{1,0:T(8,128)S(1)}, f32[40,896]{1,0:T(8,128)S(1)}, u32[]{:S(2)}, u32[]{:S(2)}) collective-permute-start(f32[40,896]{1,0:T(8,128)S(1)} %pad_maximum_fusion), channel_id=1, source_target_pairs={{0,8},{4,12},{8,0},{12,4},{1,9},{5,13},{9,1},{13,5},{2,10},{6,14},... | collective-permute-start | bytes 430088 | tf_op jit(solution)/shard_map/ppermute | solution.py:380
  10.0 2.0 %collective-permute-start.2 = (f32[40,896]{1,0:T(8,128)S(1)}, f32[40,896]{1,0:T(8,128)S(1)}, u32[]{:S(2)}, u32[]{:S(2)}) collective-permute-start(f32[40,896]{1,0:T(8,128)S(1)} %pad_maximum_fusion), channel_id=1, source_target_pairs={{0,12},{4,8},{8,4},{12,0},{1,13},{5,9},{9,5},{13,1},{2,14},{6,10},... | collective-permute-start | bytes 430088 | tf_op jit(solution)/shard_map/ppermute | solution.py:380
  12.0 8.5 %incidence.1 = (bf16[33024,128]{1,0:T(8,128)(2,1)S(1)}, bf16[33024,128]{1,0:T(8,128)(2,1)S(1)}, s32[4,144]{1,0:T(4,128)S(1)}, s32[1]{0:T(128)}, bf16[16,128,128]...) custom-call(s32[16,16]{1,0:T(8,128)} %refs_0_.2, s32[16]{0:T(128)} %refs_1_.1, s32[8,2048]{1,0:T(8,128)} %refs_2_.7, ...), custom_call_target="tpu_custom_call" | custom-call | flops 1000000000 | bytes 25000000 | tf_op jit(solution)/shard_map/incidence/pallas_call | solution.py:115
  20.6 0.9 %copy-done = f32[64,896]{1,0:T(8,128)S(1)} copy-done((f32[64,896]{1,0:T(8,128)S(1)}, f32[64,896]{1,0:T(8,128)}, u32[]{:S(2)}) %copy-start) | copy-done | bytes 229400
  21.5 4.8 %far_sweep.1 = (f32[32,2048]{1,0:T(8,128)S(1)}, f32[28,16,128]{2,1,0:T(8,128)S(1)}, f32[28,16,128]{2,1,0:T(8,128)S(1)}) custom-call(s32[4,144]{1,0:T(4,128)S(1)} %get-tuple-element.20.refs_0_, s32[1]{0:T(128)} %get-tuple-element.21.refs_1_, f32[64,896]{1,0:T(8,128)S(1)} %copy-done, f32[64,896]{1,0:T(8,128)S(1)} %collective-permute-done.refs_3_.refs_1_, ...), custom_call_target="tpu_custom_call" | custom-call | flops 1000000000 | bytes 25000000 | tf_op jit(solution)/shard_map/far_sweep/pallas_call | solution.py:237
  26.3 6.0 %collective-permute-start.7 = (f32[28,16,128]{2,1,0:T(8,128)S(1)}, f32[28,16,128]{2,1,0:T(8,128)S(1)}, u32[]{:S(2)}, u32[]{:S(2)}) collective-permute-start(f32[28,16,128]{2,1,0:T(8,128)S(1)} %get-tuple-element.31), channel_id=1, source_target_pairs={{0,4},{4,0},{8,12},{12,8},{1,5},{5,1},{9,13},{13,9},{2,6},{6,2},{1... | collective-permute-start | bytes 688136 | tf_op jit(solution)/shard_map/ppermute | solution.py:380
  32.3 5.6 %near_sweep.1 = (f32[64,2048]{1,0:T(8,128)}, f32[28,16,128]{2,1,0:T(8,128)S(1)}, f32[28,16,128]{2,1,0:T(8,128)S(1)}) custom-call(s32[4,144]{1,0:T(4,128)S(1)} %get-tuple-element.20.refs_0_, s32[1]{0:T(128)} %get-tuple-element.21.refs_1_, f32[64,896]{1,0:T(8,128)S(1)} %copy-done, f32[64,896]{1,0:T(8,128)S(1)} %collective-permute-done.refs_3_.refs_1_, ...), custom_call_target="tpu_custom_call" | custom-call | flops 1000000000 | bytes 25000000 | tf_op jit(solution)/shard_map/near_sweep/pallas_call | solution.py:237
  38.0 0.8 %collective-permute-start.6 = (f32[28,16,128]{2,1,0:T(8,128)S(1)}, f32[28,16,128]{2,1,0:T(8,128)S(1)}, u32[]{:S(2)}, u32[]{:S(2)}) collective-permute-start(f32[28,16,128]{2,1,0:T(8,128)S(1)} %get-tuple-element.29), channel_id=1, source_target_pairs={{0,4},{4,0},{8,12},{12,8},{1,5},{5,1},{9,13},{13,9},{2,6},{6,2},{1... | collective-permute-start | bytes 688136 | tf_op jit(solution)/shard_map/ppermute | solution.py:380
  38.8 0.9 %collective-permute-start.8 = (f32[28,16,128]{2,1,0:T(8,128)S(1)}, f32[28,16,128]{2,1,0:T(8,128)S(1)}, u32[]{:S(2)}, u32[]{:S(2)}) collective-permute-start(f32[28,16,128]{2,1,0:T(8,128)S(1)} %add.33), channel_id=1, source_target_pairs={{0,8},{4,12},{8,0},{12,4},{1,9},{5,13},{9,1},{13,5},{2,10},{6,14},... | collective-permute-start | bytes 688136 | tf_op jit(solution)/shard_map/ppermute | solution.py:380
  39.7 0.8 %collective-permute-start.5 = (f32[1,896]{1,0:T(1,128)S(1)}, f32[1,896]{1,0:T(1,128)S(1)}, u32[]{:S(2)}, u32[]{:S(2)}) collective-permute-start(f32[1,896]{1,0:T(1,128)S(1)} %broadcast_in_dim.17.refs_4_), channel_id=1, source_target_pairs={{0,4},{4,0},{8,12},{12,8},{1,5},{5,1},{9,13},{13,9},{2,6},{6,2},{1... | collective-permute-start | bytes 10760 | tf_op jit(solution)/shard_map/ppermute | solution.py:380
  40.6 6.0 %collective-permute-done.5.refs_5_ = f32[1,896]{1,0:T(1,128)S(1)} collective-permute-done((f32[1,896]{1,0:T(1,128)S(1)}, f32[1,896]{1,0:T(1,128)S(1)}, u32[]{:S(2)}, u32[]{:S(2)}) %collective-permute-start.5) | collective-permute-done | bytes 3616 | tf_op jit(solution)/shard_map/ppermute | solution.py:380
  46.5 2.3 %collective-permute-done.8.refs_11_ = f32[28,16,128]{2,1,0:T(8,128)S(1)} collective-permute-done((f32[28,16,128]{2,1,0:T(8,128)S(1)}, f32[28,16,128]{2,1,0:T(8,128)S(1)}, u32[]{:S(2)}, u32[]{:S(2)}) %collective-permute-start.8) | collective-permute-done | bytes 229408 | tf_op jit(solution)/shard_map/ppermute | solution.py:380
  49.2 1.2 %collective-permute-done.12 = f32[28,128]{1,0:T(8,128)S(1)} collective-permute-done((f32[28,128]{1,0:T(8,128)S(1)}, f32[28,128]{1,0:T(8,128)S(1)}, u32[]{:S(2)}, u32[]{:S(2)}) %collective-permute-start.12) | collective-permute-done | bytes 14368 | tf_op jit(solution)/shard_map/ppermute | solution.py:380
  50.4 1.5 %collective-permute-start.13 = (f32[28,128]{1,0:T(8,128)S(1)}, f32[28,128]{1,0:T(8,128)S(1)}, u32[]{:S(2)}, u32[]{:S(2)}) collective-permute-start(f32[28,128]{1,0:T(8,128)S(1)} %add.38), channel_id=1, source_target_pairs={{0,2},{2,0},{1,3},{3,1},{4,6},{6,4},{5,7},{7,5},{8,10},{10,8},{9,1... | collective-permute-start | bytes 43016 | tf_op jit(solution)/shard_map/ppermute | solution.py:380
  51.8 2.2 %collective-permute-done.13 = f32[28,128]{1,0:T(8,128)S(1)} collective-permute-done((f32[28,128]{1,0:T(8,128)S(1)}, f32[28,128]{1,0:T(8,128)S(1)}, u32[]{:S(2)}, u32[]{:S(2)}) %collective-permute-start.13) | collective-permute-done | bytes 14368 | tf_op jit(solution)/shard_map/ppermute | solution.py:380
  54.1 2.0 %collective-permute-start.9 = (f32[16,896]{1,0:T(8,128)S(1)}, f32[16,896]{1,0:T(8,128)S(1)}, u32[]{:S(2)}, u32[]{:S(2)}) collective-permute-start(f32[16,896]{1,0:T(8,128)S(1)} %get-tuple-element.33), channel_id=1, source_target_pairs={{0,4},{4,0},{8,12},{12,8},{1,5},{5,1},{9,13},{13,9},{2,6},{6,2},{1... | collective-permute-start | bytes 172040 | tf_op jit(solution)/shard_map/ppermute | solution.py:380
  56.5 2.1 %collective-permute-start.11 = (f32[16,896]{1,0:T(8,128)S(1)}, f32[16,896]{1,0:T(8,128)S(1)}, u32[]{:S(2)}, u32[]{:S(2)}) collective-permute-start(f32[16,896]{1,0:T(8,128)S(1)} %get-tuple-element.35), channel_id=1, source_target_pairs={{0,12},{4,8},{8,4},{12,0},{1,13},{5,9},{9,5},{13,1},{2,14},{6,10},... | collective-permute-start | bytes 172040 | tf_op jit(solution)/shard_map/ppermute | solution.py:380
  58.6 1.3 %collective-permute-start.15 = (f32[28,128]{1,0:T(8,128)S(1)}, f32[28,128]{1,0:T(8,128)S(1)}, u32[]{:S(2)}, u32[]{:S(2)}) collective-permute-start(f32[28,128]{1,0:T(8,128)S(1)} %add.40.refs_3_), channel_id=1, source_target_pairs={{0,8},{4,12},{8,0},{12,4},{1,9},{5,13},{9,1},{13,5},{2,10},{6,14},... | collective-permute-start | bytes 43016 | tf_op jit(solution)/shard_map/ppermute | solution.py:380
  60.0 3.4 %collective-permute-done.15.refs_4_ = f32[28,128]{1,0:T(8,128)S(1)} collective-permute-done((f32[28,128]{1,0:T(8,128)S(1)}, f32[28,128]{1,0:T(8,128)S(1)}, u32[]{:S(2)}, u32[]{:S(2)}) %collective-permute-start.15) | collective-permute-done | bytes 14368 | tf_op jit(solution)/shard_map/ppermute | solution.py:380
  63.4 2.7 %robust.1 = f32[16,128]{1,0:T(8,128)} custom-call(s32[4,144]{1,0:T(4,128)S(1)} %get-tuple-element.20.refs_0_, s32[1]{0:T(128)} %get-tuple-element.21.refs_1_, s32[8,2048]{1,0:T(8,128)S(1)} %copy-done.2, f32[28,128]{1,0:T(8,128)S(1)} %add.40.refs_3_, f32[28,128]{1,0:T(8,128)S(1)} %collective-permute-done.15.refs_4_), custom_call_target="tpu_custom_call" | custom-call | flops 100000000 | bytes 10000000 | tf_op jit(solution)/shard_map/robust/pallas_call | solution.py:366
  (39 shorter events, 1.6 us)
Async XLA Ops:
  0.6 19.9 %collective-permute-start = (f32[64,896]{1,0:T(8,128)}, f32[64,896]{1,0:T(8,128)S(1)}, u32[]{:S(2)}, u32[]{:S(2)}) collective-permute-start(f32[64,896]{1,0:T(8,128)} %refs_0_.3), channel_id=1, source_target_pairs={{0,4},{4,0},{8,12},{12,8},{1,5},{5,1},{9,13},{13,9},{2,6},{6,2},{1... | collective-permute-start | bytes 688136 | tf_op jit(solution)/shard_map/ppermute | solution.py:380
  4.7 15.8 %collective-permute-start.3 = (f32[32,896]{1,0:T(8,128)S(1)}, f32[32,896]{1,0:T(8,128)S(1)}, u32[]{:S(2)}, u32[]{:S(2)}) collective-permute-start(f32[32,896]{1,0:T(8,128)S(1)} %get-tuple-element.37), channel_id=1, source_target_pairs={{0,8},{4,12},{8,0},{12,4},{1,9},{5,13},{9,1},{13,5},{2,10},{6,14},... | collective-permute-start | bytes 344072 | tf_op jit(solution)/shard_map/ppermute | solution.py:380
  7.4 13.2 %collective-permute-start.4 = (f32[32,896]{1,0:T(8,128)S(1)}, f32[32,896]{1,0:T(8,128)S(1)}, u32[]{:S(2)}, u32[]{:S(2)}) collective-permute-start(f32[32,896]{1,0:T(8,128)S(1)} %get-tuple-element.37), channel_id=1, source_target_pairs={{0,12},{4,8},{8,4},{12,0},{1,13},{5,9},{9,5},{13,1},{2,14},{6,10},... | collective-permute-start | bytes 344072 | tf_op jit(solution)/shard_map/ppermute | solution.py:380
  8.1 24.2 %collective-permute-start.1 = (f32[40,896]{1,0:T(8,128)S(1)}, f32[40,896]{1,0:T(8,128)S(1)}, u32[]{:S(2)}, u32[]{:S(2)}) collective-permute-start(f32[40,896]{1,0:T(8,128)S(1)} %pad_maximum_fusion), channel_id=1, source_target_pairs={{0,8},{4,12},{8,0},{12,4},{1,9},{5,13},{9,1},{13,5},{2,10},{6,14},... | collective-permute-start | bytes 430088 | tf_op jit(solution)/shard_map/ppermute | solution.py:380
  10.0 22.3 %collective-permute-start.2 = (f32[40,896]{1,0:T(8,128)S(1)}, f32[40,896]{1,0:T(8,128)S(1)}, u32[]{:S(2)}, u32[]{:S(2)}) collective-permute-start(f32[40,896]{1,0:T(8,128)S(1)} %pad_maximum_fusion), channel_id=1, source_target_pairs={{0,12},{4,8},{8,4},{12,0},{1,13},{5,9},{9,5},{13,1},{2,14},{6,10},... | collective-permute-start | bytes 430088 | tf_op jit(solution)/shard_map/ppermute | solution.py:380
  20.6 0.9 %copy-start = (f32[64,896]{1,0:T(8,128)S(1)}, f32[64,896]{1,0:T(8,128)}, u32[]{:S(2)}) copy-start(f32[64,896]{1,0:T(8,128)} %refs_0_.3) | copy-start | bytes 688132
  26.3 12.5 %collective-permute-start.7 = (f32[28,16,128]{2,1,0:T(8,128)S(1)}, f32[28,16,128]{2,1,0:T(8,128)S(1)}, u32[]{:S(2)}, u32[]{:S(2)}) collective-permute-start(f32[28,16,128]{2,1,0:T(8,128)S(1)} %get-tuple-element.31), channel_id=1, source_target_pairs={{0,4},{4,0},{8,12},{12,8},{1,5},{5,1},{9,13},{13,9},{2,6},{6,2},{1... | collective-permute-start | bytes 688136 | tf_op jit(solution)/shard_map/ppermute | solution.py:380
  32.3 7.4 %copy-start.4 = (f32[896]{0:T(1024)S(1)}, f32[896]{0:T(1024)}, u32[]{:S(2)}) copy-start(f32[896]{0:T(1024)} %param.14) | copy-start | bytes 10756
  32.3 8.2 %copy-start.5 = (f32[64]{0:T(128)S(1)}, f32[64]{0:T(128)}, u32[]{:S(2)}) copy-start(f32[64]{0:T(128)} %param.15) | copy-start | bytes 772
  32.3 16.6 %copy-start.1 = (f32[64,896]{1,0:T(8,128)S(1)}, f32[64,896]{1,0:T(8,128)}, u32[]{:S(2)}) copy-start(f32[64,896]{1,0:T(8,128)} %refs_0_.3) | copy-start | bytes 688132
  32.3 31.0 %copy-start.2 = (s32[8,2048]{1,0:T(8,128)S(1)}, s32[8,2048]{1,0:T(8,128)}, u32[]{:S(2)}) copy-start(s32[8,2048]{1,0:T(8,128)} %refs_2_.7) | copy-start | bytes 196612
  38.0 8.6 %collective-permute-start.6 = (f32[28,16,128]{2,1,0:T(8,128)S(1)}, f32[28,16,128]{2,1,0:T(8,128)S(1)}, u32[]{:S(2)}, u32[]{:S(2)}) collective-permute-start(f32[28,16,128]{2,1,0:T(8,128)S(1)} %get-tuple-element.29), channel_id=1, source_target_pairs={{0,4},{4,0},{8,12},{12,8},{1,5},{5,1},{9,13},{13,9},{2,6},{6,2},{1... | collective-permute-start | bytes 688136 | tf_op jit(solution)/shard_map/ppermute | solution.py:380
  38.8 10.1 %collective-permute-start.8 = (f32[28,16,128]{2,1,0:T(8,128)S(1)}, f32[28,16,128]{2,1,0:T(8,128)S(1)}, u32[]{:S(2)}, u32[]{:S(2)}) collective-permute-start(f32[28,16,128]{2,1,0:T(8,128)S(1)} %add.33), channel_id=1, source_target_pairs={{0,8},{4,12},{8,0},{12,4},{1,9},{5,13},{9,1},{13,5},{2,10},{6,14},... | collective-permute-start | bytes 688136 | tf_op jit(solution)/shard_map/ppermute | solution.py:380
  39.7 6.8 %collective-permute-start.5 = (f32[1,896]{1,0:T(1,128)S(1)}, f32[1,896]{1,0:T(1,128)S(1)}, u32[]{:S(2)}, u32[]{:S(2)}) collective-permute-start(f32[1,896]{1,0:T(1,128)S(1)} %broadcast_in_dim.17.refs_4_), channel_id=1, source_target_pairs={{0,4},{4,0},{8,12},{12,8},{1,5},{5,1},{9,13},{13,9},{2,6},{6,2},{1... | collective-permute-start | bytes 10760 | tf_op jit(solution)/shard_map/ppermute | solution.py:380
  49.1 1.2 %collective-permute-start.12 = (f32[28,128]{1,0:T(8,128)S(1)}, f32[28,128]{1,0:T(8,128)S(1)}, u32[]{:S(2)}, u32[]{:S(2)}) collective-permute-start(f32[28,128]{1,0:T(8,128)S(1)} %get-tuple-element.36), channel_id=1, source_target_pairs={{0,1},{1,0},{2,3},{3,2},{4,5},{5,4},{6,7},{7,6},{8,9},{9,8},{10,11... | collective-permute-start | bytes 43016 | tf_op jit(solution)/shard_map/ppermute | solution.py:380
  50.4 3.7 %collective-permute-start.13 = (f32[28,128]{1,0:T(8,128)S(1)}, f32[28,128]{1,0:T(8,128)S(1)}, u32[]{:S(2)}, u32[]{:S(2)}) collective-permute-start(f32[28,128]{1,0:T(8,128)S(1)} %add.38), channel_id=1, source_target_pairs={{0,2},{2,0},{1,3},{3,1},{4,6},{6,4},{5,7},{7,5},{8,10},{10,8},{9,1... | collective-permute-start | bytes 43016 | tf_op jit(solution)/shard_map/ppermute | solution.py:380
  54.1 4.5 %collective-permute-start.14 = (f32[28,128]{1,0:T(8,128)S(1)}, f32[28,128]{1,0:T(8,128)S(1)}, u32[]{:S(2)}, u32[]{:S(2)}) collective-permute-start(f32[28,128]{1,0:T(8,128)S(1)} %add.39), channel_id=1, source_target_pairs={{0,4},{4,0},{8,12},{12,8},{1,5},{5,1},{9,13},{13,9},{2,6},{6,2},{1... | collective-permute-start | bytes 43016 | tf_op jit(solution)/shard_map/ppermute | solution.py:380
  54.1 12.0 %collective-permute-start.9 = (f32[16,896]{1,0:T(8,128)S(1)}, f32[16,896]{1,0:T(8,128)S(1)}, u32[]{:S(2)}, u32[]{:S(2)}) collective-permute-start(f32[16,896]{1,0:T(8,128)S(1)} %get-tuple-element.33), channel_id=1, source_target_pairs={{0,4},{4,0},{8,12},{12,8},{1,5},{5,1},{9,13},{13,9},{2,6},{6,2},{1... | collective-permute-start | bytes 172040 | tf_op jit(solution)/shard_map/ppermute | solution.py:380
  56.1 10.0 %collective-permute-start.10 = (f32[16,896]{1,0:T(8,128)S(1)}, f32[16,896]{1,0:T(8,128)S(1)}, u32[]{:S(2)}, u32[]{:S(2)}) collective-permute-start(f32[16,896]{1,0:T(8,128)S(1)} %get-tuple-element.34), channel_id=1, source_target_pairs={{0,8},{4,12},{8,0},{12,4},{1,9},{5,13},{9,1},{13,5},{2,10},{6,14},... | collective-permute-start | bytes 172040 | tf_op jit(solution)/shard_map/ppermute | solution.py:380
  56.5 9.6 %collective-permute-start.11 = (f32[16,896]{1,0:T(8,128)S(1)}, f32[16,896]{1,0:T(8,128)S(1)}, u32[]{:S(2)}, u32[]{:S(2)}) collective-permute-start(f32[16,896]{1,0:T(8,128)S(1)} %get-tuple-element.35), channel_id=1, source_target_pairs={{0,12},{4,8},{8,4},{12,0},{1,13},{5,9},{9,5},{13,1},{2,14},{6,10},... | collective-permute-start | bytes 172040 | tf_op jit(solution)/shard_map/ppermute | solution.py:380
  58.6 4.8 %collective-permute-start.15 = (f32[28,128]{1,0:T(8,128)S(1)}, f32[28,128]{1,0:T(8,128)S(1)}, u32[]{:S(2)}, u32[]{:S(2)}) collective-permute-start(f32[28,128]{1,0:T(8,128)S(1)} %add.40.refs_3_), channel_id=1, source_target_pairs={{0,8},{4,12},{8,0},{12,4},{1,9},{5,13},{9,1},{13,5},{2,10},{6,14},... | collective-permute-start | bytes 43016 | tf_op jit(solution)/shard_map/ppermute | solution.py:380
  66.2 0.7 %copy-start.3 = (f32[64,896]{1,0:T(8,128)}, f32[64,896]{1,0:T(8,128)S(1)}, u32[]{:S(2)}) copy-start(f32[64,896]{1,0:T(8,128)S(1)} %constant_dynamic-update-slice_fusion) | copy-start | bytes 688132

commit v3 on v2

v3 whole, which is shorter than its diff:
```python
import jax
import jax.numpy as jnp
from jax import lax
from jax.experimental import pallas as pl
from jax.experimental.pallas import tpu as pltpu
from jax.sharding import PartitionSpec as P

PATHS_PER_BLOCK = 128
LB = 128
MAXT = 16
COMMODITY_BLOCK = 32
S = 256

SOFTMIN_RATE = 0.25
STEP_RATE = 1.0
DEMAND_UNIT = 0.0625
MIB = 1024 * 1024

F32 = jnp.float32
BF16 = jnp.bfloat16
PACK = 16
BATCH = 16
GROUP = LB // COMMODITY_BLOCK

SCALARS = pl.BlockSpec(memory_space=pltpu.SMEM)
ARRAY = pl.BlockSpec(memory_space=pltpu.VMEM)
LISTS = 3
TOGETHER = 8
UNROLL = 7
LB_BITS = 7
COUNTED = 8


def split(x):
    high = x.astype(BF16)
    return high, (x - high.astype(F32)).astype(BF16)


def stacked(x):
    return jnp.concatenate(split(x), axis=0)


def aligned(start, size, unit):
    return pl.ds(pl.multiple_of(start * unit, unit), size)


def stay(*arrays):
    return tuple(pltpu.with_memory_space_constraint(a, pltpu.HBM) for a in arrays)


REMAIN = pl.BlockSpec(memory_space=pltpu.HBM)


def fetch(given, local, arrived):
    copies = [pltpu.make_async_copy(a, b, arrived.at[i]) for i, (a, b) in enumerate(zip(given, local))]
    for copy in copies:
        copy.start()
    return copies


def listing_kernel(tile_total, *refs):
    given, (list_ref, total_ref, same_ref, wanted_ref) = refs[:4], refs[4:8]
    local, arrived = refs[8:12], refs[12]
    tiles_ref, count_ref, comm_ref, demand_ref = local
    copies = fetch(given, local, arrived)
    blocks = tiles_ref.shape[0]
    spare = blocks * MAXT
    for copy in copies:
        copy.wait()

    def one_block(block, entry):
        live = count_ref[block]

        def one_pair(pair, entry):
            list_ref[0, entry] = block * MAXT + 2 * pair
            list_ref[1, entry] = tiles_ref[block, 2 * pair]
            list_ref[2, entry] = jnp.where(2 * pair + 1 < live, tiles_ref[block, 2 * pair + 1], tile_total)
            return entry + 1

        return lax.fori_loop(0, (live + 1) // 2, one_pair, entry)

    entries = lax.fori_loop(0, blocks, one_block, 0)
    batches = (entries + BATCH - 1) // BATCH
    total_ref[0] = batches
    total_ref[1] = (entries + COUNTED - 1) // COUNTED

    def pad(entry, carry):
        list_ref[0, entry] = spare
        list_ref[1, entry] = tile_total
        list_ref[2, entry] = tile_total
        return carry

    lax.fori_loop(entries, batches * BATCH, pad, 0)

    commodity_rows = lax.broadcasted_iota(jnp.int32, (LB, PATHS_PER_BLOCK), 0)
    for block in range(blocks):
        group, j = block // GROUP, block % GROUP
        demand = demand_ref[:, group * LB : (group + 1) * LB].astype(F32).astype(BF16)
        onehot = (commodity_rows == comm_ref[block : block + 1, :] + COMMODITY_BLOCK * j).astype(F32).astype(BF16)
        same = lax.dot_general(onehot, onehot, (((0,), (0,)), ((), ())), preferred_element_type=F32)
        same_ref[block] = same.astype(BF16)
        wanted_ref[block] = jnp.dot(demand, onehot, preferred_element_type=F32) * DEMAND_UNIT


def build_listing(tile_total, block_tiles, block_count, path_commodity, demand):
    blocks = block_tiles.shape[0]
    given = stay(block_tiles, block_count, path_commodity, demand)
    return pl.pallas_call(
        lambda *refs: listing_kernel(tile_total, *refs),
        in_specs=[REMAIN] * 4,
        out_specs=[SCALARS, SCALARS, ARRAY, ARRAY],
        out_shape=[
            jax.ShapeDtypeStruct((LISTS, blocks * MAXT // 2 + BATCH), jnp.int32),
            jax.ShapeDtypeStruct((2,), jnp.int32),
            jax.ShapeDtypeStruct((blocks, PATHS_PER_BLOCK, PATHS_PER_BLOCK), BF16),
            jax.ShapeDtypeStruct((blocks, demand.shape[0], PATHS_PER_BLOCK), F32),
        ],
        scratch_shapes=[pltpu.SMEM(a.shape, a.dtype) for a in given[:2]]
        + [pltpu.VMEM(a.shape, a.dtype) for a in given[2:]]
        + [pltpu.SemaphoreType.DMA((4,))],
        compiler_params=pltpu.CompilerParams(vmem_limit_bytes=8 * MIB),
        cost_estimate=pl.CostEstimate(flops=10**9, bytes_accessed=10**7, transcendentals=0),
        name="listing",
    )(*given)


def incidence_kernel(list_ref, total_ref, given_ref, hits_ref, turned_ref, links_ref, arrived):
    copies = fetch([given_ref], [links_ref], arrived)
    blocks = links_ref.shape[1] // PATHS_PER_BLOCK
    for ref in (hits_ref, turned_ref):
        ref[-2 * LB :, :] = jnp.zeros((2 * LB, LB), BF16)
    lanes = [(lax.broadcasted_iota(jnp.int32, (PACK, LB), 0) + PACK * g).astype(F32).astype(BF16) for g in range(LB // PACK)]
    one, zero = jnp.ones((PACK, PATHS_PER_BLOCK), BF16), jnp.zeros((PACK, PATHS_PER_BLOCK), BF16)
    copies[0].wait()

    def count_step(step, carry):
        done = []
        for j in range(COUNTED):
            entry = step * COUNTED + j
            slot = list_ref[0, entry]
            block = jnp.minimum(slot // MAXT, blocks - 1)
            links = links_ref[:, aligned(block, PATHS_PER_BLOCK, PATHS_PER_BLOCK)]
            for side in range(2):
                place = (links - list_ref[1 + side, entry] * LB).astype(F32)
                counts = None
                for h in range(links.shape[0]):
                    row = jnp.broadcast_to(place[h : h + 1, :], (PACK, PATHS_PER_BLOCK)).astype(BF16)
                    hit = [jnp.where(row == lane, one, zero) for lane in lanes]
                    counts = hit if counts is None else [a + b for a, b in zip(counts, hit)]
                done.append((aligned(slot + side, LB, LB), jnp.concatenate(counts, axis=0)))
        for where, table in done:
            hits_ref[where, :] = table
            turned_ref[where, :] = table.T
        return carry

    lax.fori_loop(0, total_ref[1], count_step, 0)


def build_incidence(path_links, pairs, total):
    blocks = path_links.shape[1] // PATHS_PER_BLOCK
    slots = blocks * MAXT + 2
    return pl.pallas_call(
        incidence_kernel,
        in_specs=[SCALARS, SCALARS, REMAIN],
        out_specs=[ARRAY, ARRAY],
        out_shape=[
            jax.ShapeDtypeStruct((slots * LB, PATHS_PER_BLOCK), BF16),
            jax.ShapeDtypeStruct((slots * PATHS_PER_BLOCK, LB), BF16),
        ],
        scratch_shapes=[pltpu.VMEM(path_links.shape, path_links.dtype), pltpu.SemaphoreType.DMA((1,))],
        compiler_params=pltpu.CompilerParams(vmem_limit_bytes=8 * MIB),
        cost_estimate=pl.CostEstimate(flops=10**6, bytes_accessed=20 * 10**6, transcendentals=0),
        name="incidence",
    )(pairs, total, *stay(path_links))


def sweep(list_ref, total_ref, hits_ref, turned_ref, same_ref, wanted_at, put_flow, split_ref, cost_ref, flow_ref, load_ref):
    blocks, rows2 = same_ref.shape[0], cost_ref.shape[1]
    rows = rows2 // 2
    flow_ref[blocks] = jnp.zeros(flow_ref.shape[1:], BF16)
    split_ref[split_ref.shape[0] - 1] = jnp.zeros(split_ref.shape[1:], BF16)
    load_ref[...] = jnp.zeros_like(load_ref)
    cost_ref[...] = jnp.zeros_like(cost_ref)
    batches = total_ref[0]

    def cost_batch(batch, carry):
        done = []
        for j in range(BATCH):
            slot, left, right = (list_ref[i, batch * BATCH + j] for i in range(LISTS))
            block = slot // MAXT
            chosen = jnp.concatenate([split_ref[left], split_ref[right]], axis=1)
            done.append((block, jnp.dot(chosen, hits_ref[aligned(slot, 2 * LB, LB), :], preferred_element_type=F32)))
        for block, cost in done:
            cost_ref[block] += cost
        return carry

    lax.fori_loop(0, batches, cost_batch, 0)

    for block in range(blocks):
        weight = jnp.exp(-SOFTMIN_RATE * (cost_ref[block, :rows] + cost_ref[block, rows:]))
        total = jnp.dot(stacked(weight), same_ref[block], preferred_element_type=F32)
        flow = wanted_at(block) * weight / (total[:rows] + total[rows:])
        put_flow(block, flow)
        flow_ref[block] = stacked(flow)

    def load_batch(batch, carry):
        done = []
        for j in range(BATCH):
            slot, left, right = (list_ref[i, batch * BATCH + j] for i in range(LISTS))
            block = slot // MAXT
            for side, tile in enumerate((left, right)):
                turned = turned_ref[aligned(slot + side, LB, LB), :]
                done.append((tile, jnp.dot(flow_ref[block], turned, preferred_element_type=F32)))
        for tile, load in done:
            load_ref[tile] += load
        return carry

    lax.fori_loop(0, batches, load_batch, 0)


def spread(split_ref, first, shard):
    for k in range(shard.shape[-1] // LB):
        split_ref[first + k] = stacked(shard[:, k * LB : (k + 1) * LB])


def path_columns(block):
    return slice(block * PATHS_PER_BLOCK, (block + 1) * PATHS_PER_BLOCK)


def sweep_scratch(rows, tiles, blocks):
    return [
        pltpu.VMEM((tiles + 1, 2 * rows, LB), BF16),
        pltpu.VMEM((blocks + 1, 2 * rows, PATHS_PER_BLOCK), F32),
        pltpu.VMEM((blocks + 1, 2 * rows, PATHS_PER_BLOCK), BF16),
        pltpu.VMEM((tiles + 1, 2 * rows, LB), F32),
    ]


def sweep_cost(size):
    return pl.CostEstimate(flops=10**10, bytes_accessed=size, transcendentals=0)


def half_kernel(far, n, list_ref, total_ref, *refs):
    pieces, (hits_ref, turned_ref, same_ref, wanted_ref) = refs[:n], refs[n : n + 4]
    flows_ref, mine_ref, other_ref, *scratch = refs[-7:]
    z = lax.axis_index("path")
    rows = scratch[0].shape[1] // 2
    side = lax.div(z, 2)
    side = 1 - side if far else side
    shard_tiles = pieces[0].shape[1] // LB
    for m, piece in enumerate(pieces):
        start = side if piece.shape[0] == 2 * rows else 0
        spread(scratch[0], (z ^ m) * shard_tiles, piece[aligned(start, rows, rows), :])

    def wanted_at(block):
        return wanted_ref[block, aligned(side, rows, rows), :]

    def put_flow(block, flow):
        flows_ref[:, path_columns(block)] = flow

    sweep(list_ref, total_ref, hits_ref, turned_ref, same_ref, wanted_at, put_flow, *scratch)
    load_ref = scratch[3]
    height = rows // 2
    for out_ref, place in ((mine_ref, lax.rem(z, 2)), (other_ref, 1 - lax.rem(z, 2))):
        for k in range(load_ref.shape[0] - 1):
            high = load_ref[k, aligned(place, height, height), :]
            out_ref[k] = high + load_ref[k, pl.ds(pl.multiple_of(rows + place * height, height), height), :]


def half_sweep(pieces, rows, built, far):
    hits, turned, pairs, total, same, wanted = built
    own = pieces[0].shape[1]
    n = len(pieces)
    blocks = wanted.shape[0]
    tiles = n * own // LB
    return pl.pallas_call(
        lambda *refs: half_kernel(far, n, *refs),
        in_specs=[SCALARS, SCALARS] + [ARRAY] * (n + 4),
        out_specs=[ARRAY] * 3,
        out_shape=[jax.ShapeDtypeStruct((rows, blocks * PATHS_PER_BLOCK), F32)]
        + [jax.ShapeDtypeStruct((tiles, rows // 2, LB), F32)] * 2,
        scratch_shapes=sweep_scratch(rows, tiles, blocks),
        compiler_params=pltpu.CompilerParams(vmem_limit_bytes=16 * MIB),
        cost_estimate=sweep_cost(25 * 10**6),
        name="far_sweep" if far else "near_sweep",
    )(pairs, total, *pieces, hits, turned, same, wanted)


def wide_kernel(list_ref, total_ref, lengths_ref, hits_ref, turned_ref, same_ref, wanted_ref, flows_ref, out_ref, *scratch):
    shards, _, own = lengths_ref.shape
    rows = lengths_ref.shape[1]

    def one_shard(i, carry):
        spread(scratch[0], i * (own // LB), lengths_ref[i])
        return carry

    lax.fori_loop(0, shards, one_shard, 0)

    def put_flow(block, flow):
        flows_ref[:, path_columns(block)] = flow

    sweep(
        list_ref, total_ref, hits_ref, turned_ref, same_ref, lambda block: wanted_ref[block], put_flow, *scratch
    )
    out_ref[...] = scratch[3][:-1, :rows, :] + scratch[3][:-1, rows:, :]


def wide_sweep(lengths, built):
    hits, turned, pairs, total, same, wanted = built
    shards, rows, own = lengths.shape
    blocks = wanted.shape[0]
    tiles = shards * own // LB
    return pl.pallas_call(
        wide_kernel,
        in_specs=[SCALARS, SCALARS] + [ARRAY] * 5,
        out_specs=[ARRAY] * 2,
        out_shape=[
            jax.ShapeDtypeStruct((rows, blocks * PATHS_PER_BLOCK), F32),
            jax.ShapeDtypeStruct((tiles, rows, LB), F32),
        ],
        scratch_shapes=sweep_scratch(rows, tiles, blocks),
        compiler_params=pltpu.CompilerParams(vmem_limit_bytes=48 * MIB),
        cost_estimate=sweep_cost(10**7),
        name="wide_sweep",
    )(pairs, total, lengths, hits, turned, same, wanted)


def growth_kernel(n, parts, *refs):
    lengths, capacities, weight_ref = refs[:n], refs[n : 2 * n], refs[2 * n]
    loads = refs[2 * n + 1 : 2 * n + 1 + parts]
    next_refs, mixed_ref, grown_ref = refs[-n - 2 : -2], refs[-2], refs[-1]
    z = lax.axis_index("path")
    links_total, height, _ = grown_ref.shape
    shard_tiles = links_total // n
    total = jnp.zeros((height, LB), F32)
    for m in range(n):
        row = aligned(z if lengths[m].shape[0] == n * height else lax.rem(z, 2), height, height)
        first = (z ^ m) * shard_tiles
        for k in range(shard_tiles):
            columns = slice(k * LB, (k + 1) * LB)
            load = loads[0][first + k]
            for ref in loads[1:]:
                load = load + ref[first + k]
            grown = lengths[m][row, columns] * jnp.exp(STEP_RATE * load / capacities[m][:, columns])
            grown_ref[m * shard_tiles + k] = grown
            total = total + grown
    factor = (links_total * LB) / jnp.sum(total, axis=1, keepdims=True)
    weight = weight_ref[aligned(z, height, height), :]
    for m in range(n):
        first = (z ^ m) * shard_tiles
        for k in range(shard_tiles):
            new = grown_ref[m * shard_tiles + k] * factor
            next_refs[m][:, k * LB : (k + 1) * LB] = new
            mixed_ref[pl.ds(first + k, 1), :] = jnp.sum(weight * new, axis=0, keepdims=True)


def grow(loads, lengths, capacities, weights):
    n, parts = len(lengths), len(loads)
    tiles, height, _ = loads[0].shape
    return pl.pallas_call(
        lambda *refs: growth_kernel(n, parts, *refs),
        in_specs=[ARRAY] * (2 * n + 1 + parts),
        out_specs=[ARRAY] * (n + 1),
        out_shape=[jax.ShapeDtypeStruct((height, tiles * LB // n), F32)] * n + [jax.ShapeDtypeStruct((tiles, LB), F32)],
        scratch_shapes=[pltpu.VMEM((tiles, height, LB), F32)],
        compiler_params=pltpu.CompilerParams(vmem_limit_bytes=8 * MIB),
        cost_estimate=pl.CostEstimate(flops=10**6, bytes_accessed=5 * 10**6, transcendentals=10**5),
        name="growth",
    )(*lengths, *capacities, weights, *loads)


def robust_kernel(parts, links_ref, *refs):
    part_refs, (out_ref, mixed_ref) = refs[:parts], refs[parts:]
    blocks = out_ref.shape[0]
    hops = links_ref.shape[0]
    mixed = part_refs[0][...]
    for ref in part_refs[1:]:
        mixed = mixed + ref[...]
    mixed_ref[...] = mixed
    for first in range(0, blocks, TOGETHER):
        group = range(first, min(first + TOGETHER, blocks))
        links = [links_ref[:, path_columns(block)] for block in group]

        def one_tile(tile, costs):
            table = jnp.broadcast_to(mixed_ref[pl.ds(tile, 1), :], (hops, LB))
            found = [jnp.take_along_axis(table, x & (LB - 1), axis=1) for x in links]
            return [jnp.where((x >> LB_BITS) == tile, f, c) for x, f, c in zip(links, found, costs)]

        tiles = mixed_ref.shape[0]
        costs = [jnp.zeros((hops, PATHS_PER_BLOCK), F32)] * len(links)
        step = UNROLL if tiles % UNROLL == 0 else 1

        def some_tiles(i, costs):
            for j in range(step):
                costs = one_tile(i * step + j, costs)
            return costs

        costs = lax.fori_loop(0, tiles // step, some_tiles, costs)
        for block, cost in zip(group, costs):
            out_ref[block : block + 1, :] = jnp.sum(cost, axis=0, keepdims=True) / S


def robust_costs(path_links, parts):
    hops, paths = path_links.shape
    blocks = paths // PATHS_PER_BLOCK
    out = pl.pallas_call(
        lambda *refs: robust_kernel(len(parts), *refs),
        in_specs=[ARRAY] * (len(parts) + 1),
        out_specs=ARRAY,
        out_shape=jax.ShapeDtypeStruct((blocks, PATHS_PER_BLOCK), F32),
        scratch_shapes=[pltpu.VMEM(parts[0].shape, F32)],
        compiler_params=pltpu.CompilerParams(vmem_limit_bytes=8 * MIB),
        cost_estimate=pl.CostEstimate(flops=10**6, bytes_accessed=10**6, transcendentals=0),
        name="robust",
    )(path_links, *parts)
    return out.reshape(-1)


def exchange(x, axis, n, bit):
    return lax.ppermute(x, axis, [(i, i ^ bit) for i in range(n)])


def body_paired(sizes, path_links, block_tiles, block_count, path_commodity, demand, lengths, capacity, scenario_weight):
    n = sizes["path"]
    rows, own = lengths.shape
    half, height = rows // 2, rows // n
    z = lax.axis_index("path").astype(jnp.int32)
    side = z // 2
    far = lax.dynamic_slice(lengths, ((1 - side) * half, 0), (half, own))
    near = lax.dynamic_slice(lengths, (side * half, 0), (half, own))

    def swap(x, m):
        return exchange(x, "path", n, m)

    shared = swap(lengths, 1)
    far_pieces = [far, shared, swap(near, 2), swap(near, 3)]
    pairs, total, same, wanted = build_listing(n * own // LB, block_tiles, block_count, path_commodity, demand)
    late, same = lax.optimization_barrier((far, same))
    near_pieces = [near, shared, swap(late, 2), swap(late, 3)]
    built = (*build_incidence(path_links, pairs, total), pairs, total, same, wanted)
    far_flows, straight, crossed = half_sweep(far_pieces, half, built, True)
    partial = straight + swap(crossed, 1)
    near_flows, mine, other = half_sweep(near_pieces, half, built, False)
    partial, other = lax.optimization_barrier((partial, other))
    loads = [mine, swap(other, 1), swap(partial, 2)]
    capacity_row = capacity[None, :]
    capacities = [capacity_row] + [swap(capacity_row, m) for m in range(1, n)]
    *new, mixed = grow(loads, near_pieces, capacities, scenario_weight[:, None])
    mixed = mixed + exchange(mixed, "sub", 2, 1)
    mixed = mixed + exchange(mixed, "scen", 2, 1)
    mixed = mixed + swap(mixed, 1)
    parts = [mixed, swap(mixed, 2)]
    arrived = [new[0]] + [swap(new[m], m) for m in range(1, n)]
    robust = robust_costs(path_links, parts)
    lengths_next = jnp.zeros((rows, own), F32)
    for m in range(n):
        lengths_next = lax.dynamic_update_slice(lengths_next, arrived[m], ((z ^ m) * height, 0))
    first, second = jnp.where(side == 0, near_flows, far_flows), jnp.where(side == 0, far_flows, near_flows)
    return jnp.concatenate([first, second], axis=0), lengths_next, robust


def body_wide(sizes, path_links, block_tiles, block_count, path_commodity, demand, lengths, capacity, scenario_weight):
    gathered = lax.all_gather(lengths, "path", axis=0, tiled=False)
    pairs, total, same, wanted = build_listing(gathered.shape[0] * gathered.shape[2] // LB, block_tiles, block_count, path_commodity, demand)
    built = (*build_incidence(path_links, pairs, total), pairs, total, same, wanted)
    flows, loads = wide_sweep(gathered, built)
    loads = loads.transpose(1, 0, 2).reshape(lengths.shape[0], -1)
    own_loads = lax.psum_scatter(loads, "path", scatter_dimension=1, tiled=True)
    grown = lengths * jnp.exp(STEP_RATE * own_loads / capacity[None, :])
    totals = lax.psum(jnp.sum(grown, axis=1), "path")
    lengths_next = grown * (loads.shape[1] / totals)[:, None]
    mixed = lax.psum(jnp.sum(lengths_next * scenario_weight[:, None], axis=0), ("scen", "sub"))
    mixed = lax.all_gather(mixed.reshape(-1, LB), "path", axis=0, tiled=True)
    return flows, lengths_next, robust_costs(path_links, [mixed])


def solution(mesh):
    sizes = dict(mesh.shape)

    def body(*args):
        paired = sizes["path"] == 4 and sizes["scen"] == 2 and sizes["sub"] == 2 and args[5].shape[0] % 64 == 0
        return (body_paired if paired else body_wide)(sizes, *args)

    return jax.shard_map(
        body,
        mesh=mesh,
        in_specs=(
            P(None, ("grp", "path")),
            P(("grp", "path"), None),
            P(("grp", "path")),
            P(("grp", "path"), None),
            P(("scen", "sub"), ("grp", "path")),
            P(("scen", "sub"), ("grp", "path")),
            P(("grp", "path")),
            P(("grp", "scen", "sub")),
        ),
        out_specs=(
            P(("scen", "sub"), ("grp", "path")),
            P(("scen", "sub"), ("grp", "path")),
            P(("grp", "path")),
        ),
        check_vma=False,
    )
```

time: 67.5 us -> 65.6 us (0.972)
  starting transfers between devices: 25.5 us -> 32.8 us
  waiting for transfers between devices: 15.2 us -> 9.73 us
  Pallas kernels: 21.8 us -> 18.7 us
  local copies, waits for them, and re-layouts: 3.47 us -> 1.85 us
  other arithmetic: 0.05 us -> 0.91 us
    ppermute x16 -> x18, starting transfers between devices: 25.5 us -> 32.8 us  [exchange(): return lax.ppermute(x, axis, [(i, i ^ bit) for i in range(n)])]
    ppermute x16 -> x18, waiting for transfers between devices: 15.2 us -> 9.73 us  [exchange(): return lax.ppermute(x, axis, [(i, i ^ bit) for i in range(n)])]
    pallas_call x2, Pallas kernels: 10.4 us -> 8.18 us  [half_sweep(): pl.pallas_call(lambda *refs: half_kernel(far, n, *refs), in_specs=[SCALAR...]
    unnamed x12 -> x8, local copies, waits for them, and re-layouts: 1.64 us -> 0.7 us
    concatenate x1, other arithmetic: 0.01 us -> 0.83 us  [body_paired(): return (jnp.concatenate([first, second], axis=0), lengths_next, robust)]
    broadcast_in_dim x2 -> x1, local copies, waits for them, and re-layouts: 0.69 us -> 0.01 us  [body_paired(): capacity_row = capacity[None, :]]
    pallas_call x1 -> x2, Pallas kernels: 8.49 us -> 7.91 us  [the longest x1 5.4 us: build_incidence(): pl.pallas_call(incidence_kernel, in_specs=[SCALARS, SCALARS, REMAIN], out...]
  transfers between devices with their start and end apart: 16 -> 18, of which waited for: 5 -> 4; matrix products, arithmetic and copies ran while one was open for 3% -> 3% of each run, Pallas kernels for 32% -> 29%
where the time goes in v3:
time: 65.6 us; the launch traced here: 64.8 us
  starting transfers between devices  32.8 us (50%)
  Pallas kernels  18.7 us (29%)
  waiting for transfers between devices  9.73 us (15%)
  local copies, waits for them, and re-layouts  1.85 us (3%)
  other arithmetic  0.91 us (1%)
  between operations  0.85 us (1%)
    ppermute x18, starting transfers between devices, exchange(): return lax.ppermute(x, axis, [(i, i ^ bit) for i in range(n)])  32.8 us
    ppermute x18, waiting for transfers between devices, exchange(): return lax.ppermute(x, axis, [(i, i ^ bit) for i in range(n)])  9.73 us
    pallas_call x2, Pallas kernels, half_sweep(): pl.pallas_call(lambda *refs: half_kernel(far, n, *refs), in_specs=[SCALAR...  8.18 us
    pallas_call x1, Pallas kernels, build_incidence(): pl.pallas_call(incidence_kernel, in_specs=[SCALARS, SCALARS, REMAIN], out...  5.4 us
    pallas_call x1, Pallas kernels, build_listing(): pl.pallas_call(lambda *refs: listing_kernel(tile_total, *refs), in_specs=...  2.51 us
    pallas_call x1, Pallas kernels, robust_costs(): pl.pallas_call(lambda *refs: robust_kernel(len(parts), *refs), in_specs=[...  2.42 us
  transfers between devices with their start and end apart: 18, of which 4 were waited for; matrix products, arithmetic and copies ran while one was open for 3% of the time, Pallas kernels for 29%

profile of v3, /device:TPU:0, one launch (start us, length us, event | category | flops | bytes accessed | tf_op | source)
XLA Modules:
  0.0 64.8 jit_solution(14233299045630345241)
XLA Ops:
  0.6 3.1 %collective-permute-start = (f32[64,896]{1,0:T(8,128)}, f32[64,896]{1,0:T(8,128)S(1)}, u32[]{:S(2)}, u32[]{:S(2)}) collective-permute-start(f32[64,896]{1,0:T(8,128)} %param.13), channel_id=1, source_target_pairs={{0,4},{4,0},{8,12},{12,8},{1,5},{5,1},{9,13},{13,9},{2,6},{6,2},{1... | collective-permute-start | bytes 688136 | tf_op jit(solution)/shard_map/ppermute | solution.py:420
  3.7 1.0 %constant_dynamic-slice_fusion.1 = (f32[32,896]{1,0:T(8,128)S(1)}, f32[32,896]{1,0:T(8,128)S(1)}) fusion(f32[64,896]{1,0:T(8,128)} %param.13, s32[]{:T(128)S(6)} %select_n.37, s32[]{:T(128)S(6)} %select_n.38), kind=kLoop, calls=%fused_computation.8 | loop fusion | bytes 458760 | tf_op jit(solution)/shard_map/dynamic_slice | solution.py:430
  4.7 2.7 %collective-permute-start.3 = (f32[32,896]{1,0:T(8,128)S(1)}, f32[32,896]{1,0:T(8,128)S(1)}, u32[]{:S(2)}, u32[]{:S(2)}) collective-permute-start(f32[32,896]{1,0:T(8,128)S(1)} %get-tuple-element.47.refs_2_.refs_0_), channel_id=1, source_target_pairs={{0,8},{4,12},{8,0},{12,4},{1,9},{5,13},{9,1},{13,5},{2,10},{6,14},... | collective-permute-start | bytes 344072 | tf_op jit(solution)/shard_map/ppermute | solution.py:420
  7.4 2.5 %listing.1 = (s32[3,144]{1,0:T(4,128)S(1)}, s32[2]{0:T(128)S(1)}, bf16[16,128,128]{2,1,0:T(8,128)(2,1)S(1)}, f32[16,64,128]{2,1,0:T(8,128)S(1)}) custom-call(s32[16,16]{1,0:T(8,128)} %refs_0_.2, s32[16]{0:T(128)} %refs_1_.1, s32[16,128]{1,0:T(8,128)} %refs_2_.1, s32[64,512]{1,0:T(8,128)} %refs_3_.1), custom_call_target="tpu_custom_call" | custom-call | flops 1000000000 | bytes 10000000 | tf_op jit(solution)/shard_map/listing/pallas_call | solution.py:108
  9.9 2.0 %collective-permute-start.1 = (f32[32,896]{1,0:T(8,128)S(1)}, f32[32,896]{1,0:T(8,128)S(1)}, u32[]{:S(2)}, u32[]{:S(2)}) collective-permute-start(f32[32,896]{1,0:T(8,128)S(1)} %get-tuple-element.27.refs_2_), channel_id=1, source_target_pairs={{0,8},{4,12},{8,0},{12,4},{1,9},{5,13},{9,1},{13,5},{2,10},{6,14},... | collective-permute-start | bytes 344072 | tf_op jit(solution)/shard_map/ppermute | solution.py:420
  11.9 2.0 %collective-permute-start.2 = (f32[32,896]{1,0:T(8,128)S(1)}, f32[32,896]{1,0:T(8,128)S(1)}, u32[]{:S(2)}, u32[]{:S(2)}) collective-permute-start(f32[32,896]{1,0:T(8,128)S(1)} %get-tuple-element.27.refs_2_), channel_id=1, source_target_pairs={{0,12},{4,8},{8,4},{12,0},{1,13},{5,9},{9,5},{13,1},{2,14},{6,10},... | collective-permute-start | bytes 344072 | tf_op jit(solution)/shard_map/ppermute | solution.py:420
  13.9 5.4 %incidence.1 = (bf16[33024,128]{1,0:T(8,128)(2,1)S(1)}, bf16[33024,128]{1,0:T(8,128)(2,1)S(1)}) custom-call(s32[3,144]{1,0:T(4,128)S(1)} %get-tuple-element.24.list_ref.refs_0_, s32[2]{0:T(128)S(1)} %get-tuple-element.25.total_ref.refs_1_, s32[8,2048]{1,0:T(8,128)} %refs_0_.3), custom_call_target="tpu_custom_call" | custom-call | flops 1000000 | bytes 20000000 | tf_op jit(solution)/shard_map/incidence/pallas_call | solution.py:162
  19.3 4.1 %far_sweep.1 = (f32[32,2048]{1,0:T(8,128)S(1)}, f32[28,16,128]{2,1,0:T(8,128)S(1)}, f32[28,16,128]{2,1,0:T(8,128)S(1)}) custom-call(s32[3,144]{1,0:T(4,128)S(1)} %get-tuple-element.24.list_ref.refs_0_, s32[2]{0:T(128)S(1)} %get-tuple-element.25.total_ref.refs_1_, f32[32,896]{1,0:T(8,128)S(1)} %get-tuple-element.27.refs_2_, ...), custom_call_target="tpu_custom_call" | custom-call | flops 10000000000 | bytes 25000000 | tf_op jit(solution)/shard_map/far_sweep/pallas_call | solution.py:276
  23.5 4.3 %collective-permute-start.8 = (f32[28,16,128]{2,1,0:T(8,128)S(1)}, f32[28,16,128]{2,1,0:T(8,128)S(1)}, u32[]{:S(2)}, u32[]{:S(2)}) collective-permute-start(f32[28,16,128]{2,1,0:T(8,128)S(1)} %get-tuple-element.36), channel_id=1, source_target_pairs={{0,4},{4,0},{8,12},{12,8},{1,5},{5,1},{9,13},{13,9},{2,6},{6,2},{1... | collective-permute-start | bytes 688136 | tf_op jit(solution)/shard_map/ppermute | solution.py:420
  27.7 4.1 %near_sweep.1 = (f32[32,2048]{1,0:T(8,128)S(1)}, f32[28,16,128]{2,1,0:T(8,128)S(1)}, f32[28,16,128]{2,1,0:T(8,128)S(1)}) custom-call(s32[3,144]{1,0:T(4,128)S(1)} %get-tuple-element.24.list_ref.refs_0_, s32[2]{0:T(128)S(1)} %get-tuple-element.25.total_ref.refs_1_, f32[32,896]{1,0:T(8,128)S(1)} %get-tuple-element.47.refs_2_.refs_0_, ...), custom_call_target="tpu_custom_call" | custom-call | flops 10000000000 | bytes 25000000 | tf_op jit(solution)/shard_map/near_sweep/pallas_call | solution.py:276
  31.9 5.8 %collective-permute-start.10 = (f32[28,16,128]{2,1,0:T(8,128)S(1)}, f32[28,16,128]{2,1,0:T(8,128)S(1)}, u32[]{:S(2)}, u32[]{:S(2)}) collective-permute-start(f32[28,16,128]{2,1,0:T(8,128)S(1)} %add.33), channel_id=1, source_target_pairs={{0,8},{4,12},{8,0},{12,4},{1,9},{5,13},{9,1},{13,5},{2,10},{6,14},... | collective-permute-start | bytes 688136 | tf_op jit(solution)/shard_map/ppermute | solution.py:420
  37.7 2.0 %collective-permute-start.5 = (f32[1,896]{1,0:T(1,128)S(1)}, f32[1,896]{1,0:T(1,128)S(1)}, u32[]{:S(2)}, u32[]{:S(2)}) collective-permute-start(f32[1,896]{1,0:T(1,128)S(1)} %broadcast_in_dim.10.refs_4_), channel_id=1, source_target_pairs={{0,4},{4,0},{8,12},{12,8},{1,5},{5,1},{9,13},{13,9},{2,6},{6,2},{1... | collective-permute-start | bytes 10760 | tf_op jit(solution)/shard_map/ppermute | solution.py:420
  39.8 2.4 %collective-permute-start.7 = (f32[1,896]{1,0:T(1,128)S(1)}, f32[1,896]{1,0:T(1,128)S(1)}, u32[]{:S(2)}, u32[]{:S(2)}) collective-permute-start(f32[1,896]{1,0:T(1,128)S(1)} %broadcast_in_dim.10.refs_4_), channel_id=1, source_target_pairs={{0,12},{4,8},{8,4},{12,0},{1,13},{5,9},{9,5},{13,1},{2,14},{6,10},... | collective-permute-start | bytes 10760 | tf_op jit(solution)/shard_map/ppermute | solution.py:420
  42.3 3.0 %collective-permute-done.5.refs_5_ = f32[1,896]{1,0:T(1,128)S(1)} collective-permute-done((f32[1,896]{1,0:T(1,128)S(1)}, f32[1,896]{1,0:T(1,128)S(1)}, u32[]{:S(2)}, u32[]{:S(2)}) %collective-permute-start.5) | collective-permute-done | bytes 3616 | tf_op jit(solution)/shard_map/ppermute | solution.py:420
  45.7 1.1 %collective-permute-done.14 = f32[28,128]{1,0:T(8,128)S(1)} collective-permute-done((f32[28,128]{1,0:T(8,128)S(1)}, f32[28,128]{1,0:T(8,128)S(1)}, u32[]{:S(2)}, u32[]{:S(2)}) %collective-permute-start.14) | collective-permute-done | bytes 14368 | tf_op jit(solution)/shard_map/ppermute | solution.py:420
  46.8 1.5 %collective-permute-start.15 = (f32[28,128]{1,0:T(8,128)S(1)}, f32[28,128]{1,0:T(8,128)S(1)}, u32[]{:S(2)}, u32[]{:S(2)}) collective-permute-start(f32[28,128]{1,0:T(8,128)S(1)} %add.38), channel_id=1, source_target_pairs={{0,2},{2,0},{1,3},{3,1},{4,6},{6,4},{5,7},{7,5},{8,10},{10,8},{9,1... | collective-permute-start | bytes 43016 | tf_op jit(solution)/shard_map/ppermute | solution.py:420
  48.3 2.2 %collective-permute-done.15 = f32[28,128]{1,0:T(8,128)S(1)} collective-permute-done((f32[28,128]{1,0:T(8,128)S(1)}, f32[28,128]{1,0:T(8,128)S(1)}, u32[]{:S(2)}, u32[]{:S(2)}) %collective-permute-start.15) | collective-permute-done | bytes 14368 | tf_op jit(solution)/shard_map/ppermute | solution.py:420
  50.6 1.0 %collective-permute-start.16 = (f32[28,128]{1,0:T(8,128)S(1)}, f32[28,128]{1,0:T(8,128)S(1)}, u32[]{:S(2)}, u32[]{:S(2)}) collective-permute-start(f32[28,128]{1,0:T(8,128)S(1)} %add.39), channel_id=1, source_target_pairs={{0,4},{4,0},{8,12},{12,8},{1,5},{5,1},{9,13},{13,9},{2,6},{6,2},{1... | collective-permute-start | bytes 43016 | tf_op jit(solution)/shard_map/ppermute | solution.py:420
  52.3 1.1 %collective-permute-start.11 = (f32[16,896]{1,0:T(8,128)S(1)}, f32[16,896]{1,0:T(8,128)S(1)}, u32[]{:S(2)}, u32[]{:S(2)}) collective-permute-start(f32[16,896]{1,0:T(8,128)S(1)} %get-tuple-element.41), channel_id=1, source_target_pairs={{0,4},{4,0},{8,12},{12,8},{1,5},{5,1},{9,13},{13,9},{2,6},{6,2},{1... | collective-permute-start | bytes 172040 | tf_op jit(solution)/shard_map/ppermute | solution.py:420
  53.4 1.9 %collective-permute-start.12 = (f32[16,896]{1,0:T(8,128)S(1)}, f32[16,896]{1,0:T(8,128)S(1)}, u32[]{:S(2)}, u32[]{:S(2)}) collective-permute-start(f32[16,896]{1,0:T(8,128)S(1)} %get-tuple-element.42), channel_id=1, source_target_pairs={{0,8},{4,12},{8,0},{12,4},{1,9},{5,13},{9,1},{13,5},{2,10},{6,14},... | collective-permute-start | bytes 172040 | tf_op jit(solution)/shard_map/ppermute | solution.py:420
  55.3 1.4 %collective-permute-start.13 = (f32[16,896]{1,0:T(8,128)S(1)}, f32[16,896]{1,0:T(8,128)S(1)}, u32[]{:S(2)}, u32[]{:S(2)}) collective-permute-start(f32[16,896]{1,0:T(8,128)S(1)} %get-tuple-element.43), channel_id=1, source_target_pairs={{0,12},{4,8},{8,4},{12,0},{1,13},{5,9},{9,5},{13,1},{2,14},{6,10},... | collective-permute-start | bytes 172040 | tf_op jit(solution)/shard_map/ppermute | solution.py:420
  56.7 1.6 %collective-permute-start.17 = (f32[28,128]{1,0:T(8,128)S(1)}, f32[28,128]{1,0:T(8,128)S(1)}, u32[]{:S(2)}, u32[]{:S(2)}) collective-permute-start(f32[28,128]{1,0:T(8,128)S(1)} %add.40.refs_1_), channel_id=1, source_target_pairs={{0,8},{4,12},{8,0},{12,4},{1,9},{5,13},{9,1},{13,5},{2,10},{6,14},... | collective-permute-start | bytes 43016 | tf_op jit(solution)/shard_map/ppermute | solution.py:420
  58.4 3.3 %collective-permute-done.17.refs_2_ = f32[28,128]{1,0:T(8,128)S(1)} collective-permute-done((f32[28,128]{1,0:T(8,128)S(1)}, f32[28,128]{1,0:T(8,128)S(1)}, u32[]{:S(2)}, u32[]{:S(2)}) %collective-permute-start.17) | collective-permute-done | bytes 14368 | tf_op jit(solution)/shard_map/ppermute | solution.py:420
  61.6 2.4 %robust.1 = f32[16,128]{1,0:T(8,128)} custom-call(s32[8,2048]{1,0:T(8,128)S(1)} %copy-done, f32[28,128]{1,0:T(8,128)S(1)} %add.40.refs_1_, f32[28,128]{1,0:T(8,128)S(1)} %collective-permute-done.17.refs_2_), custom_call_target="tpu_custom_call" | custom-call | flops 1000000 | bytes 1000000 | tf_op jit(solution)/shard_map/robust/pallas_call | solution.py:406
  (40 shorter events, 2.2 us)
Async XLA Ops:
  0.6 18.7 %collective-permute-start = (f32[64,896]{1,0:T(8,128)}, f32[64,896]{1,0:T(8,128)S(1)}, u32[]{:S(2)}, u32[]{:S(2)}) collective-permute-start(f32[64,896]{1,0:T(8,128)} %param.13), channel_id=1, source_target_pairs={{0,4},{4,0},{8,12},{12,8},{1,5},{5,1},{9,13},{13,9},{2,6},{6,2},{1... | collective-permute-start | bytes 688136 | tf_op jit(solution)/shard_map/ppermute | solution.py:420
  4.7 14.6 %collective-permute-start.3 = (f32[32,896]{1,0:T(8,128)S(1)}, f32[32,896]{1,0:T(8,128)S(1)}, u32[]{:S(2)}, u32[]{:S(2)}) collective-permute-start(f32[32,896]{1,0:T(8,128)S(1)} %get-tuple-element.47.refs_2_.refs_0_), channel_id=1, source_target_pairs={{0,8},{4,12},{8,0},{12,4},{1,9},{5,13},{9,1},{13,5},{2,10},{6,14},... | collective-permute-start | bytes 344072 | tf_op jit(solution)/shard_map/ppermute | solution.py:420
  7.4 11.9 %collective-permute-start.4 = (f32[32,896]{1,0:T(8,128)S(1)}, f32[32,896]{1,0:T(8,128)S(1)}, u32[]{:S(2)}, u32[]{:S(2)}) collective-permute-start(f32[32,896]{1,0:T(8,128)S(1)} %get-tuple-element.47.refs_2_.refs_0_), channel_id=1, source_target_pairs={{0,12},{4,8},{8,4},{12,0},{1,13},{5,9},{9,5},{13,1},{2,14},{6,10},... | collective-permute-start | bytes 344072 | tf_op jit(solution)/shard_map/ppermute | solution.py:420
  9.9 17.8 %collective-permute-start.1 = (f32[32,896]{1,0:T(8,128)S(1)}, f32[32,896]{1,0:T(8,128)S(1)}, u32[]{:S(2)}, u32[]{:S(2)}) collective-permute-start(f32[32,896]{1,0:T(8,128)S(1)} %get-tuple-element.27.refs_2_), channel_id=1, source_target_pairs={{0,8},{4,12},{8,0},{12,4},{1,9},{5,13},{9,1},{13,5},{2,10},{6,14},... | collective-permute-start | bytes 344072 | tf_op jit(solution)/shard_map/ppermute | solution.py:420
  11.9 15.8 %collective-permute-start.2 = (f32[32,896]{1,0:T(8,128)S(1)}, f32[32,896]{1,0:T(8,128)S(1)}, u32[]{:S(2)}, u32[]{:S(2)}) collective-permute-start(f32[32,896]{1,0:T(8,128)S(1)} %get-tuple-element.27.refs_2_), channel_id=1, source_target_pairs={{0,12},{4,8},{8,4},{12,0},{1,13},{5,9},{9,5},{13,1},{2,14},{6,10},... | collective-permute-start | bytes 344072 | tf_op jit(solution)/shard_map/ppermute | solution.py:420
  23.4 14.3 %copy-start.2 = (f32[896]{0:T(1024)S(1)}, f32[896]{0:T(1024)}, u32[]{:S(2)}) copy-start(f32[896]{0:T(1024)} %param.14) | copy-start | bytes 10756
  23.4 18.7 %copy-start.3 = (f32[64]{0:T(128)S(1)}, f32[64]{0:T(128)}, u32[]{:S(2)}) copy-start(f32[64]{0:T(128)} %param.15) | copy-start | bytes 772
  23.4 38.2 %copy-start = (s32[8,2048]{1,0:T(8,128)S(1)}, s32[8,2048]{1,0:T(8,128)}, u32[]{:S(2)}) copy-start(s32[8,2048]{1,0:T(8,128)} %refs_0_.3) | copy-start | bytes 196612
  23.5 8.4 %collective-permute-start.8 = (f32[28,16,128]{2,1,0:T(8,128)S(1)}, f32[28,16,128]{2,1,0:T(8,128)S(1)}, u32[]{:S(2)}, u32[]{:S(2)}) collective-permute-start(f32[28,16,128]{2,1,0:T(8,128)S(1)} %get-tuple-element.36), channel_id=1, source_target_pairs={{0,4},{4,0},{8,12},{12,8},{1,5},{5,1},{9,13},{13,9},{2,6},{6,2},{1... | collective-permute-start | bytes 688136 | tf_op jit(solution)/shard_map/ppermute | solution.py:420
  31.9 13.4 %collective-permute-start.10 = (f32[28,16,128]{2,1,0:T(8,128)S(1)}, f32[28,16,128]{2,1,0:T(8,128)S(1)}, u32[]{:S(2)}, u32[]{:S(2)}) collective-permute-start(f32[28,16,128]{2,1,0:T(8,128)S(1)} %add.33), channel_id=1, source_target_pairs={{0,8},{4,12},{8,0},{12,4},{1,9},{5,13},{9,1},{13,5},{2,10},{6,14},... | collective-permute-start | bytes 688136 | tf_op jit(solution)/shard_map/ppermute | solution.py:420
  37.7 7.6 %collective-permute-start.9 = (f32[28,16,128]{2,1,0:T(8,128)S(1)}, f32[28,16,128]{2,1,0:T(8,128)S(1)}, u32[]{:S(2)}, u32[]{:S(2)}) collective-permute-start(f32[28,16,128]{2,1,0:T(8,128)S(1)} %get-tuple-element.38), channel_id=1, source_target_pairs={{0,4},{4,0},{8,12},{12,8},{1,5},{5,1},{9,13},{13,9},{2,6},{6,2},{1... | collective-permute-start | bytes 688136 | tf_op jit(solution)/shard_map/ppermute | solution.py:420
  37.7 7.6 %collective-permute-start.5 = (f32[1,896]{1,0:T(1,128)S(1)}, f32[1,896]{1,0:T(1,128)S(1)}, u32[]{:S(2)}, u32[]{:S(2)}) collective-permute-start(f32[1,896]{1,0:T(1,128)S(1)} %broadcast_in_dim.10.refs_4_), channel_id=1, source_target_pairs={{0,4},{4,0},{8,12},{12,8},{1,5},{5,1},{9,13},{13,9},{2,6},{6,2},{1... | collective-permute-start | bytes 10760 | tf_op jit(solution)/shard_map/ppermute | solution.py:420
  39.7 5.6 %collective-permute-start.6 = (f32[1,896]{1,0:T(1,128)S(1)}, f32[1,896]{1,0:T(1,128)S(1)}, u32[]{:S(2)}, u32[]{:S(2)}) collective-permute-start(f32[1,896]{1,0:T(1,128)S(1)} %broadcast_in_dim.10.refs_4_), channel_id=1, source_target_pairs={{0,8},{4,12},{8,0},{12,4},{1,9},{5,13},{9,1},{13,5},{2,10},{6,14},... | collective-permute-start | bytes 10760 | tf_op jit(solution)/shard_map/ppermute | solution.py:420
  39.8 5.5 %collective-permute-start.7 = (f32[1,896]{1,0:T(1,128)S(1)}, f32[1,896]{1,0:T(1,128)S(1)}, u32[]{:S(2)}, u32[]{:S(2)}) collective-permute-start(f32[1,896]{1,0:T(1,128)S(1)} %broadcast_in_dim.10.refs_4_), channel_id=1, source_target_pairs={{0,12},{4,8},{8,4},{12,0},{1,13},{5,9},{9,5},{13,1},{2,14},{6,10},... | collective-permute-start | bytes 10760 | tf_op jit(solution)/shard_map/ppermute | solution.py:420
  45.6 1.2 %collective-permute-start.14 = (f32[28,128]{1,0:T(8,128)S(1)}, f32[28,128]{1,0:T(8,128)S(1)}, u32[]{:S(2)}, u32[]{:S(2)}) collective-permute-start(f32[28,128]{1,0:T(8,128)S(1)} %get-tuple-element.44), channel_id=1, source_target_pairs={{0,1},{1,0},{2,3},{3,2},{4,5},{5,4},{6,7},{7,6},{8,9},{9,8},{10,11... | collective-permute-start | bytes 43016 | tf_op jit(solution)/shard_map/ppermute | solution.py:420
  46.8 3.7 %collective-permute-start.15 = (f32[28,128]{1,0:T(8,128)S(1)}, f32[28,128]{1,0:T(8,128)S(1)}, u32[]{:S(2)}, u32[]{:S(2)}) collective-permute-start(f32[28,128]{1,0:T(8,128)S(1)} %add.38), channel_id=1, source_target_pairs={{0,2},{2,0},{1,3},{3,1},{4,6},{6,4},{5,7},{7,5},{8,10},{10,8},{9,1... | collective-permute-start | bytes 43016 | tf_op jit(solution)/shard_map/ppermute | solution.py:420
  50.6 6.2 %collective-permute-start.16 = (f32[28,128]{1,0:T(8,128)S(1)}, f32[28,128]{1,0:T(8,128)S(1)}, u32[]{:S(2)}, u32[]{:S(2)}) collective-permute-start(f32[28,128]{1,0:T(8,128)S(1)} %add.39), channel_id=1, source_target_pairs={{0,4},{4,0},{8,12},{12,8},{1,5},{5,1},{9,13},{13,9},{2,6},{6,2},{1... | collective-permute-start | bytes 43016 | tf_op jit(solution)/shard_map/ppermute | solution.py:420
  52.3 11.7 %collective-permute-start.11 = (f32[16,896]{1,0:T(8,128)S(1)}, f32[16,896]{1,0:T(8,128)S(1)}, u32[]{:S(2)}, u32[]{:S(2)}) collective-permute-start(f32[16,896]{1,0:T(8,128)S(1)} %get-tuple-element.41), channel_id=1, source_target_pairs={{0,4},{4,0},{8,12},{12,8},{1,5},{5,1},{9,13},{13,9},{2,6},{6,2},{1... | collective-permute-start | bytes 172040 | tf_op jit(solution)/shard_map/ppermute | solution.py:420
  53.4 10.7 %collective-permute-start.12 = (f32[16,896]{1,0:T(8,128)S(1)}, f32[16,896]{1,0:T(8,128)S(1)}, u32[]{:S(2)}, u32[]{:S(2)}) collective-permute-start(f32[16,896]{1,0:T(8,128)S(1)} %get-tuple-element.42), channel_id=1, source_target_pairs={{0,8},{4,12},{8,0},{12,4},{1,9},{5,13},{9,1},{13,5},{2,10},{6,14},... | collective-permute-start | bytes 172040 | tf_op jit(solution)/shard_map/ppermute | solution.py:420
  55.3 8.8 %collective-permute-start.13 = (f32[16,896]{1,0:T(8,128)S(1)}, f32[16,896]{1,0:T(8,128)S(1)}, u32[]{:S(2)}, u32[]{:S(2)}) collective-permute-start(f32[16,896]{1,0:T(8,128)S(1)} %get-tuple-element.43), channel_id=1, source_target_pairs={{0,12},{4,8},{8,4},{12,0},{1,13},{5,9},{9,5},{13,1},{2,14},{6,10},... | collective-permute-start | bytes 172040 | tf_op jit(solution)/shard_map/ppermute | solution.py:420
  56.7 4.9 %collective-permute-start.17 = (f32[28,128]{1,0:T(8,128)S(1)}, f32[28,128]{1,0:T(8,128)S(1)}, u32[]{:S(2)}, u32[]{:S(2)}) collective-permute-start(f32[28,128]{1,0:T(8,128)S(1)} %add.40.refs_1_), channel_id=1, source_target_pairs={{0,8},{4,12},{8,0},{12,4},{1,9},{5,13},{9,1},{13,5},{2,10},{6,14},... | collective-permute-start | bytes 43016 | tf_op jit(solution)/shard_map/ppermute | solution.py:420
  64.1 0.7 %copy-start.1 = (f32[64,896]{1,0:T(8,128)}, f32[64,896]{1,0:T(8,128)S(1)}, u32[]{:S(2)}) copy-start(f32[64,896]{1,0:T(8,128)S(1)} %constant_dynamic-update-slice_fusion) | copy-start | bytes 688132

commit v4 on v3

--- a/solution.py
+++ b/solution.py
@@ -26,7 +26,7 @@
 ARRAY = pl.BlockSpec(memory_space=pltpu.VMEM)
 LISTS = 3
 TOGETHER = 8
-UNROLL = 7
+UNROLL = 28
 LB_BITS = 7
 COUNTED = 8
 
@@ -59,9 +59,9 @@
 
 
 def listing_kernel(tile_total, *refs):
-    given, (list_ref, total_ref, same_ref, wanted_ref) = refs[:4], refs[4:8]
-    local, arrived = refs[8:12], refs[12]
-    tiles_ref, count_ref, comm_ref, demand_ref = local
+    given, (list_ref, total_ref, same_ref, wanted_ref, kept_ref) = refs[:5], refs[5:10]
+    local, arrived = refs[10:15], refs[15]
+    tiles_ref, count_ref, comm_ref, demand_ref, capacity_ref = local
     copies = fetch(given, local, arrived)
     blocks = tiles_ref.shape[0]
     spare = blocks * MAXT
@@ -91,6 +91,7 @@
         return carry
 
     lax.fori_loop(entries, batches * BATCH, pad, 0)
+    kept_ref[...] = capacity_ref[...]
 
     commodity_rows = lax.broadcasted_iota(jnp.int32, (LB, PATHS_PER_BLOCK), 0)
     for block in range(blocks):
@@ -102,22 +103,23 @@
         wanted_ref[block] = jnp.dot(demand, onehot, preferred_element_type=F32) * DEMAND_UNIT
 
 
-def build_listing(tile_total, block_tiles, block_count, path_commodity, demand):
+def build_listing(tile_total, block_tiles, block_count, path_commodity, demand, capacity):
     blocks = block_tiles.shape[0]
-    given = stay(block_tiles, block_count, path_commodity, demand)
+    given = stay(block_tiles, block_count, path_commodity, demand, capacity.reshape(-1, LB))
     return pl.pallas_call(
         lambda *refs: listing_kernel(tile_total, *refs),
-        in_specs=[REMAIN] * 4,
-        out_specs=[SCALARS, SCALARS, ARRAY, ARRAY],
+        in_specs=[REMAIN] * 5,
+        out_specs=[SCALARS, SCALARS, ARRAY, ARRAY, ARRAY],
         out_shape=[
             jax.ShapeDtypeStruct((LISTS, blocks * MAXT // 2 + BATCH), jnp.int32),
             jax.ShapeDtypeStruct((2,), jnp.int32),
             jax.ShapeDtypeStruct((blocks, PATHS_PER_BLOCK, PATHS_PER_BLOCK), BF16),
             jax.ShapeDtypeStruct((blocks, demand.shape[0], PATHS_PER_BLOCK), F32),
+            jax.ShapeDtypeStruct(given[4].shape, F32),
         ],
         scratch_shapes=[pltpu.SMEM(a.shape, a.dtype) for a in given[:2]]
         + [pltpu.VMEM(a.shape, a.dtype) for a in given[2:]]
-        + [pltpu.SemaphoreType.DMA((4,))],
+        + [pltpu.SemaphoreType.DMA((5,))],
         compiler_params=pltpu.CompilerParams(vmem_limit_bytes=8 * MIB),
         cost_estimate=pl.CostEstimate(flops=10**9, bytes_accessed=10**7, transcendentals=0),
         name="listing",
@@ -241,7 +243,7 @@
 
 
 def half_kernel(far, n, list_ref, total_ref, *refs):
-    pieces, (hits_ref, turned_ref, same_ref, wanted_ref) = refs[:n], refs[n : n + 4]
+    pieces, (hits_ref, turned_ref, same_ref, wanted_ref, capacity_ref) = refs[:n], refs[n : n + 5]
     flows_ref, mine_ref, other_ref, *scratch = refs[-7:]
     z = lax.axis_index("path")
     rows = scratch[0].shape[1] // 2
@@ -265,9 +267,12 @@
         for k in range(load_ref.shape[0] - 1):
             high = load_ref[k, aligned(place, height, height), :]
             out_ref[k] = high + load_ref[k, pl.ds(pl.multiple_of(rows + place * height, height), height), :]
-
-
-def half_sweep(pieces, rows, built, far):
+    for out_ref, start in ((mine_ref, 0), (other_ref, height // 2 if far else 0)):
+        out_ref[load_ref.shape[0] - 1] = jnp.zeros((height, LB), F32)
+        out_ref[load_ref.shape[0] - 1, start : start + shard_tiles, :] = capacity_ref[...]
+
+
+def half_sweep(pieces, rows, built, capacity, far):
     hits, turned, pairs, total, same, wanted = built
     own = pieces[0].shape[1]
     n = len(pieces)
@@ -275,15 +280,15 @@
     tiles = n * own // LB
     return pl.pallas_call(
         lambda *refs: half_kernel(far, n, *refs),
-        in_specs=[SCALARS, SCALARS] + [ARRAY] * (n + 4),
+        in_specs=[SCALARS, SCALARS] + [ARRAY] * (n + 5),
         out_specs=[ARRAY] * 3,
         out_shape=[jax.ShapeDtypeStruct((rows, blocks * PATHS_PER_BLOCK), F32)]
-        + [jax.ShapeDtypeStruct((tiles, rows // 2, LB), F32)] * 2,
+        + [jax.ShapeDtypeStruct((tiles + 1, rows // 2, LB), F32)] * 2,
         scratch_shapes=sweep_scratch(rows, tiles, blocks),
         compiler_params=pltpu.CompilerParams(vmem_limit_bytes=16 * MIB),
         cost_estimate=sweep_cost(25 * 10**6),
         name="far_sweep" if far else "near_sweep",
-    )(pairs, total, *pieces, hits, turned, same, wanted)
+    )(pairs, total, *pieces, hits, turned, same, wanted, capacity)
 
 
 def wide_kernel(list_ref, total_ref, lengths_ref, hits_ref, turned_ref, same_ref, wanted_ref, flows_ref, out_ref, *scratch):
@@ -326,13 +331,15 @@
 
 
 def growth_kernel(n, parts, *refs):
-    lengths, capacities, weight_ref = refs[:n], refs[n : 2 * n], refs[2 * n]
-    loads = refs[2 * n + 1 : 2 * n + 1 + parts]
+    lengths, (capacity_ref, weight_ref) = refs[:n], refs[n : n + 2]
+    loads = refs[n + 2 : n + 2 + parts]
     next_refs, mixed_ref, grown_ref = refs[-n - 2 : -2], refs[-2], refs[-1]
     z = lax.axis_index("path")
     links_total, height, _ = grown_ref.shape
     shard_tiles = links_total // n
     total = jnp.zeros((height, LB), F32)
+    own, near, far = capacity_ref[...], loads[1][links_total], loads[2][links_total]
+    capacities = (own, near, far, far[height // 2 :])
     for m in range(n):
         row = aligned(z if lengths[m].shape[0] == n * height else lax.rem(z, 2), height, height)
         first = (z ^ m) * shard_tiles
@@ -341,7 +348,7 @@
             load = loads[0][first + k]
             for ref in loads[1:]:
                 load = load + ref[first + k]
-            grown = lengths[m][row, columns] * jnp.exp(STEP_RATE * load / capacities[m][:, columns])
+            grown = lengths[m][row, columns] * jnp.exp(STEP_RATE * load / capacities[m][k : k + 1])
             grown_ref[m * shard_tiles + k] = grown
             total = total + grown
     factor = (links_total * LB) / jnp.sum(total, axis=1, keepdims=True)
@@ -354,19 +361,19 @@
             mixed_ref[pl.ds(first + k, 1), :] = jnp.sum(weight * new, axis=0, keepdims=True)
 
 
-def grow(loads, lengths, capacities, weights):
+def grow(loads, lengths, capacity, weights):
     n, parts = len(lengths), len(loads)
-    tiles, height, _ = loads[0].shape
+    tiles, height = loads[0].shape[0] - 1, loads[0].shape[1]
     return pl.pallas_call(
         lambda *refs: growth_kernel(n, parts, *refs),
-        in_specs=[ARRAY] * (2 * n + 1 + parts),
+        in_specs=[ARRAY] * (n + 2 + parts),
         out_specs=[ARRAY] * (n + 1),
         out_shape=[jax.ShapeDtypeStruct((height, tiles * LB // n), F32)] * n + [jax.ShapeDtypeStruct((tiles, LB), F32)],
         scratch_shapes=[pltpu.VMEM((tiles, height, LB), F32)],
         compiler_params=pltpu.CompilerParams(vmem_limit_bytes=8 * MIB),
         cost_estimate=pl.CostEstimate(flops=10**6, bytes_accessed=5 * 10**6, transcendentals=10**5),
         name="growth",
-    )(*lengths, *capacities, weights, *loads)
+    )(*lengths, capacity, weights, *loads)
 
 
 def robust_kernel(parts, links_ref, *refs):
@@ -434,34 +441,39 @@
 
     shared = swap(lengths, 1)
     far_pieces = [far, shared, swap(near, 2), swap(near, 3)]
-    pairs, total, same, wanted = build_listing(n * own // LB, block_tiles, block_count, path_commodity, demand)
-    late, same = lax.optimization_barrier((far, same))
-    near_pieces = [near, shared, swap(late, 2), swap(late, 3)]
+    pairs, total, same, wanted, capacity_tiles = build_listing(
+        n * own // LB, block_tiles, block_count, path_commodity, demand, capacity
+    )
+    straight_rows = swap(far, 2)
+    near_pieces = [near, shared, straight_rows, swap(straight_rows, 1)]
     built = (*build_incidence(path_links, pairs, total), pairs, total, same, wanted)
-    far_flows, straight, crossed = half_sweep(far_pieces, half, built, True)
+    far_flows, straight, crossed = half_sweep(far_pieces, half, built, capacity_tiles, True)
     partial = straight + swap(crossed, 1)
-    near_flows, mine, other = half_sweep(near_pieces, half, built, False)
-    partial, other = lax.optimization_barrier((partial, other))
+    near_flows, mine, other = half_sweep(near_pieces, half, built, capacity_tiles, False)
+    partial, other, near_flows = lax.optimization_barrier((partial, other, near_flows))
     loads = [mine, swap(other, 1), swap(partial, 2)]
-    capacity_row = capacity[None, :]
-    capacities = [capacity_row] + [swap(capacity_row, m) for m in range(1, n)]
-    *new, mixed = grow(loads, near_pieces, capacities, scenario_weight[:, None])
+    first, second = jnp.where(side == 0, near_flows, far_flows), jnp.where(side == 0, far_flows, near_flows)
+    flows = jnp.concatenate([first, second], axis=0)
+    weight_column = scenario_weight[:, None]
+    flows, weight_column = lax.optimization_barrier((flows, weight_column))
+    *new, mixed = grow(loads, near_pieces, capacity_tiles, weight_column)
     mixed = mixed + exchange(mixed, "sub", 2, 1)
     mixed = mixed + exchange(mixed, "scen", 2, 1)
     mixed = mixed + swap(mixed, 1)
     parts = [mixed, swap(mixed, 2)]
     arrived = [new[0]] + [swap(new[m], m) for m in range(1, n)]
-    robust = robust_costs(path_links, parts)
     lengths_next = jnp.zeros((rows, own), F32)
     for m in range(n):
         lengths_next = lax.dynamic_update_slice(lengths_next, arrived[m], ((z ^ m) * height, 0))
-    first, second = jnp.where(side == 0, near_flows, far_flows), jnp.where(side == 0, far_flows, near_flows)
-    return jnp.concatenate([first, second], axis=0), lengths_next, robust
+    parts[1], lengths_next = lax.optimization_barrier((parts[1], lengths_next))
+    robust = robust_costs(path_links, parts)
+    return flows, lengths_next, robust
 
 
 def body_wide(sizes, path_links, block_tiles, block_count, path_commodity, demand, lengths, capacity, scenario_weight):
     gathered = lax.all_gather(lengths, "path", axis=0, tiled=False)
-    pairs, total, same, wanted = build_listing(gathered.shape[0] * gathered.shape[2] // LB, block_tiles, block_count, path_commodity, demand)
+    tiles = gathered.shape[0] * gathered.shape[2] // LB
+    pairs, total, same, wanted, _ = build_listing(tiles, block_tiles, block_count, path_commodity, demand, capacity)
     built = (*build_incidence(path_links, pairs, total), pairs, total, same, wanted)
     flows, loads = wide_sweep(gathered, built)
     loads = loads.transpose(1, 0, 2).reshape(lengths.shape[0], -1)
@@ -478,7 +490,7 @@
     sizes = dict(mesh.shape)
 
     def body(*args):
-        paired = sizes["path"] == 4 and sizes["scen"] == 2 and sizes["sub"] == 2 and args[5].shape[0] % 64 == 0
+        paired = sizes["path"] == 4 and sizes["scen"] == 2 and sizes["sub"] == 2 and args[5].shape[0] % 64 == 0 and args[5].shape[1] // LB <= args[5].shape[0] // 8
         return (body_paired if paired else body_wide)(sizes, *args)
 
     return jax.shard_map(

time: 65.6 us -> 64.5 us (0.983)
  waiting for transfers between devices: 9.73 us -> 21.7 us
  starting transfers between devices: 32.8 us -> 21.5 us
  local copies, waits for them, and re-layouts: 1.85 us -> 1.16 us
    ppermute x18 -> x15, waiting for transfers between devices: 9.73 us -> 21.7 us  [exchange(): return lax.ppermute(x, axis, [(i, i ^ bit) for i in range(n)])]
    ppermute x18 -> x15, starting transfers between devices: 32.8 us -> 21.5 us  [exchange(): return lax.ppermute(x, axis, [(i, i ^ bit) for i in range(n)])]
    unnamed x8 -> x6, local copies, waits for them, and re-layouts: 0.7 us -> 0.02 us
  transfers between devices with their start and end apart: 18 -> 15, of which waited for: 4 -> 7; matrix products, arithmetic and copies ran while one was open for 3% -> 3% of each run, Pallas kernels for 29% -> 25%
where the time goes in v4:
time: 64.5 us; the launch traced here: 64.3 us
  waiting for transfers between devices  21.7 us (34%)
  starting transfers between devices  21.5 us (33%)
  Pallas kernels  18.2 us (28%)
  local copies, waits for them, and re-layouts  1.16 us (2%)
  other arithmetic  0.91 us (1%)
  between operations  0.79 us (1%)
    ppermute x15, waiting for transfers between devices, exchange(): return lax.ppermute(x, axis, [(i, i ^ bit) for i in range(n)])  21.7 us
    ppermute x15, starting transfers between devices, exchange(): return lax.ppermute(x, axis, [(i, i ^ bit) for i in range(n)])  21.5 us
    pallas_call x2, Pallas kernels, half_sweep(): pl.pallas_call(lambda *refs: half_kernel(far, n, *refs), in_specs=[SCALAR...  8.14 us
    pallas_call x1, Pallas kernels, build_incidence(): pl.pallas_call(incidence_kernel, in_specs=[SCALARS, SCALARS, REMAIN], out...  5.4 us
    pallas_call x1, Pallas kernels, build_listing(): pl.pallas_call(lambda *refs: listing_kernel(tile_total, *refs), in_specs=...  2.5 us
    pallas_call x1, Pallas kernels, robust_costs(): pl.pallas_call(lambda *refs: robust_kernel(len(parts), *refs), in_specs=[...  1.93 us
  transfers between devices with their start and end apart: 15, of which 7 were waited for; matrix products, arithmetic and copies ran while one was open for 3% of the time, Pallas kernels for 25%

profile of v4, /device:TPU:0, one launch (start us, length us, event | category | flops | bytes accessed | tf_op | source)
XLA Modules:
  0.0 64.3 jit_solution(17551865409228110658)
XLA Ops:
  0.6 3.1 %collective-permute-start = (f32[64,896]{1,0:T(8,128)}, f32[64,896]{1,0:T(8,128)S(1)}, u32[]{:S(2)}, u32[]{:S(2)}) collective-permute-start(f32[64,896]{1,0:T(8,128)} %param.13), channel_id=1, source_target_pairs={{0,4},{4,0},{8,12},{12,8},{1,5},{5,1},{9,13},{13,9},{2,6},{6,2},{1... | collective-permute-start | bytes 688136 | tf_op jit(solution)/shard_map/ppermute | solution.py:427
  3.7 1.0 %constant_dynamic-slice_fusion = (f32[32,896]{1,0:T(8,128)S(1)}, f32[32,896]{1,0:T(8,128)S(1)}) fusion(f32[64,896]{1,0:T(8,128)} %param.13, s32[]{:T(128)S(6)} %select_n.38, s32[]{:T(128)S(6)} %select_n.37), kind=kLoop, calls=%fused_computation.7 | loop fusion | bytes 458760 | tf_op jit(solution)/shard_map/dynamic_slice | solution.py:437
  4.7 2.7 %collective-permute-start.4 = (f32[32,896]{1,0:T(8,128)S(1)}, f32[32,896]{1,0:T(8,128)S(1)}, u32[]{:S(2)}, u32[]{:S(2)}) collective-permute-start(f32[32,896]{1,0:T(8,128)S(1)} %get-tuple-element.56.refs_2_), channel_id=1, source_target_pairs={{0,8},{4,12},{8,0},{12,4},{1,9},{5,13},{9,1},{13,5},{2,10},{6,14},... | collective-permute-start | bytes 344072 | tf_op jit(solution)/shard_map/ppermute | solution.py:427
  7.7 2.5 %collective-permute-start.2 = (f32[32,896]{1,0:T(8,128)S(1)}, f32[32,896]{1,0:T(8,128)S(1)}, u32[]{:S(2)}, u32[]{:S(2)}) collective-permute-start(f32[32,896]{1,0:T(8,128)S(1)} %get-tuple-element.55.refs_2_.refs_0_), channel_id=1, source_target_pairs={{0,12},{4,8},{8,4},{12,0},{1,13},{5,9},{9,5},{13,1},{2,14},{6,10},... | collective-permute-start | bytes 344072 | tf_op jit(solution)/shard_map/ppermute | solution.py:427
  10.2 2.5 %listing.1 = (s32[3,144]{1,0:T(4,128)S(1)}, s32[2]{0:T(128)S(1)}, bf16[16,128,128]{2,1,0:T(8,128)(2,1)S(1)}, f32[16,64,128]{2,1,0:T(8,128)S(1)}, f32[7,128]{1,0:T(8,128)S(1)}) custom-call(s32[16,16]{1,0:T(8,128)} %refs_0_.2, s32[16]{0:T(128)} %refs_1_.1, s32[16,128]{1,0:T(8,128)} %refs_2_.1, s32[64,512]{1,0:T(8,128)} %refs_3_.1, f32[7,128]{1,0:T(8,128)} %bitcast.5), custom_call_target="tpu_custom_call" | custom-call | flops 1000000000 | bytes 10000000 | tf_op jit(solution)/shard_map/listing/pallas_call | solution.py:109
  12.7 5.4 %incidence.1 = (bf16[33024,128]{1,0:T(8,128)(2,1)S(1)}, bf16[33024,128]{1,0:T(8,128)(2,1)S(1)}) custom-call(s32[3,144]{1,0:T(4,128)S(1)} %get-tuple-element.28.list_ref.refs_0_, s32[2]{0:T(128)S(1)} %get-tuple-element.29.total_ref.refs_1_, s32[8,2048]{1,0:T(8,128)} %refs_0_.3), custom_call_target="tpu_custom_call" | custom-call | flops 1000000 | bytes 20000000 | tf_op jit(solution)/shard_map/incidence/pallas_call | solution.py:164
  18.1 1.4 %collective-permute-start.5 = (f32[32,896]{1,0:T(8,128)S(1)}, f32[32,896]{1,0:T(8,128)S(1)}, u32[]{:S(2)}, u32[]{:S(2)}) collective-permute-start(f32[32,896]{1,0:T(8,128)S(1)} %collective-permute-done.4.refs_4_.refs_2_), channel_id=1, source_target_pairs={{0,4},{4,0},{8,12},{12,8},{1,5},{5,1},{9,13},{13,9},{2,6},{6,2},{1... | collective-permute-start | bytes 344072 | tf_op jit(solution)/shard_map/ppermute | solution.py:427
  19.5 1.6 %collective-permute-done.1.refs_4_ = f32[32,896]{1,0:T(8,128)S(1)} collective-permute-done((f32[32,896]{1,0:T(8,128)S(1)}, f32[32,896]{1,0:T(8,128)S(1)}, u32[]{:S(2)}, u32[]{:S(2)}) %collective-permute-start.1) | collective-permute-done | bytes 114720 | tf_op jit(solution)/shard_map/ppermute | solution.py:427
  21.1 4.1 %far_sweep.1 = (f32[32,2048]{1,0:T(8,128)S(1)}, f32[29,16,128]{2,1,0:T(8,128)S(1)}, f32[29,16,128]{2,1,0:T(8,128)S(1)}) custom-call(s32[3,144]{1,0:T(4,128)S(1)} %get-tuple-element.28.list_ref.refs_0_, s32[2]{0:T(128)S(1)} %get-tuple-element.29.total_ref.refs_1_, f32[32,896]{1,0:T(8,128)S(1)} %get-tuple-element.56.refs_2_, ...), custom_call_target="tpu_custom_call" | custom-call | flops 10000000000 | bytes 25000000 | tf_op jit(solution)/shard_map/far_sweep/pallas_call | solution.py:281
  25.2 2.3 %collective-permute-start.3 = (f32[29,16,128]{2,1,0:T(8,128)S(1)}, f32[29,16,128]{2,1,0:T(8,128)S(1)}, u32[]{:S(2)}, u32[]{:S(2)}) collective-permute-start(f32[29,16,128]{2,1,0:T(8,128)S(1)} %get-tuple-element.36), channel_id=1, source_target_pairs={{0,4},{4,0},{8,12},{12,8},{1,5},{5,1},{9,13},{13,9},{2,6},{6,2},{1... | collective-permute-start | bytes 712712 | tf_op jit(solution)/shard_map/ppermute | solution.py:427
  27.5 4.1 %near_sweep.1 = (f32[32,2048]{1,0:T(8,128)S(1)}, f32[29,16,128]{2,1,0:T(8,128)S(1)}, f32[29,16,128]{2,1,0:T(8,128)S(1)}) custom-call(s32[3,144]{1,0:T(4,128)S(1)} %get-tuple-element.28.list_ref.refs_0_, s32[2]{0:T(128)S(1)} %get-tuple-element.29.total_ref.refs_1_, f32[32,896]{1,0:T(8,128)S(1)} %get-tuple-element.55.refs_2_.refs_0_, ...), custom_call_target="tpu_custom_call" | custom-call | flops 10000000000 | bytes 25000000 | tf_op jit(solution)/shard_map/near_sweep/pallas_call | solution.py:281
  31.6 1.2 %collective-permute-done.3 = f32[29,16,128]{2,1,0:T(8,128)S(1)} collective-permute-done((f32[29,16,128]{2,1,0:T(8,128)S(1)}, f32[29,16,128]{2,1,0:T(8,128)S(1)}, u32[]{:S(2)}, u32[]{:S(2)}) %collective-permute-start.3) | collective-permute-done | bytes 237600 | tf_op jit(solution)/shard_map/ppermute | solution.py:427
  32.8 1.8 %collective-permute-start.6 = (f32[29,16,128]{2,1,0:T(8,128)S(1)}, f32[29,16,128]{2,1,0:T(8,128)S(1)}, u32[]{:S(2)}, u32[]{:S(2)}) collective-permute-start(f32[29,16,128]{2,1,0:T(8,128)S(1)} %get-tuple-element.44), channel_id=1, source_target_pairs={{0,4},{4,0},{8,12},{12,8},{1,5},{5,1},{9,13},{13,9},{2,6},{6,2},{1... | collective-permute-start | bytes 712712 | tf_op jit(solution)/shard_map/ppermute | solution.py:427
  34.6 1.1 %collective-permute-start.7 = (f32[29,16,128]{2,1,0:T(8,128)S(1)}, f32[29,16,128]{2,1,0:T(8,128)S(1)}, u32[]{:S(2)}, u32[]{:S(2)}) collective-permute-start(f32[29,16,128]{2,1,0:T(8,128)S(1)} %add.33), channel_id=1, source_target_pairs={{0,8},{4,12},{8,0},{12,4},{1,9},{5,13},{9,1},{13,5},{2,10},{6,14},... | collective-permute-start | bytes 712712 | tf_op jit(solution)/shard_map/ppermute | solution.py:427
  35.7 0.8 %pad_maximum_fusion = f32[64,2048]{1,0:T(8,128)} fusion(f32[32,2048]{1,0:T(8,128)S(1)} %get-tuple-element.54, f32[32,2048]{1,0:T(8,128)S(1)} %get-tuple-element.53), kind=kLoop, calls=%fused_computation | loop fusion | flops 131072 | bytes 1048576 | tf_op jit(solution)/shard_map/concatenate | solution.py:456
  36.6 5.5 %collective-permute-done.6.refs_7_ = f32[29,16,128]{2,1,0:T(8,128)S(1)} collective-permute-done((f32[29,16,128]{2,1,0:T(8,128)S(1)}, f32[29,16,128]{2,1,0:T(8,128)S(1)}, u32[]{:S(2)}, u32[]{:S(2)}) %collective-permute-start.6) | collective-permute-done | bytes 237600 | tf_op jit(solution)/shard_map/ppermute | solution.py:427
  42.1 4.3 %collective-permute-done.7.refs_8_ = f32[29,16,128]{2,1,0:T(8,128)S(1)} collective-permute-done((f32[29,16,128]{2,1,0:T(8,128)S(1)}, f32[29,16,128]{2,1,0:T(8,128)S(1)}, u32[]{:S(2)}, u32[]{:S(2)}) %collective-permute-start.7) | collective-permute-done | bytes 237600 | tf_op jit(solution)/shard_map/ppermute | solution.py:427
  46.7 1.2 %collective-permute-done.8 = f32[28,128]{1,0:T(8,128)S(1)} collective-permute-done((f32[28,128]{1,0:T(8,128)S(1)}, f32[28,128]{1,0:T(8,128)S(1)}, u32[]{:S(2)}, u32[]{:S(2)}) %collective-permute-start.8) | collective-permute-done | bytes 14368 | tf_op jit(solution)/shard_map/ppermute | solution.py:427
  47.9 1.5 %collective-permute-start.9 = (f32[28,128]{1,0:T(8,128)S(1)}, f32[28,128]{1,0:T(8,128)S(1)}, u32[]{:S(2)}, u32[]{:S(2)}) collective-permute-start(f32[28,128]{1,0:T(8,128)S(1)} %add.34), channel_id=1, source_target_pairs={{0,2},{2,0},{1,3},{3,1},{4,6},{6,4},{5,7},{7,5},{8,10},{10,8},{9,1... | collective-permute-start | bytes 43016 | tf_op jit(solution)/shard_map/ppermute | solution.py:427
  49.4 1.9 %collective-permute-start.13 = (f32[16,896]{1,0:T(8,128)S(1)}, f32[16,896]{1,0:T(8,128)S(1)}, u32[]{:S(2)}, u32[]{:S(2)}) collective-permute-start(f32[16,896]{1,0:T(8,128)S(1)} %get-tuple-element.49), channel_id=1, source_target_pairs={{0,8},{4,12},{8,0},{12,4},{1,9},{5,13},{9,1},{13,5},{2,10},{6,14},... | collective-permute-start | bytes 172040 | tf_op jit(solution)/shard_map/ppermute | solution.py:427
  51.3 2.5 %collective-permute-start.14 = (f32[16,896]{1,0:T(8,128)S(1)}, f32[16,896]{1,0:T(8,128)S(1)}, u32[]{:S(2)}, u32[]{:S(2)}) collective-permute-start(f32[16,896]{1,0:T(8,128)S(1)} %get-tuple-element.50), channel_id=1, source_target_pairs={{0,12},{4,8},{8,4},{12,0},{1,13},{5,9},{9,5},{13,1},{2,14},{6,10},... | collective-permute-start | bytes 172040 | tf_op jit(solution)/shard_map/ppermute | solution.py:427
  53.9 3.7 %collective-permute-done.10 = f32[28,128]{1,0:T(8,128)S(1)} collective-permute-done((f32[28,128]{1,0:T(8,128)S(1)}, f32[28,128]{1,0:T(8,128)S(1)}, u32[]{:S(2)}, u32[]{:S(2)}) %collective-permute-start.10) | collective-permute-done | bytes 14368 | tf_op jit(solution)/shard_map/ppermute | solution.py:427
  58.1 4.3 %collective-permute-done.11.refs_2_ = f32[28,128]{1,0:T(8,128)S(1)} collective-permute-done((f32[28,128]{1,0:T(8,128)S(1)}, f32[28,128]{1,0:T(8,128)S(1)}, u32[]{:S(2)}, u32[]{:S(2)}) %collective-permute-start.11) | collective-permute-done | bytes 14368 | tf_op jit(solution)/shard_map/ppermute | solution.py:427
  62.4 1.9 %robust.1 = f32[16,128]{1,0:T(8,128)} custom-call(s32[8,2048]{1,0:T(8,128)S(1)} %copy-done, f32[28,128]{1,0:T(8,128)S(1)} %add.36.refs_1_, f32[28,128]{1,0:T(8,128)S(1)} %collective-permute-done.11.refs_2_), custom_call_target="tpu_custom_call" | custom-call | flops 1000000 | bytes 1000000 | tf_op jit(solution)/shard_map/robust/pallas_call | solution.py:413
  (31 shorter events, 1.4 us)
Async XLA Ops:
  0.6 20.5 %collective-permute-start = (f32[64,896]{1,0:T(8,128)}, f32[64,896]{1,0:T(8,128)S(1)}, u32[]{:S(2)}, u32[]{:S(2)}) collective-permute-start(f32[64,896]{1,0:T(8,128)} %param.13), channel_id=1, source_target_pairs={{0,4},{4,0},{8,12},{12,8},{1,5},{5,1},{9,13},{13,9},{2,6},{6,2},{1... | collective-permute-start | bytes 688136 | tf_op jit(solution)/shard_map/ppermute | solution.py:427
  4.7 13.4 %collective-permute-start.4 = (f32[32,896]{1,0:T(8,128)S(1)}, f32[32,896]{1,0:T(8,128)S(1)}, u32[]{:S(2)}, u32[]{:S(2)}) collective-permute-start(f32[32,896]{1,0:T(8,128)S(1)} %get-tuple-element.56.refs_2_), channel_id=1, source_target_pairs={{0,8},{4,12},{8,0},{12,4},{1,9},{5,13},{9,1},{13,5},{2,10},{6,14},... | collective-permute-start | bytes 344072 | tf_op jit(solution)/shard_map/ppermute | solution.py:427
  7.4 13.7 %collective-permute-start.1 = (f32[32,896]{1,0:T(8,128)S(1)}, f32[32,896]{1,0:T(8,128)S(1)}, u32[]{:S(2)}, u32[]{:S(2)}) collective-permute-start(f32[32,896]{1,0:T(8,128)S(1)} %get-tuple-element.55.refs_2_.refs_0_), channel_id=1, source_target_pairs={{0,8},{4,12},{8,0},{12,4},{1,9},{5,13},{9,1},{13,5},{2,10},{6,14},... | collective-permute-start | bytes 344072 | tf_op jit(solution)/shard_map/ppermute | solution.py:427
  7.7 13.4 %collective-permute-start.2 = (f32[32,896]{1,0:T(8,128)S(1)}, f32[32,896]{1,0:T(8,128)S(1)}, u32[]{:S(2)}, u32[]{:S(2)}) collective-permute-start(f32[32,896]{1,0:T(8,128)S(1)} %get-tuple-element.55.refs_2_.refs_0_), channel_id=1, source_target_pairs={{0,12},{4,8},{8,4},{12,0},{1,13},{5,9},{9,5},{13,1},{2,14},{6,10},... | collective-permute-start | bytes 344072 | tf_op jit(solution)/shard_map/ppermute | solution.py:427
  18.1 9.4 %collective-permute-start.5 = (f32[32,896]{1,0:T(8,128)S(1)}, f32[32,896]{1,0:T(8,128)S(1)}, u32[]{:S(2)}, u32[]{:S(2)}) collective-permute-start(f32[32,896]{1,0:T(8,128)S(1)} %collective-permute-done.4.refs_4_.refs_2_), channel_id=1, source_target_pairs={{0,4},{4,0},{8,12},{12,8},{1,5},{5,1},{9,13},{13,9},{2,6},{6,2},{1... | collective-permute-start | bytes 344072 | tf_op jit(solution)/shard_map/ppermute | solution.py:427
  25.2 11.3 %copy-start.2 = (f32[64]{0:T(128)S(1)}, f32[64]{0:T(128)}, u32[]{:S(2)}) copy-start(f32[64]{0:T(128)} %param.15) | copy-start | bytes 772
  25.2 37.2 %copy-start = (s32[8,2048]{1,0:T(8,128)S(1)}, s32[8,2048]{1,0:T(8,128)}, u32[]{:S(2)}) copy-start(s32[8,2048]{1,0:T(8,128)} %refs_0_.3) | copy-start | bytes 196612
  25.2 7.5 %collective-permute-start.3 = (f32[29,16,128]{2,1,0:T(8,128)S(1)}, f32[29,16,128]{2,1,0:T(8,128)S(1)}, u32[]{:S(2)}, u32[]{:S(2)}) collective-permute-start(f32[29,16,128]{2,1,0:T(8,128)S(1)} %get-tuple-element.36), channel_id=1, source_target_pairs={{0,4},{4,0},{8,12},{12,8},{1,5},{5,1},{9,13},{13,9},{2,6},{6,2},{1... | collective-permute-start | bytes 712712 | tf_op jit(solution)/shard_map/ppermute | solution.py:427
  32.8 9.3 %collective-permute-start.6 = (f32[29,16,128]{2,1,0:T(8,128)S(1)}, f32[29,16,128]{2,1,0:T(8,128)S(1)}, u32[]{:S(2)}, u32[]{:S(2)}) collective-permute-start(f32[29,16,128]{2,1,0:T(8,128)S(1)} %get-tuple-element.44), channel_id=1, source_target_pairs={{0,4},{4,0},{8,12},{12,8},{1,5},{5,1},{9,13},{13,9},{2,6},{6,2},{1... | collective-permute-start | bytes 712712 | tf_op jit(solution)/shard_map/ppermute | solution.py:427
  34.6 11.8 %collective-permute-start.7 = (f32[29,16,128]{2,1,0:T(8,128)S(1)}, f32[29,16,128]{2,1,0:T(8,128)S(1)}, u32[]{:S(2)}, u32[]{:S(2)}) collective-permute-start(f32[29,16,128]{2,1,0:T(8,128)S(1)} %add.33), channel_id=1, source_target_pairs={{0,8},{4,12},{8,0},{12,4},{1,9},{5,13},{9,1},{13,5},{2,10},{6,14},... | collective-permute-start | bytes 712712 | tf_op jit(solution)/shard_map/ppermute | solution.py:427
  46.6 1.2 %collective-permute-start.8 = (f32[28,128]{1,0:T(8,128)S(1)}, f32[28,128]{1,0:T(8,128)S(1)}, u32[]{:S(2)}, u32[]{:S(2)}) collective-permute-start(f32[28,128]{1,0:T(8,128)S(1)} %get-tuple-element.46), channel_id=1, source_target_pairs={{0,1},{1,0},{2,3},{3,2},{4,5},{5,4},{6,7},{7,6},{8,9},{9,8},{10,11... | collective-permute-start | bytes 43016 | tf_op jit(solution)/shard_map/ppermute | solution.py:427
  47.9 5.9 %collective-permute-start.9 = (f32[28,128]{1,0:T(8,128)S(1)}, f32[28,128]{1,0:T(8,128)S(1)}, u32[]{:S(2)}, u32[]{:S(2)}) collective-permute-start(f32[28,128]{1,0:T(8,128)S(1)} %add.34), channel_id=1, source_target_pairs={{0,2},{2,0},{1,3},{3,1},{4,6},{6,4},{5,7},{7,5},{8,10},{10,8},{9,1... | collective-permute-start | bytes 43016 | tf_op jit(solution)/shard_map/ppermute | solution.py:427
  49.4 8.7 %collective-permute-start.12 = (f32[16,896]{1,0:T(8,128)S(1)}, f32[16,896]{1,0:T(8,128)S(1)}, u32[]{:S(2)}, u32[]{:S(2)}) collective-permute-start(f32[16,896]{1,0:T(8,128)S(1)} %get-tuple-element.48), channel_id=1, source_target_pairs={{0,4},{4,0},{8,12},{12,8},{1,5},{5,1},{9,13},{13,9},{2,6},{6,2},{1... | collective-permute-start | bytes 172040 | tf_op jit(solution)/shard_map/ppermute | solution.py:427
  49.4 8.7 %collective-permute-start.13 = (f32[16,896]{1,0:T(8,128)S(1)}, f32[16,896]{1,0:T(8,128)S(1)}, u32[]{:S(2)}, u32[]{:S(2)}) collective-permute-start(f32[16,896]{1,0:T(8,128)S(1)} %get-tuple-element.49), channel_id=1, source_target_pairs={{0,8},{4,12},{8,0},{12,4},{1,9},{5,13},{9,1},{13,5},{2,10},{6,14},... | collective-permute-start | bytes 172040 | tf_op jit(solution)/shard_map/ppermute | solution.py:427
  51.3 6.8 %collective-permute-start.14 = (f32[16,896]{1,0:T(8,128)S(1)}, f32[16,896]{1,0:T(8,128)S(1)}, u32[]{:S(2)}, u32[]{:S(2)}) collective-permute-start(f32[16,896]{1,0:T(8,128)S(1)} %get-tuple-element.50), channel_id=1, source_target_pairs={{0,12},{4,8},{8,4},{12,0},{1,13},{5,9},{9,5},{13,1},{2,14},{6,10},... | collective-permute-start | bytes 172040 | tf_op jit(solution)/shard_map/ppermute | solution.py:427
  53.8 3.8 %collective-permute-start.10 = (f32[28,128]{1,0:T(8,128)S(1)}, f32[28,128]{1,0:T(8,128)S(1)}, u32[]{:S(2)}, u32[]{:S(2)}) collective-permute-start(f32[28,128]{1,0:T(8,128)S(1)} %add.35), channel_id=1, source_target_pairs={{0,4},{4,0},{8,12},{12,8},{1,5},{5,1},{9,13},{13,9},{2,6},{6,2},{1... | collective-permute-start | bytes 43016 | tf_op jit(solution)/shard_map/ppermute | solution.py:427
  57.6 4.8 %collective-permute-start.11 = (f32[28,128]{1,0:T(8,128)S(1)}, f32[28,128]{1,0:T(8,128)S(1)}, u32[]{:S(2)}, u32[]{:S(2)}) collective-permute-start(f32[28,128]{1,0:T(8,128)S(1)} %add.36.refs_1_), channel_id=1, source_target_pairs={{0,8},{4,12},{8,0},{12,4},{1,9},{5,13},{9,1},{13,5},{2,10},{6,14},... | collective-permute-start | bytes 43016 | tf_op jit(solution)/shard_map/ppermute | solution.py:427
  58.1 6.2 %copy-start.1 = (f32[64,896]{1,0:T(8,128)}, f32[64,896]{1,0:T(8,128)S(1)}, u32[]{:S(2)}) copy-start(f32[64,896]{1,0:T(8,128)S(1)} %constant_dynamic-update-slice_fusion) | copy-start | bytes 688132

commit v5 on v4

--- a/solution.py
+++ b/solution.py
@@ -439,13 +439,14 @@
     def swap(x, m):
         return exchange(x, "path", n, m)
 
-    shared = swap(lengths, 1)
-    far_pieces = [far, shared, swap(near, 2), swap(near, 3)]
+    near_straight, near_crossed = swap(near, 2), swap(near, 3)
     pairs, total, same, wanted, capacity_tiles = build_listing(
         n * own // LB, block_tiles, block_count, path_commodity, demand, capacity
     )
-    straight_rows = swap(far, 2)
-    near_pieces = [near, shared, straight_rows, swap(straight_rows, 1)]
+    late, same = lax.optimization_barrier((far, same))
+    shared = swap(lengths, 1)
+    far_pieces = [far, shared, near_straight, near_crossed]
+    near_pieces = [near, shared, swap(late, 2), swap(late, 3)]
     built = (*build_incidence(path_links, pairs, total), pairs, total, same, wanted)
     far_flows, straight, crossed = half_sweep(far_pieces, half, built, capacity_tiles, True)
     partial = straight + swap(crossed, 1)

time: 64.5 us -> 62.9 us (0.975)
  waiting for transfers between devices: 21.7 us -> 11.2 us
  starting transfers between devices: 21.5 us -> 30.1 us
    ppermute x15, waiting for transfers between devices: 21.7 us -> 11.2 us  [exchange(): return lax.ppermute(x, axis, [(i, i ^ bit) for i in range(n)])]
    ppermute x15, starting transfers between devices: 21.5 us -> 30.1 us  [exchange(): return lax.ppermute(x, axis, [(i, i ^ bit) for i in range(n)])]
  transfers between devices with their start and end apart: 15 -> 15, of which waited for: 7 -> 5; matrix products, arithmetic and copies ran while one was open for 3% -> 3% of each run, Pallas kernels for 25% -> 26%
where the time goes in v5:
time: 62.9 us; the launch traced here: 62.4 us
  starting transfers between devices  30.1 us (48%)
  Pallas kernels  18.2 us (29%)
  waiting for transfers between devices  11.2 us (18%)
  local copies, waits for them, and re-layouts  1.16 us (2%)
  other arithmetic  0.91 us (1%)
  between operations  0.8 us (1%)
    ppermute x15, starting transfers between devices, exchange(): return lax.ppermute(x, axis, [(i, i ^ bit) for i in range(n)])  30.1 us
    ppermute x15, waiting for transfers between devices, exchange(): return lax.ppermute(x, axis, [(i, i ^ bit) for i in range(n)])  11.2 us
    pallas_call x2, Pallas kernels, half_sweep(): pl.pallas_call(lambda *refs: half_kernel(far, n, *refs), in_specs=[SCALAR...  8.15 us
    pallas_call x1, Pallas kernels, build_incidence(): pl.pallas_call(incidence_kernel, in_specs=[SCALARS, SCALARS, REMAIN], out...  5.4 us
    pallas_call x1, Pallas kernels, build_listing(): pl.pallas_call(lambda *refs: listing_kernel(tile_total, *refs), in_specs=...  2.49 us
    pallas_call x1, Pallas kernels, robust_costs(): pl.pallas_call(lambda *refs: robust_kernel(len(parts), *refs), in_specs=[...  1.93 us
  transfers between devices with their start and end apart: 15, of which 5 were waited for; matrix products, arithmetic and copies ran while one was open for 3% of the time, Pallas kernels for 26%

profile of v5, /device:TPU:0, one launch (start us, length us, event | category | flops | bytes accessed | tf_op | source)
XLA Modules:
  0.0 62.4 jit_solution(9572519491487076159)
XLA Ops:
  0.6 3.1 %collective-permute-start = (f32[64,896]{1,0:T(8,128)}, f32[64,896]{1,0:T(8,128)S(1)}, u32[]{:S(2)}, u32[]{:S(2)}) collective-permute-start(f32[64,896]{1,0:T(8,128)} %param.13), channel_id=1, source_target_pairs={{0,4},{4,0},{8,12},{12,8},{1,5},{5,1},{9,13},{13,9},{2,6},{6,2},{1... | collective-permute-start | bytes 688136 | tf_op jit(solution)/shard_map/ppermute | solution.py:427
  3.7 1.0 %constant_dynamic-slice_fusion = (f32[32,896]{1,0:T(8,128)S(1)}, f32[32,896]{1,0:T(8,128)S(1)}) fusion(f32[64,896]{1,0:T(8,128)} %param.13, s32[]{:T(128)S(6)} %select_n.38, s32[]{:T(128)S(6)} %select_n.37), kind=kLoop, calls=%fused_computation.7 | loop fusion | bytes 458760 | tf_op jit(solution)/shard_map/dynamic_slice | solution.py:437
  4.7 2.7 %collective-permute-start.1 = (f32[32,896]{1,0:T(8,128)S(1)}, f32[32,896]{1,0:T(8,128)S(1)}, u32[]{:S(2)}, u32[]{:S(2)}) collective-permute-start(f32[32,896]{1,0:T(8,128)S(1)} %get-tuple-element.59.refs_2_.refs_0_), channel_id=1, source_target_pairs={{0,8},{4,12},{8,0},{12,4},{1,9},{5,13},{9,1},{13,5},{2,10},{6,14},... | collective-permute-start | bytes 344072 | tf_op jit(solution)/shard_map/ppermute | solution.py:427
  7.4 2.5 %listing.1 = (s32[3,144]{1,0:T(4,128)S(1)}, s32[2]{0:T(128)S(1)}, bf16[16,128,128]{2,1,0:T(8,128)(2,1)S(1)}, f32[16,64,128]{2,1,0:T(8,128)S(1)}, f32[7,128]{1,0:T(8,128)S(1)}) custom-call(s32[16,16]{1,0:T(8,128)} %refs_0_.2, s32[16]{0:T(128)} %refs_1_.1, s32[16,128]{1,0:T(8,128)} %refs_2_.1, s32[64,512]{1,0:T(8,128)} %refs_3_.1, f32[7,128]{1,0:T(8,128)} %bitcast.5), custom_call_target="tpu_custom_call" | custom-call | flops 1000000000 | bytes 10000000 | tf_op jit(solution)/shard_map/listing/pallas_call | solution.py:109
  9.9 2.0 %collective-permute-start.4 = (f32[32,896]{1,0:T(8,128)S(1)}, f32[32,896]{1,0:T(8,128)S(1)}, u32[]{:S(2)}, u32[]{:S(2)}) collective-permute-start(f32[32,896]{1,0:T(8,128)S(1)} %get-tuple-element.40.refs_2_), channel_id=1, source_target_pairs={{0,8},{4,12},{8,0},{12,4},{1,9},{5,13},{9,1},{13,5},{2,10},{6,14},... | collective-permute-start | bytes 344072 | tf_op jit(solution)/shard_map/ppermute | solution.py:427
  11.9 2.2 %collective-permute-start.5 = (f32[32,896]{1,0:T(8,128)S(1)}, f32[32,896]{1,0:T(8,128)S(1)}, u32[]{:S(2)}, u32[]{:S(2)}) collective-permute-start(f32[32,896]{1,0:T(8,128)S(1)} %get-tuple-element.40.refs_2_), channel_id=1, source_target_pairs={{0,12},{4,8},{8,4},{12,0},{1,13},{5,9},{9,5},{13,1},{2,14},{6,10},... | collective-permute-start | bytes 344072 | tf_op jit(solution)/shard_map/ppermute | solution.py:427
  14.0 5.4 %incidence.1 = (bf16[33024,128]{1,0:T(8,128)(2,1)S(1)}, bf16[33024,128]{1,0:T(8,128)(2,1)S(1)}) custom-call(s32[3,144]{1,0:T(4,128)S(1)} %get-tuple-element.30.list_ref.refs_0_, s32[2]{0:T(128)S(1)} %get-tuple-element.31.total_ref.refs_1_, s32[8,2048]{1,0:T(8,128)} %refs_0_.3), custom_call_target="tpu_custom_call" | custom-call | flops 1000000 | bytes 20000000 | tf_op jit(solution)/shard_map/incidence/pallas_call | solution.py:164
  19.5 4.1 %far_sweep.1 = (f32[32,2048]{1,0:T(8,128)S(1)}, f32[29,16,128]{2,1,0:T(8,128)S(1)}, f32[29,16,128]{2,1,0:T(8,128)S(1)}) custom-call(s32[3,144]{1,0:T(4,128)S(1)} %get-tuple-element.30.list_ref.refs_0_, s32[2]{0:T(128)S(1)} %get-tuple-element.31.total_ref.refs_1_, f32[32,896]{1,0:T(8,128)S(1)} %get-tuple-element.40.refs_2_, ...), custom_call_target="tpu_custom_call" | custom-call | flops 10000000000 | bytes 25000000 | tf_op jit(solution)/shard_map/far_sweep/pallas_call | solution.py:281
  23.6 5.6 %collective-permute-start.3 = (f32[29,16,128]{2,1,0:T(8,128)S(1)}, f32[29,16,128]{2,1,0:T(8,128)S(1)}, u32[]{:S(2)}, u32[]{:S(2)}) collective-permute-start(f32[29,16,128]{2,1,0:T(8,128)S(1)} %get-tuple-element.39), channel_id=1, source_target_pairs={{0,4},{4,0},{8,12},{12,8},{1,5},{5,1},{9,13},{13,9},{2,6},{6,2},{1... | collective-permute-start | bytes 712712 | tf_op jit(solution)/shard_map/ppermute | solution.py:427
  29.2 4.1 %near_sweep.1 = (f32[32,2048]{1,0:T(8,128)S(1)}, f32[29,16,128]{2,1,0:T(8,128)S(1)}, f32[29,16,128]{2,1,0:T(8,128)S(1)}) custom-call(s32[3,144]{1,0:T(4,128)S(1)} %get-tuple-element.30.list_ref.refs_0_, s32[2]{0:T(128)S(1)} %get-tuple-element.31.total_ref.refs_1_, f32[32,896]{1,0:T(8,128)S(1)} %get-tuple-element.59.refs_2_.refs_0_, ...), custom_call_target="tpu_custom_call" | custom-call | flops 10000000000 | bytes 25000000 | tf_op jit(solution)/shard_map/near_sweep/pallas_call | solution.py:281
  33.3 0.3 collective-permute-done.3
  33.6 2.4 %collective-permute-start.6 = (f32[29,16,128]{2,1,0:T(8,128)S(1)}, f32[29,16,128]{2,1,0:T(8,128)S(1)}, u32[]{:S(2)}, u32[]{:S(2)}) collective-permute-start(f32[29,16,128]{2,1,0:T(8,128)S(1)} %get-tuple-element.48), channel_id=1, source_target_pairs={{0,4},{4,0},{8,12},{12,8},{1,5},{5,1},{9,13},{13,9},{2,6},{6,2},{1... | collective-permute-start | bytes 712712 | tf_op jit(solution)/shard_map/ppermute | solution.py:427
  36.0 1.5 %collective-permute-start.7 = (f32[29,16,128]{2,1,0:T(8,128)S(1)}, f32[29,16,128]{2,1,0:T(8,128)S(1)}, u32[]{:S(2)}, u32[]{:S(2)}) collective-permute-start(f32[29,16,128]{2,1,0:T(8,128)S(1)} %add.33), channel_id=1, source_target_pairs={{0,8},{4,12},{8,0},{12,4},{1,9},{5,13},{9,1},{13,5},{2,10},{6,14},... | collective-permute-start | bytes 712712 | tf_op jit(solution)/shard_map/ppermute | solution.py:427
  37.6 0.8 %pad_maximum_fusion = f32[64,2048]{1,0:T(8,128)} fusion(f32[32,2048]{1,0:T(8,128)S(1)} %get-tuple-element.58, f32[32,2048]{1,0:T(8,128)S(1)} %get-tuple-element.57), kind=kLoop, calls=%fused_computation | loop fusion | flops 131072 | bytes 1048576 | tf_op jit(solution)/shard_map/concatenate | solution.py:457
  38.5 5.0 %collective-permute-done.6.refs_7_ = f32[29,16,128]{2,1,0:T(8,128)S(1)} collective-permute-done((f32[29,16,128]{2,1,0:T(8,128)S(1)}, f32[29,16,128]{2,1,0:T(8,128)S(1)}, u32[]{:S(2)}, u32[]{:S(2)}) %collective-permute-start.6) | collective-permute-done | bytes 237600 | tf_op jit(solution)/shard_map/ppermute | solution.py:427
  43.8 1.2 %collective-permute-done.8 = f32[28,128]{1,0:T(8,128)S(1)} collective-permute-done((f32[28,128]{1,0:T(8,128)S(1)}, f32[28,128]{1,0:T(8,128)S(1)}, u32[]{:S(2)}, u32[]{:S(2)}) %collective-permute-start.8) | collective-permute-done | bytes 14368 | tf_op jit(solution)/shard_map/ppermute | solution.py:427
  45.0 1.5 %collective-permute-start.9 = (f32[28,128]{1,0:T(8,128)S(1)}, f32[28,128]{1,0:T(8,128)S(1)}, u32[]{:S(2)}, u32[]{:S(2)}) collective-permute-start(f32[28,128]{1,0:T(8,128)S(1)} %add.34), channel_id=1, source_target_pairs={{0,2},{2,0},{1,3},{3,1},{4,6},{6,4},{5,7},{7,5},{8,10},{10,8},{9,1... | collective-permute-start | bytes 43016 | tf_op jit(solution)/shard_map/ppermute | solution.py:427
  46.4 2.7 %collective-permute-start.12 = (f32[16,896]{1,0:T(8,128)S(1)}, f32[16,896]{1,0:T(8,128)S(1)}, u32[]{:S(2)}, u32[]{:S(2)}) collective-permute-start(f32[16,896]{1,0:T(8,128)S(1)} %get-tuple-element.52), channel_id=1, source_target_pairs={{0,4},{4,0},{8,12},{12,8},{1,5},{5,1},{9,13},{13,9},{2,6},{6,2},{1... | collective-permute-start | bytes 172040 | tf_op jit(solution)/shard_map/ppermute | solution.py:427
  49.1 2.9 %collective-permute-start.13 = (f32[16,896]{1,0:T(8,128)S(1)}, f32[16,896]{1,0:T(8,128)S(1)}, u32[]{:S(2)}, u32[]{:S(2)}) collective-permute-start(f32[16,896]{1,0:T(8,128)S(1)} %get-tuple-element.53), channel_id=1, source_target_pairs={{0,8},{4,12},{8,0},{12,4},{1,9},{5,13},{9,1},{13,5},{2,10},{6,14},... | collective-permute-start | bytes 172040 | tf_op jit(solution)/shard_map/ppermute | solution.py:427
  52.0 0.7 %collective-permute-start.10 = (f32[28,128]{1,0:T(8,128)S(1)}, f32[28,128]{1,0:T(8,128)S(1)}, u32[]{:S(2)}, u32[]{:S(2)}) collective-permute-start(f32[28,128]{1,0:T(8,128)S(1)} %add.35), channel_id=1, source_target_pairs={{0,4},{4,0},{8,12},{12,8},{1,5},{5,1},{9,13},{13,9},{2,6},{6,2},{1... | collective-permute-start | bytes 43016 | tf_op jit(solution)/shard_map/ppermute | solution.py:427
  52.7 3.1 %collective-permute-done.10 = f32[28,128]{1,0:T(8,128)S(1)} collective-permute-done((f32[28,128]{1,0:T(8,128)S(1)}, f32[28,128]{1,0:T(8,128)S(1)}, u32[]{:S(2)}, u32[]{:S(2)}) %collective-permute-start.10) | collective-permute-done | bytes 14368 | tf_op jit(solution)/shard_map/ppermute | solution.py:427
  55.8 2.9 %collective-permute-start.11 = (f32[28,128]{1,0:T(8,128)S(1)}, f32[28,128]{1,0:T(8,128)S(1)}, u32[]{:S(2)}, u32[]{:S(2)}) collective-permute-start(f32[28,128]{1,0:T(8,128)S(1)} %add.36.refs_1_), channel_id=1, source_target_pairs={{0,8},{4,12},{8,0},{12,4},{1,9},{5,13},{9,1},{13,5},{2,10},{6,14},... | collective-permute-start | bytes 43016 | tf_op jit(solution)/shard_map/ppermute | solution.py:427
  58.8 1.7 %collective-permute-done.11.refs_2_ = f32[28,128]{1,0:T(8,128)S(1)} collective-permute-done((f32[28,128]{1,0:T(8,128)S(1)}, f32[28,128]{1,0:T(8,128)S(1)}, u32[]{:S(2)}, u32[]{:S(2)}) %collective-permute-start.11) | collective-permute-done | bytes 14368 | tf_op jit(solution)/shard_map/ppermute | solution.py:427
  60.5 1.9 %robust.1 = f32[16,128]{1,0:T(8,128)} custom-call(s32[8,2048]{1,0:T(8,128)S(1)} %copy-done, f32[28,128]{1,0:T(8,128)S(1)} %add.36.refs_1_, f32[28,128]{1,0:T(8,128)S(1)} %collective-permute-done.11.refs_2_), custom_call_target="tpu_custom_call" | custom-call | flops 1000000 | bytes 1000000 | tf_op jit(solution)/shard_map/robust/pallas_call | solution.py:413
  (31 shorter events, 0.6 us)
Async XLA Ops:
  0.6 18.8 %collective-permute-start = (f32[64,896]{1,0:T(8,128)}, f32[64,896]{1,0:T(8,128)S(1)}, u32[]{:S(2)}, u32[]{:S(2)}) collective-permute-start(f32[64,896]{1,0:T(8,128)} %param.13), channel_id=1, source_target_pairs={{0,4},{4,0},{8,12},{12,8},{1,5},{5,1},{9,13},{13,9},{2,6},{6,2},{1... | collective-permute-start | bytes 688136 | tf_op jit(solution)/shard_map/ppermute | solution.py:427
  4.7 14.7 %collective-permute-start.1 = (f32[32,896]{1,0:T(8,128)S(1)}, f32[32,896]{1,0:T(8,128)S(1)}, u32[]{:S(2)}, u32[]{:S(2)}) collective-permute-start(f32[32,896]{1,0:T(8,128)S(1)} %get-tuple-element.59.refs_2_.refs_0_), channel_id=1, source_target_pairs={{0,8},{4,12},{8,0},{12,4},{1,9},{5,13},{9,1},{13,5},{2,10},{6,14},... | collective-permute-start | bytes 344072 | tf_op jit(solution)/shard_map/ppermute | solution.py:427
  7.4 12.1 %collective-permute-start.2 = (f32[32,896]{1,0:T(8,128)S(1)}, f32[32,896]{1,0:T(8,128)S(1)}, u32[]{:S(2)}, u32[]{:S(2)}) collective-permute-start(f32[32,896]{1,0:T(8,128)S(1)} %get-tuple-element.59.refs_2_.refs_0_), channel_id=1, source_target_pairs={{0,12},{4,8},{8,4},{12,0},{1,13},{5,9},{9,5},{13,1},{2,14},{6,10},... | collective-permute-start | bytes 344072 | tf_op jit(solution)/shard_map/ppermute | solution.py:427
  9.9 19.3 %collective-permute-start.4 = (f32[32,896]{1,0:T(8,128)S(1)}, f32[32,896]{1,0:T(8,128)S(1)}, u32[]{:S(2)}, u32[]{:S(2)}) collective-permute-start(f32[32,896]{1,0:T(8,128)S(1)} %get-tuple-element.40.refs_2_), channel_id=1, source_target_pairs={{0,8},{4,12},{8,0},{12,4},{1,9},{5,13},{9,1},{13,5},{2,10},{6,14},... | collective-permute-start | bytes 344072 | tf_op jit(solution)/shard_map/ppermute | solution.py:427
  11.9 17.3 %collective-permute-start.5 = (f32[32,896]{1,0:T(8,128)S(1)}, f32[32,896]{1,0:T(8,128)S(1)}, u32[]{:S(2)}, u32[]{:S(2)}) collective-permute-start(f32[32,896]{1,0:T(8,128)S(1)} %get-tuple-element.40.refs_2_), channel_id=1, source_target_pairs={{0,12},{4,8},{8,4},{12,0},{1,13},{5,9},{9,5},{13,1},{2,14},{6,10},... | collective-permute-start | bytes 344072 | tf_op jit(solution)/shard_map/ppermute | solution.py:427
  23.6 14.8 %copy-start.2 = (f32[64]{0:T(128)S(1)}, f32[64]{0:T(128)}, u32[]{:S(2)}) copy-start(f32[64]{0:T(128)} %param.15) | copy-start | bytes 772
  23.6 36.9 %copy-start = (s32[8,2048]{1,0:T(8,128)S(1)}, s32[8,2048]{1,0:T(8,128)}, u32[]{:S(2)}) copy-start(s32[8,2048]{1,0:T(8,128)} %refs_0_.3) | copy-start | bytes 196612
  23.6 10.0 %collective-permute-start.3 = (f32[29,16,128]{2,1,0:T(8,128)S(1)}, f32[29,16,128]{2,1,0:T(8,128)S(1)}, u32[]{:S(2)}, u32[]{:S(2)}) collective-permute-start(f32[29,16,128]{2,1,0:T(8,128)S(1)} %get-tuple-element.39), channel_id=1, source_target_pairs={{0,4},{4,0},{8,12},{12,8},{1,5},{5,1},{9,13},{13,9},{2,6},{6,2},{1... | collective-permute-start | bytes 712712 | tf_op jit(solution)/shard_map/ppermute | solution.py:427
  33.6 9.8 %collective-permute-start.6 = (f32[29,16,128]{2,1,0:T(8,128)S(1)}, f32[29,16,128]{2,1,0:T(8,128)S(1)}, u32[]{:S(2)}, u32[]{:S(2)}) collective-permute-start(f32[29,16,128]{2,1,0:T(8,128)S(1)} %get-tuple-element.48), channel_id=1, source_target_pairs={{0,4},{4,0},{8,12},{12,8},{1,5},{5,1},{9,13},{13,9},{2,6},{6,2},{1... | collective-permute-start | bytes 712712 | tf_op jit(solution)/shard_map/ppermute | solution.py:427
  36.0 7.5 %collective-permute-start.7 = (f32[29,16,128]{2,1,0:T(8,128)S(1)}, f32[29,16,128]{2,1,0:T(8,128)S(1)}, u32[]{:S(2)}, u32[]{:S(2)}) collective-permute-start(f32[29,16,128]{2,1,0:T(8,128)S(1)} %add.33), channel_id=1, source_target_pairs={{0,8},{4,12},{8,0},{12,4},{1,9},{5,13},{9,1},{13,5},{2,10},{6,14},... | collective-permute-start | bytes 712712 | tf_op jit(solution)/shard_map/ppermute | solution.py:427
  43.7 1.2 %collective-permute-start.8 = (f32[28,128]{1,0:T(8,128)S(1)}, f32[28,128]{1,0:T(8,128)S(1)}, u32[]{:S(2)}, u32[]{:S(2)}) collective-permute-start(f32[28,128]{1,0:T(8,128)S(1)} %get-tuple-element.50), channel_id=1, source_target_pairs={{0,1},{1,0},{2,3},{3,2},{4,5},{5,4},{6,7},{7,6},{8,9},{9,8},{10,11... | collective-permute-start | bytes 43016 | tf_op jit(solution)/shard_map/ppermute | solution.py:427
  45.0 7.1 %collective-permute-start.9 = (f32[28,128]{1,0:T(8,128)S(1)}, f32[28,128]{1,0:T(8,128)S(1)}, u32[]{:S(2)}, u32[]{:S(2)}) collective-permute-start(f32[28,128]{1,0:T(8,128)S(1)} %add.34), channel_id=1, source_target_pairs={{0,2},{2,0},{1,3},{3,1},{4,6},{6,4},{5,7},{7,5},{8,10},{10,8},{9,1... | collective-permute-start | bytes 43016 | tf_op jit(solution)/shard_map/ppermute | solution.py:427
  46.4 12.3 %collective-permute-start.12 = (f32[16,896]{1,0:T(8,128)S(1)}, f32[16,896]{1,0:T(8,128)S(1)}, u32[]{:S(2)}, u32[]{:S(2)}) collective-permute-start(f32[16,896]{1,0:T(8,128)S(1)} %get-tuple-element.52), channel_id=1, source_target_pairs={{0,4},{4,0},{8,12},{12,8},{1,5},{5,1},{9,13},{13,9},{2,6},{6,2},{1... | collective-permute-start | bytes 172040 | tf_op jit(solution)/shard_map/ppermute | solution.py:427
  49.1 9.6 %collective-permute-start.13 = (f32[16,896]{1,0:T(8,128)S(1)}, f32[16,896]{1,0:T(8,128)S(1)}, u32[]{:S(2)}, u32[]{:S(2)}) collective-permute-start(f32[16,896]{1,0:T(8,128)S(1)} %get-tuple-element.53), channel_id=1, source_target_pairs={{0,8},{4,12},{8,0},{12,4},{1,9},{5,13},{9,1},{13,5},{2,10},{6,14},... | collective-permute-start | bytes 172040 | tf_op jit(solution)/shard_map/ppermute | solution.py:427
  52.0 6.8 %collective-permute-start.14 = (f32[16,896]{1,0:T(8,128)S(1)}, f32[16,896]{1,0:T(8,128)S(1)}, u32[]{:S(2)}, u32[]{:S(2)}) collective-permute-start(f32[16,896]{1,0:T(8,128)S(1)} %get-tuple-element.54), channel_id=1, source_target_pairs={{0,12},{4,8},{8,4},{12,0},{1,13},{5,9},{9,5},{13,1},{2,14},{6,10},... | collective-permute-start | bytes 172040 | tf_op jit(solution)/shard_map/ppermute | solution.py:427
  52.0 3.8 %collective-permute-start.10 = (f32[28,128]{1,0:T(8,128)S(1)}, f32[28,128]{1,0:T(8,128)S(1)}, u32[]{:S(2)}, u32[]{:S(2)}) collective-permute-start(f32[28,128]{1,0:T(8,128)S(1)} %add.35), channel_id=1, source_target_pairs={{0,4},{4,0},{8,12},{12,8},{1,5},{5,1},{9,13},{13,9},{2,6},{6,2},{1... | collective-permute-start | bytes 43016 | tf_op jit(solution)/shard_map/ppermute | solution.py:427
  55.8 4.6 %collective-permute-start.11 = (f32[28,128]{1,0:T(8,128)S(1)}, f32[28,128]{1,0:T(8,128)S(1)}, u32[]{:S(2)}, u32[]{:S(2)}) collective-permute-start(f32[28,128]{1,0:T(8,128)S(1)} %add.36.refs_1_), channel_id=1, source_target_pairs={{0,8},{4,12},{8,0},{12,4},{1,9},{5,13},{9,1},{13,5},{2,10},{6,14},... | collective-permute-start | bytes 43016 | tf_op jit(solution)/shard_map/ppermute | solution.py:427
  58.8 3.6 %copy-start.1 = (f32[64,896]{1,0:T(8,128)}, f32[64,896]{1,0:T(8,128)S(1)}, u32[]{:S(2)}) copy-start(f32[64,896]{1,0:T(8,128)S(1)} %constant_dynamic-update-slice_fusion) | copy-start | bytes 688132

commit v6 on v5

--- a/solution.py
+++ b/solution.py
@@ -459,8 +459,9 @@
     flows, weight_column = lax.optimization_barrier((flows, weight_column))
     *new, mixed = grow(loads, near_pieces, capacity_tiles, weight_column)
     mixed = mixed + exchange(mixed, "sub", 2, 1)
-    mixed = mixed + exchange(mixed, "scen", 2, 1)
-    mixed = mixed + swap(mixed, 1)
+    mixed, *new[1:] = lax.optimization_barrier((mixed, *new[1:]))
+    diagonal = exchange(mixed, ("path", "scen"), 2 * n, 3)
+    mixed = mixed + exchange(mixed, "scen", 2, 1) + swap(mixed, 1) + diagonal
     parts = [mixed, swap(mixed, 2)]
     arrived = [new[0]] + [swap(new[m], m) for m in range(1, n)]
     lengths_next = jnp.zeros((rows, own), F32)

time: 62.9 us -> 63.1 us (level)
  starting transfers between devices: 30.1 us -> 31.5 us
  waiting for transfers between devices: 11.2 us -> 10.3 us
    ppermute x15 -> x16, starting transfers between devices: 30.1 us -> 31.5 us  [exchange(): return lax.ppermute(x, axis, [(i, i ^ bit) for i in range(n)])]
    ppermute x15 -> x16, waiting for transfers between devices: 11.2 us -> 10.3 us  [exchange(): return lax.ppermute(x, axis, [(i, i ^ bit) for i in range(n)])]
  transfers between devices with their start and end apart: 15 -> 16, of which waited for: 5 -> 6; matrix products, arithmetic and copies ran while one was open for 3% -> 3% of each run, Pallas kernels for 26% -> 26%
where the time goes in v6:
time: 63.1 us; the launch traced here: 62.8 us
  starting transfers between devices  31.5 us (50%)
  Pallas kernels  18.2 us (29%)
  waiting for transfers between devices  10.3 us (16%)
  local copies, waits for them, and re-layouts  1.15 us (2%)
  other arithmetic  0.91 us (1%)
  between operations  0.8 us (1%)
    ppermute x16, starting transfers between devices, exchange(): return lax.ppermute(x, axis, [(i, i ^ bit) for i in range(n)])  31.5 us
    ppermute x16, waiting for transfers between devices, exchange(): return lax.ppermute(x, axis, [(i, i ^ bit) for i in range(n)])  10.3 us
    pallas_call x2, Pallas kernels, half_sweep(): pl.pallas_call(lambda *refs: half_kernel(far, n, *refs), in_specs=[SCALAR...  8.13 us
    pallas_call x1, Pallas kernels, build_incidence(): pl.pallas_call(incidence_kernel, in_specs=[SCALARS, SCALARS, REMAIN], out...  5.4 us
    pallas_call x1, Pallas kernels, build_listing(): pl.pallas_call(lambda *refs: listing_kernel(tile_total, *refs), in_specs=...  2.52 us
    pallas_call x1, Pallas kernels, robust_costs(): pl.pallas_call(lambda *refs: robust_kernel(len(parts), *refs), in_specs=[...  1.93 us
  transfers between devices with their start and end apart: 16, of which 6 were waited for; matrix products, arithmetic and copies ran while one was open for 3% of the time, Pallas kernels for 26%

profile of v6, /device:TPU:0, one launch (start us, length us, event | category | flops | bytes accessed | tf_op | source)
XLA Modules:
  0.0 62.8 jit_solution(17558048477469118766)
XLA Ops:
  0.6 3.1 %collective-permute-start = (f32[64,896]{1,0:T(8,128)}, f32[64,896]{1,0:T(8,128)S(1)}, u32[]{:S(2)}, u32[]{:S(2)}) collective-permute-start(f32[64,896]{1,0:T(8,128)} %param.13), channel_id=1, source_target_pairs={{0,4},{4,0},{8,12},{12,8},{1,5},{5,1},{9,13},{13,9},{2,6},{6,2},{1... | collective-permute-start | bytes 688136 | tf_op jit(solution)/shard_map/ppermute | solution.py:427
  3.7 1.0 %constant_dynamic-slice_fusion = (f32[32,896]{1,0:T(8,128)S(1)}, f32[32,896]{1,0:T(8,128)S(1)}) fusion(f32[64,896]{1,0:T(8,128)} %param.13, s32[]{:T(128)S(6)} %select_n.38, s32[]{:T(128)S(6)} %select_n.37), kind=kLoop, calls=%fused_computation.8 | loop fusion | bytes 458760 | tf_op jit(solution)/shard_map/dynamic_slice | solution.py:437
  4.7 2.7 %collective-permute-start.1 = (f32[32,896]{1,0:T(8,128)S(1)}, f32[32,896]{1,0:T(8,128)S(1)}, u32[]{:S(2)}, u32[]{:S(2)}) collective-permute-start(f32[32,896]{1,0:T(8,128)S(1)} %get-tuple-element.67.refs_2_.refs_0_), channel_id=1, source_target_pairs={{0,8},{4,12},{8,0},{12,4},{1,9},{5,13},{9,1},{13,5},{2,10},{6,14},... | collective-permute-start | bytes 344072 | tf_op jit(solution)/shard_map/ppermute | solution.py:427
  7.4 2.5 %listing.1 = (s32[3,144]{1,0:T(4,128)S(1)}, s32[2]{0:T(128)S(1)}, bf16[16,128,128]{2,1,0:T(8,128)(2,1)S(1)}, f32[16,64,128]{2,1,0:T(8,128)S(1)}, f32[7,128]{1,0:T(8,128)S(1)}) custom-call(s32[16,16]{1,0:T(8,128)} %refs_0_.2, s32[16]{0:T(128)} %refs_1_.1, s32[16,128]{1,0:T(8,128)} %refs_2_.1, s32[64,512]{1,0:T(8,128)} %refs_3_.1, f32[7,128]{1,0:T(8,128)} %bitcast.5), custom_call_target="tpu_custom_call" | custom-call | flops 1000000000 | bytes 10000000 | tf_op jit(solution)/shard_map/listing/pallas_call | solution.py:109
  9.9 2.2 %collective-permute-start.4 = (f32[32,896]{1,0:T(8,128)S(1)}, f32[32,896]{1,0:T(8,128)S(1)}, u32[]{:S(2)}, u32[]{:S(2)}) collective-permute-start(f32[32,896]{1,0:T(8,128)S(1)} %get-tuple-element.44.refs_2_), channel_id=1, source_target_pairs={{0,8},{4,12},{8,0},{12,4},{1,9},{5,13},{9,1},{13,5},{2,10},{6,14},... | collective-permute-start | bytes 344072 | tf_op jit(solution)/shard_map/ppermute | solution.py:427
  12.1 1.8 %collective-permute-start.5 = (f32[32,896]{1,0:T(8,128)S(1)}, f32[32,896]{1,0:T(8,128)S(1)}, u32[]{:S(2)}, u32[]{:S(2)}) collective-permute-start(f32[32,896]{1,0:T(8,128)S(1)} %get-tuple-element.44.refs_2_), channel_id=1, source_target_pairs={{0,12},{4,8},{8,4},{12,0},{1,13},{5,9},{9,5},{13,1},{2,14},{6,10},... | collective-permute-start | bytes 344072 | tf_op jit(solution)/shard_map/ppermute | solution.py:427
  13.9 5.4 %incidence.1 = (bf16[33024,128]{1,0:T(8,128)(2,1)S(1)}, bf16[33024,128]{1,0:T(8,128)(2,1)S(1)}) custom-call(s32[3,144]{1,0:T(4,128)S(1)} %get-tuple-element.34.list_ref.refs_0_, s32[2]{0:T(128)S(1)} %get-tuple-element.35.total_ref.refs_1_, s32[8,2048]{1,0:T(8,128)} %refs_0_.3), custom_call_target="tpu_custom_call" | custom-call | flops 1000000 | bytes 20000000 | tf_op jit(solution)/shard_map/incidence/pallas_call | solution.py:164
  19.3 4.1 %far_sweep.1 = (f32[32,2048]{1,0:T(8,128)S(1)}, f32[29,16,128]{2,1,0:T(8,128)S(1)}, f32[29,16,128]{2,1,0:T(8,128)S(1)}) custom-call(s32[3,144]{1,0:T(4,128)S(1)} %get-tuple-element.34.list_ref.refs_0_, s32[2]{0:T(128)S(1)} %get-tuple-element.35.total_ref.refs_1_, f32[32,896]{1,0:T(8,128)S(1)} %get-tuple-element.44.refs_2_, ...), custom_call_target="tpu_custom_call" | custom-call | flops 10000000000 | bytes 25000000 | tf_op jit(solution)/shard_map/far_sweep/pallas_call | solution.py:281
  23.4 5.8 %collective-permute-start.3 = (f32[29,16,128]{2,1,0:T(8,128)S(1)}, f32[29,16,128]{2,1,0:T(8,128)S(1)}, u32[]{:S(2)}, u32[]{:S(2)}) collective-permute-start(f32[29,16,128]{2,1,0:T(8,128)S(1)} %get-tuple-element.43), channel_id=1, source_target_pairs={{0,4},{4,0},{8,12},{12,8},{1,5},{5,1},{9,13},{13,9},{2,6},{6,2},{1... | collective-permute-start | bytes 712712 | tf_op jit(solution)/shard_map/ppermute | solution.py:427
  29.2 4.1 %near_sweep.1 = (f32[32,2048]{1,0:T(8,128)S(1)}, f32[29,16,128]{2,1,0:T(8,128)S(1)}, f32[29,16,128]{2,1,0:T(8,128)S(1)}) custom-call(s32[3,144]{1,0:T(4,128)S(1)} %get-tuple-element.34.list_ref.refs_0_, s32[2]{0:T(128)S(1)} %get-tuple-element.35.total_ref.refs_1_, f32[32,896]{1,0:T(8,128)S(1)} %get-tuple-element.67.refs_2_.refs_0_, ...), custom_call_target="tpu_custom_call" | custom-call | flops 10000000000 | bytes 25000000 | tf_op jit(solution)/shard_map/near_sweep/pallas_call | solution.py:281
  33.6 2.4 %collective-permute-start.6 = (f32[29,16,128]{2,1,0:T(8,128)S(1)}, f32[29,16,128]{2,1,0:T(8,128)S(1)}, u32[]{:S(2)}, u32[]{:S(2)}) collective-permute-start(f32[29,16,128]{2,1,0:T(8,128)S(1)} %get-tuple-element.52), channel_id=1, source_target_pairs={{0,4},{4,0},{8,12},{12,8},{1,5},{5,1},{9,13},{13,9},{2,6},{6,2},{1... | collective-permute-start | bytes 712712 | tf_op jit(solution)/shard_map/ppermute | solution.py:427
  36.0 2.3 %collective-permute-start.7 = (f32[29,16,128]{2,1,0:T(8,128)S(1)}, f32[29,16,128]{2,1,0:T(8,128)S(1)}, u32[]{:S(2)}, u32[]{:S(2)}) collective-permute-start(f32[29,16,128]{2,1,0:T(8,128)S(1)} %add.36), channel_id=1, source_target_pairs={{0,8},{4,12},{8,0},{12,4},{1,9},{5,13},{9,1},{13,5},{2,10},{6,14},... | collective-permute-start | bytes 712712 | tf_op jit(solution)/shard_map/ppermute | solution.py:427
  38.3 0.8 %pad_maximum_fusion = f32[64,2048]{1,0:T(8,128)} fusion(f32[32,2048]{1,0:T(8,128)S(1)} %get-tuple-element.66, f32[32,2048]{1,0:T(8,128)S(1)} %get-tuple-element.65), kind=kLoop, calls=%fused_computation | loop fusion | flops 131072 | bytes 1048576 | tf_op jit(solution)/shard_map/concatenate | solution.py:457
  39.2 1.7 %collective-permute-done.6.refs_7_ = f32[29,16,128]{2,1,0:T(8,128)S(1)} collective-permute-done((f32[29,16,128]{2,1,0:T(8,128)S(1)}, f32[29,16,128]{2,1,0:T(8,128)S(1)}, u32[]{:S(2)}, u32[]{:S(2)}) %collective-permute-start.6) | collective-permute-done | bytes 237600 | tf_op jit(solution)/shard_map/ppermute | solution.py:427
  41.0 2.7 %collective-permute-done.7.refs_8_ = f32[29,16,128]{2,1,0:T(8,128)S(1)} collective-permute-done((f32[29,16,128]{2,1,0:T(8,128)S(1)}, f32[29,16,128]{2,1,0:T(8,128)S(1)}, u32[]{:S(2)}, u32[]{:S(2)}) %collective-permute-start.7) | collective-permute-done | bytes 237600 | tf_op jit(solution)/shard_map/ppermute | solution.py:427
  44.0 1.1 %collective-permute-done.8 = f32[28,128]{1,0:T(8,128)S(1)} collective-permute-done((f32[28,128]{1,0:T(8,128)S(1)}, f32[28,128]{1,0:T(8,128)S(1)}, u32[]{:S(2)}, u32[]{:S(2)}) %collective-permute-start.8) | collective-permute-done | bytes 14368 | tf_op jit(solution)/shard_map/ppermute | solution.py:427
  45.2 4.1 %collective-permute-start.11 = (f32[28,128]{1,0:T(8,128)S(1)}, f32[28,128]{1,0:T(8,128)S(1)}, u32[]{:S(2)}, u32[]{:S(2)}) collective-permute-start(f32[28,128]{1,0:T(8,128)S(1)} %add.37), channel_id=1, source_target_pairs={{0,6},{2,4},{4,2},{6,0},{8,14},{10,12},{12,10},{14,8},{1,7},{3,5},... | collective-permute-start | bytes 43016 | tf_op jit(solution)/shard_map/ppermute | solution.py:427
  49.3 0.6 %collective-permute-start.9 = (f32[28,128]{1,0:T(8,128)S(1)}, f32[28,128]{1,0:T(8,128)S(1)}, u32[]{:S(2)}, u32[]{:S(2)}) collective-permute-start(f32[28,128]{1,0:T(8,128)S(1)} %add.37), channel_id=1, source_target_pairs={{0,2},{2,0},{1,3},{3,1},{4,6},{6,4},{5,7},{7,5},{8,10},{10,8},{9,1... | collective-permute-start | bytes 43016 | tf_op jit(solution)/shard_map/ppermute | solution.py:427
  49.9 2.0 %collective-permute-start.13 = (f32[16,896]{1,0:T(8,128)S(1)}, f32[16,896]{1,0:T(8,128)S(1)}, u32[]{:S(2)}, u32[]{:S(2)}) collective-permute-start(f32[16,896]{1,0:T(8,128)S(1)} %get-tuple-element.60), channel_id=1, source_target_pairs={{0,4},{4,0},{8,12},{12,8},{1,5},{5,1},{9,13},{13,9},{2,6},{6,2},{1... | collective-permute-start | bytes 172040 | tf_op jit(solution)/shard_map/ppermute | solution.py:427
  51.9 3.0 %collective-permute-start.14 = (f32[16,896]{1,0:T(8,128)S(1)}, f32[16,896]{1,0:T(8,128)S(1)}, u32[]{:S(2)}, u32[]{:S(2)}) collective-permute-start(f32[16,896]{1,0:T(8,128)S(1)} %get-tuple-element.61), channel_id=1, source_target_pairs={{0,8},{4,12},{8,0},{12,4},{1,9},{5,13},{9,1},{13,5},{2,10},{6,14},... | collective-permute-start | bytes 172040 | tf_op jit(solution)/shard_map/ppermute | solution.py:427
  55.4 1.2 %collective-permute-start.12 = (f32[28,128]{1,0:T(8,128)S(1)}, f32[28,128]{1,0:T(8,128)S(1)}, u32[]{:S(2)}, u32[]{:S(2)}) collective-permute-start(f32[28,128]{1,0:T(8,128)S(1)} %add_add_fusion.refs_1_), channel_id=1, source_target_pairs={{0,8},{4,12},{8,0},{12,4},{1,9},{5,13},{9,1},{13,5},{2,10},{6,14},... | collective-permute-start | bytes 43016 | tf_op jit(solution)/shard_map/ppermute | solution.py:427
  56.5 1.5 %collective-permute-done.14 = f32[16,896]{1,0:T(8,128)S(1)} collective-permute-done((f32[16,896]{1,0:T(8,128)S(1)}, f32[16,896]{1,0:T(8,128)S(1)}, u32[]{:S(2)}, u32[]{:S(2)}) %collective-permute-start.14) | collective-permute-done | bytes 57376 | tf_op jit(solution)/shard_map/ppermute | solution.py:427
  58.0 2.8 %collective-permute-done.15 = f32[16,896]{1,0:T(8,128)S(1)} collective-permute-done((f32[16,896]{1,0:T(8,128)S(1)}, f32[16,896]{1,0:T(8,128)S(1)}, u32[]{:S(2)}, u32[]{:S(2)}) %collective-permute-start.15) | collective-permute-done | bytes 57376 | tf_op jit(solution)/shard_map/ppermute | solution.py:427
  60.9 1.9 %robust.1 = f32[16,128]{1,0:T(8,128)} custom-call(s32[8,2048]{1,0:T(8,128)S(1)} %copy-done, f32[28,128]{1,0:T(8,128)S(1)} %add_add_fusion.refs_1_, f32[28,128]{1,0:T(8,128)S(1)} %collective-permute-done.12.refs_2_), custom_call_target="tpu_custom_call" | custom-call | flops 1000000 | bytes 1000000 | tf_op jit(solution)/shard_map/robust/pallas_call | solution.py:413
  (32 shorter events, 1.3 us)
Async XLA Ops:
  0.6 18.7 %collective-permute-start = (f32[64,896]{1,0:T(8,128)}, f32[64,896]{1,0:T(8,128)S(1)}, u32[]{:S(2)}, u32[]{:S(2)}) collective-permute-start(f32[64,896]{1,0:T(8,128)} %param.13), channel_id=1, source_target_pairs={{0,4},{4,0},{8,12},{12,8},{1,5},{5,1},{9,13},{13,9},{2,6},{6,2},{1... | collective-permute-start | bytes 688136 | tf_op jit(solution)/shard_map/ppermute | solution.py:427
  4.7 14.6 %collective-permute-start.1 = (f32[32,896]{1,0:T(8,128)S(1)}, f32[32,896]{1,0:T(8,128)S(1)}, u32[]{:S(2)}, u32[]{:S(2)}) collective-permute-start(f32[32,896]{1,0:T(8,128)S(1)} %get-tuple-element.67.refs_2_.refs_0_), channel_id=1, source_target_pairs={{0,8},{4,12},{8,0},{12,4},{1,9},{5,13},{9,1},{13,5},{2,10},{6,14},... | collective-permute-start | bytes 344072 | tf_op jit(solution)/shard_map/ppermute | solution.py:427
  7.4 11.9 %collective-permute-start.2 = (f32[32,896]{1,0:T(8,128)S(1)}, f32[32,896]{1,0:T(8,128)S(1)}, u32[]{:S(2)}, u32[]{:S(2)}) collective-permute-start(f32[32,896]{1,0:T(8,128)S(1)} %get-tuple-element.67.refs_2_.refs_0_), channel_id=1, source_target_pairs={{0,12},{4,8},{8,4},{12,0},{1,13},{5,9},{9,5},{13,1},{2,14},{6,10},... | collective-permute-start | bytes 344072 | tf_op jit(solution)/shard_map/ppermute | solution.py:427
  9.9 19.3 %collective-permute-start.4 = (f32[32,896]{1,0:T(8,128)S(1)}, f32[32,896]{1,0:T(8,128)S(1)}, u32[]{:S(2)}, u32[]{:S(2)}) collective-permute-start(f32[32,896]{1,0:T(8,128)S(1)} %get-tuple-element.44.refs_2_), channel_id=1, source_target_pairs={{0,8},{4,12},{8,0},{12,4},{1,9},{5,13},{9,1},{13,5},{2,10},{6,14},... | collective-permute-start | bytes 344072 | tf_op jit(solution)/shard_map/ppermute | solution.py:427
  12.1 17.1 %collective-permute-start.5 = (f32[32,896]{1,0:T(8,128)S(1)}, f32[32,896]{1,0:T(8,128)S(1)}, u32[]{:S(2)}, u32[]{:S(2)}) collective-permute-start(f32[32,896]{1,0:T(8,128)S(1)} %get-tuple-element.44.refs_2_), channel_id=1, source_target_pairs={{0,12},{4,8},{8,4},{12,0},{1,13},{5,9},{9,5},{13,1},{2,14},{6,10},... | collective-permute-start | bytes 344072 | tf_op jit(solution)/shard_map/ppermute | solution.py:427
  23.4 15.8 %copy-start.2 = (f32[64]{0:T(128)S(1)}, f32[64]{0:T(128)}, u32[]{:S(2)}) copy-start(f32[64]{0:T(128)} %param.15) | copy-start | bytes 772
  23.4 37.5 %copy-start = (s32[8,2048]{1,0:T(8,128)S(1)}, s32[8,2048]{1,0:T(8,128)}, u32[]{:S(2)}) copy-start(s32[8,2048]{1,0:T(8,128)} %refs_0_.3) | copy-start | bytes 196612
  23.4 10.2 %collective-permute-start.3 = (f32[29,16,128]{2,1,0:T(8,128)S(1)}, f32[29,16,128]{2,1,0:T(8,128)S(1)}, u32[]{:S(2)}, u32[]{:S(2)}) collective-permute-start(f32[29,16,128]{2,1,0:T(8,128)S(1)} %get-tuple-element.43), channel_id=1, source_target_pairs={{0,4},{4,0},{8,12},{12,8},{1,5},{5,1},{9,13},{13,9},{2,6},{6,2},{1... | collective-permute-start | bytes 712712 | tf_op jit(solution)/shard_map/ppermute | solution.py:427
  33.6 7.4 %collective-permute-start.6 = (f32[29,16,128]{2,1,0:T(8,128)S(1)}, f32[29,16,128]{2,1,0:T(8,128)S(1)}, u32[]{:S(2)}, u32[]{:S(2)}) collective-permute-start(f32[29,16,128]{2,1,0:T(8,128)S(1)} %get-tuple-element.52), channel_id=1, source_target_pairs={{0,4},{4,0},{8,12},{12,8},{1,5},{5,1},{9,13},{13,9},{2,6},{6,2},{1... | collective-permute-start | bytes 712712 | tf_op jit(solution)/shard_map/ppermute | solution.py:427
  36.0 7.7 %collective-permute-start.7 = (f32[29,16,128]{2,1,0:T(8,128)S(1)}, f32[29,16,128]{2,1,0:T(8,128)S(1)}, u32[]{:S(2)}, u32[]{:S(2)}) collective-permute-start(f32[29,16,128]{2,1,0:T(8,128)S(1)} %add.36), channel_id=1, source_target_pairs={{0,8},{4,12},{8,0},{12,4},{1,9},{5,13},{9,1},{13,5},{2,10},{6,14},... | collective-permute-start | bytes 712712 | tf_op jit(solution)/shard_map/ppermute | solution.py:427
  43.9 1.2 %collective-permute-start.8 = (f32[28,128]{1,0:T(8,128)S(1)}, f32[28,128]{1,0:T(8,128)S(1)}, u32[]{:S(2)}, u32[]{:S(2)}) collective-permute-start(f32[28,128]{1,0:T(8,128)S(1)} %get-tuple-element.54), channel_id=1, source_target_pairs={{0,1},{1,0},{2,3},{3,2},{4,5},{5,4},{6,7},{7,6},{8,9},{9,8},{10,11... | collective-permute-start | bytes 43016 | tf_op jit(solution)/shard_map/ppermute | solution.py:427
  45.2 9.7 %collective-permute-start.11 = (f32[28,128]{1,0:T(8,128)S(1)}, f32[28,128]{1,0:T(8,128)S(1)}, u32[]{:S(2)}, u32[]{:S(2)}) collective-permute-start(f32[28,128]{1,0:T(8,128)S(1)} %add.37), channel_id=1, source_target_pairs={{0,6},{2,4},{4,2},{6,0},{8,14},{10,12},{12,10},{14,8},{1,7},{3,5},... | collective-permute-start | bytes 43016 | tf_op jit(solution)/shard_map/ppermute | solution.py:427
  49.3 6.1 %collective-permute-start.10 = (f32[28,128]{1,0:T(8,128)S(1)}, f32[28,128]{1,0:T(8,128)S(1)}, u32[]{:S(2)}, u32[]{:S(2)}) collective-permute-start(f32[28,128]{1,0:T(8,128)S(1)} %add.37), channel_id=1, source_target_pairs={{0,4},{4,0},{8,12},{12,8},{1,5},{5,1},{9,13},{13,9},{2,6},{6,2},{1... | collective-permute-start | bytes 43016 | tf_op jit(solution)/shard_map/ppermute | solution.py:427
  49.3 6.1 %collective-permute-start.9 = (f32[28,128]{1,0:T(8,128)S(1)}, f32[28,128]{1,0:T(8,128)S(1)}, u32[]{:S(2)}, u32[]{:S(2)}) collective-permute-start(f32[28,128]{1,0:T(8,128)S(1)} %add.37), channel_id=1, source_target_pairs={{0,2},{2,0},{1,3},{3,1},{4,6},{6,4},{5,7},{7,5},{8,10},{10,8},{9,1... | collective-permute-start | bytes 43016 | tf_op jit(solution)/shard_map/ppermute | solution.py:427
  49.9 6.6 %collective-permute-start.13 = (f32[16,896]{1,0:T(8,128)S(1)}, f32[16,896]{1,0:T(8,128)S(1)}, u32[]{:S(2)}, u32[]{:S(2)}) collective-permute-start(f32[16,896]{1,0:T(8,128)S(1)} %get-tuple-element.60), channel_id=1, source_target_pairs={{0,4},{4,0},{8,12},{12,8},{1,5},{5,1},{9,13},{13,9},{2,6},{6,2},{1... | collective-permute-start | bytes 172040 | tf_op jit(solution)/shard_map/ppermute | solution.py:427
  51.9 6.1 %collective-permute-start.14 = (f32[16,896]{1,0:T(8,128)S(1)}, f32[16,896]{1,0:T(8,128)S(1)}, u32[]{:S(2)}, u32[]{:S(2)}) collective-permute-start(f32[16,896]{1,0:T(8,128)S(1)} %get-tuple-element.61), channel_id=1, source_target_pairs={{0,8},{4,12},{8,0},{12,4},{1,9},{5,13},{9,1},{13,5},{2,10},{6,14},... | collective-permute-start | bytes 172040 | tf_op jit(solution)/shard_map/ppermute | solution.py:427
  54.9 6.0 %collective-permute-start.15 = (f32[16,896]{1,0:T(8,128)S(1)}, f32[16,896]{1,0:T(8,128)S(1)}, u32[]{:S(2)}, u32[]{:S(2)}) collective-permute-start(f32[16,896]{1,0:T(8,128)S(1)} %get-tuple-element.62), channel_id=1, source_target_pairs={{0,12},{4,8},{8,4},{12,0},{1,13},{5,9},{9,5},{13,1},{2,14},{6,10},... | collective-permute-start | bytes 172040 | tf_op jit(solution)/shard_map/ppermute | solution.py:427
  55.4 5.5 %collective-permute-start.12 = (f32[28,128]{1,0:T(8,128)S(1)}, f32[28,128]{1,0:T(8,128)S(1)}, u32[]{:S(2)}, u32[]{:S(2)}) collective-permute-start(f32[28,128]{1,0:T(8,128)S(1)} %add_add_fusion.refs_1_), channel_id=1, source_target_pairs={{0,8},{4,12},{8,0},{12,4},{1,9},{5,13},{9,1},{13,5},{2,10},{6,14},... | collective-permute-start | bytes 43016 | tf_op jit(solution)/shard_map/ppermute | solution.py:427
  60.9 2.0 %copy-start.1 = (f32[64,896]{1,0:T(8,128)}, f32[64,896]{1,0:T(8,128)S(1)}, u32[]{:S(2)}) copy-start(f32[64,896]{1,0:T(8,128)S(1)} %constant_dynamic-update-slice_fusion) | copy-start | bytes 688132

commit v7 on v6

--- a/solution.py
+++ b/solution.py
@@ -28,7 +28,7 @@
 TOGETHER = 8
 UNROLL = 28
 LB_BITS = 7
-COUNTED = 8
+COUNTED = 16
 
 
 def split(x):
@@ -439,6 +439,7 @@
     def swap(x, m):
         return exchange(x, "path", n, m)
 
+    lengths, far, near = lax.optimization_barrier((lengths, far, near))
     near_straight, near_crossed = swap(near, 2), swap(near, 3)
     pairs, total, same, wanted, capacity_tiles = build_listing(
         n * own // LB, block_tiles, block_count, path_commodity, demand, capacity

time: 63.1 us -> 61.7 us (0.978)
  starting transfers between devices: 31.5 us -> 29.4 us
    ppermute x16, starting transfers between devices: 31.5 us -> 29.4 us  [exchange(): return lax.ppermute(x, axis, [(i, i ^ bit) for i in range(n)])]
  transfers between devices with their start and end apart: 16 -> 16, of which waited for: 6 -> 5; matrix products, arithmetic and copies ran while one was open for 3% -> 2% of each run, Pallas kernels for 26% -> 27%
where the time goes in v7:
time: 61.7 us; the launch traced here: 61.6 us
  starting transfers between devices  29.4 us (48%)
  Pallas kernels  18.6 us (30%)
  waiting for transfers between devices  10.8 us (18%)
  local copies, waits for them, and re-layouts  1.14 us (2%)
  other arithmetic  0.91 us (1%)
  between operations  0.83 us (1%)
    ppermute x16, starting transfers between devices, exchange(): return lax.ppermute(x, axis, [(i, i ^ bit) for i in range(n)])  29.4 us
    ppermute x16, waiting for transfers between devices, exchange(): return lax.ppermute(x, axis, [(i, i ^ bit) for i in range(n)])  10.8 us
    pallas_call x2, Pallas kernels, half_sweep(): pl.pallas_call(lambda *refs: half_kernel(far, n, *refs), in_specs=[SCALAR...  8.14 us
    pallas_call x1, Pallas kernels, build_incidence(): pl.pallas_call(incidence_kernel, in_specs=[SCALARS, SCALARS, REMAIN], out...  5.74 us
    pallas_call x1, Pallas kernels, build_listing(): pl.pallas_call(lambda *refs: listing_kernel(tile_total, *refs), in_specs=...  2.55 us
    pallas_call x1, Pallas kernels, robust_costs(): pl.pallas_call(lambda *refs: robust_kernel(len(parts), *refs), in_specs=[...  1.93 us
  transfers between devices with their start and end apart: 16, of which 5 were waited for; matrix products, arithmetic and copies ran while one was open for 2% of the time, Pallas kernels for 27%

profile of v7, /device:TPU:0, one launch (start us, length us, event | category | flops | bytes accessed | tf_op | source)
XLA Modules:
  0.0 61.6 jit_solution(14110037219131712999)
XLA Ops:
  0.7 1.0 %constant_dynamic-slice_fusion = (f32[32,896]{1,0:T(8,128)S(1)}, f32[32,896]{1,0:T(8,128)S(1)}) fusion(f32[64,896]{1,0:T(8,128)} %param.13, s32[]{:T(128)S(6)} %select_n.38, s32[]{:T(128)S(6)} %select_n.37), kind=kLoop, calls=%fused_computation.8 | loop fusion | bytes 458760 | tf_op jit(solution)/shard_map/dynamic_slice | solution.py:437
  1.6 3.1 %collective-permute-start = (f32[64,896]{1,0:T(8,128)}, f32[64,896]{1,0:T(8,128)S(1)}, u32[]{:S(2)}, u32[]{:S(2)}) collective-permute-start(f32[64,896]{1,0:T(8,128)} %param.13), channel_id=1, source_target_pairs={{0,4},{4,0},{8,12},{12,8},{1,5},{5,1},{9,13},{13,9},{2,6},{6,2},{1... | collective-permute-start | bytes 688136 | tf_op jit(solution)/shard_map/ppermute | solution.py:427
  4.7 2.6 %collective-permute-start.1 = (f32[32,896]{1,0:T(8,128)S(1)}, f32[32,896]{1,0:T(8,128)S(1)}, u32[]{:S(2)}, u32[]{:S(2)}) collective-permute-start(f32[32,896]{1,0:T(8,128)S(1)} %get-tuple-element.41.refs_2_.refs_0_), channel_id=1, source_target_pairs={{0,8},{4,12},{8,0},{12,4},{1,9},{5,13},{9,1},{13,5},{2,10},{6,14},... | collective-permute-start | bytes 344072 | tf_op jit(solution)/shard_map/ppermute | solution.py:427
  7.3 2.5 %listing.1 = (s32[3,144]{1,0:T(4,128)S(1)}, s32[2]{0:T(128)S(1)}, bf16[16,128,128]{2,1,0:T(8,128)(2,1)S(1)}, f32[16,64,128]{2,1,0:T(8,128)S(1)}, f32[7,128]{1,0:T(8,128)S(1)}) custom-call(s32[16,16]{1,0:T(8,128)} %refs_0_.2, s32[16]{0:T(128)} %refs_1_.1, s32[16,128]{1,0:T(8,128)} %refs_2_.1, s32[64,512]{1,0:T(8,128)} %refs_3_.1, f32[7,128]{1,0:T(8,128)} %bitcast.5), custom_call_target="tpu_custom_call" | custom-call | flops 1000000000 | bytes 10000000 | tf_op jit(solution)/shard_map/listing/pallas_call | solution.py:109
  9.9 2.2 %collective-permute-start.4 = (f32[32,896]{1,0:T(8,128)S(1)}, f32[32,896]{1,0:T(8,128)S(1)}, u32[]{:S(2)}, u32[]{:S(2)}) collective-permute-start(f32[32,896]{1,0:T(8,128)S(1)} %get-tuple-element.50.refs_2_), channel_id=1, source_target_pairs={{0,8},{4,12},{8,0},{12,4},{1,9},{5,13},{9,1},{13,5},{2,10},{6,14},... | collective-permute-start | bytes 344072 | tf_op jit(solution)/shard_map/ppermute | solution.py:427
  12.0 2.0 %collective-permute-start.5 = (f32[32,896]{1,0:T(8,128)S(1)}, f32[32,896]{1,0:T(8,128)S(1)}, u32[]{:S(2)}, u32[]{:S(2)}) collective-permute-start(f32[32,896]{1,0:T(8,128)S(1)} %get-tuple-element.50.refs_2_), channel_id=1, source_target_pairs={{0,12},{4,8},{8,4},{12,0},{1,13},{5,9},{9,5},{13,1},{2,14},{6,10},... | collective-permute-start | bytes 344072 | tf_op jit(solution)/shard_map/ppermute | solution.py:427
  14.0 5.7 %incidence.1 = (bf16[33024,128]{1,0:T(8,128)(2,1)S(1)}, bf16[33024,128]{1,0:T(8,128)(2,1)S(1)}) custom-call(s32[3,144]{1,0:T(4,128)S(1)} %get-tuple-element.37.list_ref.refs_0_, s32[2]{0:T(128)S(1)} %get-tuple-element.38.total_ref.refs_1_, s32[8,2048]{1,0:T(8,128)} %refs_0_.3), custom_call_target="tpu_custom_call" | custom-call | flops 1000000 | bytes 20000000 | tf_op jit(solution)/shard_map/incidence/pallas_call | solution.py:164
  19.8 4.1 %far_sweep.1 = (f32[32,2048]{1,0:T(8,128)S(1)}, f32[29,16,128]{2,1,0:T(8,128)S(1)}, f32[29,16,128]{2,1,0:T(8,128)S(1)}) custom-call(s32[3,144]{1,0:T(4,128)S(1)} %get-tuple-element.37.list_ref.refs_0_, s32[2]{0:T(128)S(1)} %get-tuple-element.38.total_ref.refs_1_, f32[32,896]{1,0:T(8,128)S(1)} %get-tuple-element.50.refs_2_, ...), custom_call_target="tpu_custom_call" | custom-call | flops 10000000000 | bytes 25000000 | tf_op jit(solution)/shard_map/far_sweep/pallas_call | solution.py:281
  23.9 4.0 %collective-permute-start.3 = (f32[29,16,128]{2,1,0:T(8,128)S(1)}, f32[29,16,128]{2,1,0:T(8,128)S(1)}, u32[]{:S(2)}, u32[]{:S(2)}) collective-permute-start(f32[29,16,128]{2,1,0:T(8,128)S(1)} %get-tuple-element.49), channel_id=1, source_target_pairs={{0,4},{4,0},{8,12},{12,8},{1,5},{5,1},{9,13},{13,9},{2,6},{6,2},{1... | collective-permute-start | bytes 712712 | tf_op jit(solution)/shard_map/ppermute | solution.py:427
  27.9 4.1 %near_sweep.1 = (f32[32,2048]{1,0:T(8,128)S(1)}, f32[29,16,128]{2,1,0:T(8,128)S(1)}, f32[29,16,128]{2,1,0:T(8,128)S(1)}) custom-call(s32[3,144]{1,0:T(4,128)S(1)} %get-tuple-element.37.list_ref.refs_0_, s32[2]{0:T(128)S(1)} %get-tuple-element.38.total_ref.refs_1_, f32[32,896]{1,0:T(8,128)S(1)} %get-tuple-element.41.refs_2_.refs_0_, ...), custom_call_target="tpu_custom_call" | custom-call | flops 10000000000 | bytes 25000000 | tf_op jit(solution)/shard_map/near_sweep/pallas_call | solution.py:281
  32.0 2.1 %collective-permute-start.6 = (f32[29,16,128]{2,1,0:T(8,128)S(1)}, f32[29,16,128]{2,1,0:T(8,128)S(1)}, u32[]{:S(2)}, u32[]{:S(2)}) collective-permute-start(f32[29,16,128]{2,1,0:T(8,128)S(1)} %get-tuple-element.58), channel_id=1, source_target_pairs={{0,4},{4,0},{8,12},{12,8},{1,5},{5,1},{9,13},{13,9},{2,6},{6,2},{1... | collective-permute-start | bytes 712712 | tf_op jit(solution)/shard_map/ppermute | solution.py:427
  34.1 2.9 %collective-permute-start.7 = (f32[29,16,128]{2,1,0:T(8,128)S(1)}, f32[29,16,128]{2,1,0:T(8,128)S(1)}, u32[]{:S(2)}, u32[]{:S(2)}) collective-permute-start(f32[29,16,128]{2,1,0:T(8,128)S(1)} %add.36), channel_id=1, source_target_pairs={{0,8},{4,12},{8,0},{12,4},{1,9},{5,13},{9,1},{13,5},{2,10},{6,14},... | collective-permute-start | bytes 712712 | tf_op jit(solution)/shard_map/ppermute | solution.py:427
  37.0 0.8 %pad_maximum_fusion = f32[64,2048]{1,0:T(8,128)} fusion(f32[32,2048]{1,0:T(8,128)S(1)} %get-tuple-element.72, f32[32,2048]{1,0:T(8,128)S(1)} %get-tuple-element.71), kind=kLoop, calls=%fused_computation | loop fusion | flops 131072 | bytes 1048576 | tf_op jit(solution)/shard_map/concatenate | solution.py:458
  37.9 3.0 %collective-permute-done.6.refs_7_ = f32[29,16,128]{2,1,0:T(8,128)S(1)} collective-permute-done((f32[29,16,128]{2,1,0:T(8,128)S(1)}, f32[29,16,128]{2,1,0:T(8,128)S(1)}, u32[]{:S(2)}, u32[]{:S(2)}) %collective-permute-start.6) | collective-permute-done | bytes 237600 | tf_op jit(solution)/shard_map/ppermute | solution.py:427
  41.0 2.2 %collective-permute-done.7.refs_8_ = f32[29,16,128]{2,1,0:T(8,128)S(1)} collective-permute-done((f32[29,16,128]{2,1,0:T(8,128)S(1)}, f32[29,16,128]{2,1,0:T(8,128)S(1)}, u32[]{:S(2)}, u32[]{:S(2)}) %collective-permute-start.7) | collective-permute-done | bytes 237600 | tf_op jit(solution)/shard_map/ppermute | solution.py:427
  43.5 1.1 %collective-permute-done.8 = f32[28,128]{1,0:T(8,128)S(1)} collective-permute-done((f32[28,128]{1,0:T(8,128)S(1)}, f32[28,128]{1,0:T(8,128)S(1)}, u32[]{:S(2)}, u32[]{:S(2)}) %collective-permute-start.8) | collective-permute-done | bytes 14368 | tf_op jit(solution)/shard_map/ppermute | solution.py:427
  44.7 4.0 %collective-permute-start.11 = (f32[28,128]{1,0:T(8,128)S(1)}, f32[28,128]{1,0:T(8,128)S(1)}, u32[]{:S(2)}, u32[]{:S(2)}) collective-permute-start(f32[28,128]{1,0:T(8,128)S(1)} %add.37), channel_id=1, source_target_pairs={{0,6},{2,4},{4,2},{6,0},{8,14},{10,12},{12,10},{14,8},{1,7},{3,5},... | collective-permute-start | bytes 43016 | tf_op jit(solution)/shard_map/ppermute | solution.py:427
  48.7 0.6 %collective-permute-start.9 = (f32[28,128]{1,0:T(8,128)S(1)}, f32[28,128]{1,0:T(8,128)S(1)}, u32[]{:S(2)}, u32[]{:S(2)}) collective-permute-start(f32[28,128]{1,0:T(8,128)S(1)} %add.37), channel_id=1, source_target_pairs={{0,2},{2,0},{1,3},{3,1},{4,6},{6,4},{5,7},{7,5},{8,10},{10,8},{9,1... | collective-permute-start | bytes 43016 | tf_op jit(solution)/shard_map/ppermute | solution.py:427
  49.4 2.0 %collective-permute-start.13 = (f32[16,896]{1,0:T(8,128)S(1)}, f32[16,896]{1,0:T(8,128)S(1)}, u32[]{:S(2)}, u32[]{:S(2)}) collective-permute-start(f32[16,896]{1,0:T(8,128)S(1)} %get-tuple-element.66), channel_id=1, source_target_pairs={{0,4},{4,0},{8,12},{12,8},{1,5},{5,1},{9,13},{13,9},{2,6},{6,2},{1... | collective-permute-start | bytes 172040 | tf_op jit(solution)/shard_map/ppermute | solution.py:427
  51.4 2.3 %collective-permute-start.14 = (f32[16,896]{1,0:T(8,128)S(1)}, f32[16,896]{1,0:T(8,128)S(1)}, u32[]{:S(2)}, u32[]{:S(2)}) collective-permute-start(f32[16,896]{1,0:T(8,128)S(1)} %get-tuple-element.67), channel_id=1, source_target_pairs={{0,8},{4,12},{8,0},{12,4},{1,9},{5,13},{9,1},{13,5},{2,10},{6,14},... | collective-permute-start | bytes 172040 | tf_op jit(solution)/shard_map/ppermute | solution.py:427
  54.1 1.2 %collective-permute-start.12 = (f32[28,128]{1,0:T(8,128)S(1)}, f32[28,128]{1,0:T(8,128)S(1)}, u32[]{:S(2)}, u32[]{:S(2)}) collective-permute-start(f32[28,128]{1,0:T(8,128)S(1)} %add_add_fusion.refs_1_), channel_id=1, source_target_pairs={{0,8},{4,12},{8,0},{12,4},{1,9},{5,13},{9,1},{13,5},{2,10},{6,14},... | collective-permute-start | bytes 43016 | tf_op jit(solution)/shard_map/ppermute | solution.py:427
  55.3 2.7 %collective-permute-done.14 = f32[16,896]{1,0:T(8,128)S(1)} collective-permute-done((f32[16,896]{1,0:T(8,128)S(1)}, f32[16,896]{1,0:T(8,128)S(1)}, u32[]{:S(2)}, u32[]{:S(2)}) %collective-permute-start.14) | collective-permute-done | bytes 57376 | tf_op jit(solution)/shard_map/ppermute | solution.py:427
  57.9 1.7 %collective-permute-done.15 = f32[16,896]{1,0:T(8,128)S(1)} collective-permute-done((f32[16,896]{1,0:T(8,128)S(1)}, f32[16,896]{1,0:T(8,128)S(1)}, u32[]{:S(2)}, u32[]{:S(2)}) %collective-permute-start.15) | collective-permute-done | bytes 57376 | tf_op jit(solution)/shard_map/ppermute | solution.py:427
  59.7 1.9 %robust.1 = f32[16,128]{1,0:T(8,128)} custom-call(s32[8,2048]{1,0:T(8,128)S(1)} %copy-done, f32[28,128]{1,0:T(8,128)S(1)} %add_add_fusion.refs_1_, f32[28,128]{1,0:T(8,128)S(1)} %collective-permute-done.12.refs_2_), custom_call_target="tpu_custom_call" | custom-call | flops 1000000 | bytes 1000000 | tf_op jit(solution)/shard_map/robust/pallas_call | solution.py:413
  (32 shorter events, 1.0 us)
Async XLA Ops:
  1.6 18.1 %collective-permute-start = (f32[64,896]{1,0:T(8,128)}, f32[64,896]{1,0:T(8,128)S(1)}, u32[]{:S(2)}, u32[]{:S(2)}) collective-permute-start(f32[64,896]{1,0:T(8,128)} %param.13), channel_id=1, source_target_pairs={{0,4},{4,0},{8,12},{12,8},{1,5},{5,1},{9,13},{13,9},{2,6},{6,2},{1... | collective-permute-start | bytes 688136 | tf_op jit(solution)/shard_map/ppermute | solution.py:427
  4.7 15.0 %collective-permute-start.1 = (f32[32,896]{1,0:T(8,128)S(1)}, f32[32,896]{1,0:T(8,128)S(1)}, u32[]{:S(2)}, u32[]{:S(2)}) collective-permute-start(f32[32,896]{1,0:T(8,128)S(1)} %get-tuple-element.41.refs_2_.refs_0_), channel_id=1, source_target_pairs={{0,8},{4,12},{8,0},{12,4},{1,9},{5,13},{9,1},{13,5},{2,10},{6,14},... | collective-permute-start | bytes 344072 | tf_op jit(solution)/shard_map/ppermute | solution.py:427
  7.3 12.4 %collective-permute-start.2 = (f32[32,896]{1,0:T(8,128)S(1)}, f32[32,896]{1,0:T(8,128)S(1)}, u32[]{:S(2)}, u32[]{:S(2)}) collective-permute-start(f32[32,896]{1,0:T(8,128)S(1)} %get-tuple-element.41.refs_2_.refs_0_), channel_id=1, source_target_pairs={{0,12},{4,8},{8,4},{12,0},{1,13},{5,9},{9,5},{13,1},{2,14},{6,10},... | collective-permute-start | bytes 344072 | tf_op jit(solution)/shard_map/ppermute | solution.py:427
  9.9 18.0 %collective-permute-start.4 = (f32[32,896]{1,0:T(8,128)S(1)}, f32[32,896]{1,0:T(8,128)S(1)}, u32[]{:S(2)}, u32[]{:S(2)}) collective-permute-start(f32[32,896]{1,0:T(8,128)S(1)} %get-tuple-element.50.refs_2_), channel_id=1, source_target_pairs={{0,8},{4,12},{8,0},{12,4},{1,9},{5,13},{9,1},{13,5},{2,10},{6,14},... | collective-permute-start | bytes 344072 | tf_op jit(solution)/shard_map/ppermute | solution.py:427
  12.0 15.8 %collective-permute-start.5 = (f32[32,896]{1,0:T(8,128)S(1)}, f32[32,896]{1,0:T(8,128)S(1)}, u32[]{:S(2)}, u32[]{:S(2)}) collective-permute-start(f32[32,896]{1,0:T(8,128)S(1)} %get-tuple-element.50.refs_2_), channel_id=1, source_target_pairs={{0,12},{4,8},{8,4},{12,0},{1,13},{5,9},{9,5},{13,1},{2,14},{6,10},... | collective-permute-start | bytes 344072 | tf_op jit(solution)/shard_map/ppermute | solution.py:427
  23.9 14.0 %copy-start.2 = (f32[64]{0:T(128)S(1)}, f32[64]{0:T(128)}, u32[]{:S(2)}) copy-start(f32[64]{0:T(128)} %param.15) | copy-start | bytes 772
  23.9 35.8 %copy-start = (s32[8,2048]{1,0:T(8,128)S(1)}, s32[8,2048]{1,0:T(8,128)}, u32[]{:S(2)}) copy-start(s32[8,2048]{1,0:T(8,128)} %refs_0_.3) | copy-start | bytes 196612
  23.9 8.1 %collective-permute-start.3 = (f32[29,16,128]{2,1,0:T(8,128)S(1)}, f32[29,16,128]{2,1,0:T(8,128)S(1)}, u32[]{:S(2)}, u32[]{:S(2)}) collective-permute-start(f32[29,16,128]{2,1,0:T(8,128)S(1)} %get-tuple-element.49), channel_id=1, source_target_pairs={{0,4},{4,0},{8,12},{12,8},{1,5},{5,1},{9,13},{13,9},{2,6},{6,2},{1... | collective-permute-start | bytes 712712 | tf_op jit(solution)/shard_map/ppermute | solution.py:427
  32.0 9.0 %collective-permute-start.6 = (f32[29,16,128]{2,1,0:T(8,128)S(1)}, f32[29,16,128]{2,1,0:T(8,128)S(1)}, u32[]{:S(2)}, u32[]{:S(2)}) collective-permute-start(f32[29,16,128]{2,1,0:T(8,128)S(1)} %get-tuple-element.58), channel_id=1, source_target_pairs={{0,4},{4,0},{8,12},{12,8},{1,5},{5,1},{9,13},{13,9},{2,6},{6,2},{1... | collective-permute-start | bytes 712712 | tf_op jit(solution)/shard_map/ppermute | solution.py:427
  34.1 9.1 %collective-permute-start.7 = (f32[29,16,128]{2,1,0:T(8,128)S(1)}, f32[29,16,128]{2,1,0:T(8,128)S(1)}, u32[]{:S(2)}, u32[]{:S(2)}) collective-permute-start(f32[29,16,128]{2,1,0:T(8,128)S(1)} %add.36), channel_id=1, source_target_pairs={{0,8},{4,12},{8,0},{12,4},{1,9},{5,13},{9,1},{13,5},{2,10},{6,14},... | collective-permute-start | bytes 712712 | tf_op jit(solution)/shard_map/ppermute | solution.py:427
  43.4 1.2 %collective-permute-start.8 = (f32[28,128]{1,0:T(8,128)S(1)}, f32[28,128]{1,0:T(8,128)S(1)}, u32[]{:S(2)}, u32[]{:S(2)}) collective-permute-start(f32[28,128]{1,0:T(8,128)S(1)} %get-tuple-element.60), channel_id=1, source_target_pairs={{0,1},{1,0},{2,3},{3,2},{4,5},{5,4},{6,7},{7,6},{8,9},{9,8},{10,11... | collective-permute-start | bytes 43016 | tf_op jit(solution)/shard_map/ppermute | solution.py:427
  44.7 9.0 %collective-permute-start.11 = (f32[28,128]{1,0:T(8,128)S(1)}, f32[28,128]{1,0:T(8,128)S(1)}, u32[]{:S(2)}, u32[]{:S(2)}) collective-permute-start(f32[28,128]{1,0:T(8,128)S(1)} %add.37), channel_id=1, source_target_pairs={{0,6},{2,4},{4,2},{6,0},{8,14},{10,12},{12,10},{14,8},{1,7},{3,5},... | collective-permute-start | bytes 43016 | tf_op jit(solution)/shard_map/ppermute | solution.py:427
  48.7 5.4 %collective-permute-start.10 = (f32[28,128]{1,0:T(8,128)S(1)}, f32[28,128]{1,0:T(8,128)S(1)}, u32[]{:S(2)}, u32[]{:S(2)}) collective-permute-start(f32[28,128]{1,0:T(8,128)S(1)} %add.37), channel_id=1, source_target_pairs={{0,4},{4,0},{8,12},{12,8},{1,5},{5,1},{9,13},{13,9},{2,6},{6,2},{1... | collective-permute-start | bytes 43016 | tf_op jit(solution)/shard_map/ppermute | solution.py:427
  48.7 5.4 %collective-permute-start.9 = (f32[28,128]{1,0:T(8,128)S(1)}, f32[28,128]{1,0:T(8,128)S(1)}, u32[]{:S(2)}, u32[]{:S(2)}) collective-permute-start(f32[28,128]{1,0:T(8,128)S(1)} %add.37), channel_id=1, source_target_pairs={{0,2},{2,0},{1,3},{3,1},{4,6},{6,4},{5,7},{7,5},{8,10},{10,8},{9,1... | collective-permute-start | bytes 43016 | tf_op jit(solution)/shard_map/ppermute | solution.py:427
  49.4 5.9 %collective-permute-start.13 = (f32[16,896]{1,0:T(8,128)S(1)}, f32[16,896]{1,0:T(8,128)S(1)}, u32[]{:S(2)}, u32[]{:S(2)}) collective-permute-start(f32[16,896]{1,0:T(8,128)S(1)} %get-tuple-element.66), channel_id=1, source_target_pairs={{0,4},{4,0},{8,12},{12,8},{1,5},{5,1},{9,13},{13,9},{2,6},{6,2},{1... | collective-permute-start | bytes 172040 | tf_op jit(solution)/shard_map/ppermute | solution.py:427
  51.4 6.6 %collective-permute-start.14 = (f32[16,896]{1,0:T(8,128)S(1)}, f32[16,896]{1,0:T(8,128)S(1)}, u32[]{:S(2)}, u32[]{:S(2)}) collective-permute-start(f32[16,896]{1,0:T(8,128)S(1)} %get-tuple-element.67), channel_id=1, source_target_pairs={{0,8},{4,12},{8,0},{12,4},{1,9},{5,13},{9,1},{13,5},{2,10},{6,14},... | collective-permute-start | bytes 172040 | tf_op jit(solution)/shard_map/ppermute | solution.py:427
  53.7 6.0 %collective-permute-start.15 = (f32[16,896]{1,0:T(8,128)S(1)}, f32[16,896]{1,0:T(8,128)S(1)}, u32[]{:S(2)}, u32[]{:S(2)}) collective-permute-start(f32[16,896]{1,0:T(8,128)S(1)} %get-tuple-element.68), channel_id=1, source_target_pairs={{0,12},{4,8},{8,4},{12,0},{1,13},{5,9},{9,5},{13,1},{2,14},{6,10},... | collective-permute-start | bytes 172040 | tf_op jit(solution)/shard_map/ppermute | solution.py:427
  54.1 5.5 %collective-permute-start.12 = (f32[28,128]{1,0:T(8,128)S(1)}, f32[28,128]{1,0:T(8,128)S(1)}, u32[]{:S(2)}, u32[]{:S(2)}) collective-permute-start(f32[28,128]{1,0:T(8,128)S(1)} %add_add_fusion.refs_1_), channel_id=1, source_target_pairs={{0,8},{4,12},{8,0},{12,4},{1,9},{5,13},{9,1},{13,5},{2,10},{6,14},... | collective-permute-start | bytes 43016 | tf_op jit(solution)/shard_map/ppermute | solution.py:427
  59.6 2.0 %copy-start.1 = (f32[64,896]{1,0:T(8,128)}, f32[64,896]{1,0:T(8,128)S(1)}, u32[]{:S(2)}) copy-start(f32[64,896]{1,0:T(8,128)S(1)} %constant_dynamic-update-slice_fusion) | copy-start | bytes 688132
